TPU v7x, 128 devices: a whole 4x4x4 slice. The times are simulated.
128 devices in a mesh: row: 8 (over y, core), col: 16 (over x, z).
Axes of the slice: x: 4, y: 4, z: 4, core: 2. Of those that a mesh axis runs over, the one named last changes fastest.
Arguments:
- slab: float32 [65536, 8192], P(('row', 'col')), may hold values from -80 to 80, as said below
- sketch: float32 [8192, 128], replicated, may hold values from -0.0625 to 0.0625
Outputs:
- basis: float32 [65536, 128], P(('row', 'col'))
- projection: float32 [128, 8192], replicated
Inputs may be any that keep to these rules, and one draw needn't show every extreme that they name: `slab`: each entry is one hidden-state value.
All inputs are finite; a program needn't handle non-finite values.
Results may differ from a plain program's by a relative error of at most 0.000084.
Values sent between devices are 32-bit elements; how exact they have to be, the bound alone decides.
No kernel may reach another device: no remote copies, remote signals or barrier semaphores. Data moves between devices by JAX's collectives and lax.ppermute only.
A program may use at most 128 MiB of HBM per device.

v0:
```python
import math

import jax
import jax.numpy as jnp
from jax import lax
from jax.sharding import PartitionSpec as P


def from_partner(value, axis, apart):
    mask = 2**apart
    pairs = [(source, source ^ mask) for source in range(lax.axis_size(axis))]
    return lax.ppermute(value, axis, pairs)


def merge_level(lower, partner):
    highest = lax.Precision.HIGHEST
    combined = jnp.dot(lower, lower.T, precision=highest) + jnp.dot(
        partner, partner.T, precision=highest
    )
    return jnp.linalg.cholesky(combined)


def row_levels(lower):
    for bit in range(lax.axis_size("row").bit_length() - 1):
        lower = merge_level(lower, from_partner(lower, "row", bit))
    return lower


def col_levels(lower):
    for bit in range(lax.axis_size("col").bit_length() - 1):
        lower = merge_level(lower, from_partner(lower, "col", bit))
    return lower


def per_device(slab, sketch):
    highest = lax.Precision.HIGHEST
    sampled = jnp.dot(slab, sketch, precision=highest, preferred_element_type=jnp.float32)
    local_gram = jnp.dot(sampled.T, sampled, precision=highest)
    lower = jnp.linalg.cholesky(local_gram)
    lower = col_levels(row_levels(lower))
    transposed = jax.scipy.linalg.solve_triangular(lower, sampled.T, lower=True)
    total_rows = slab.shape[0] * lax.axis_size("row") * lax.axis_size("col")
    basis = transposed.T * math.sqrt(total_rows)
    projection = lax.psum(jnp.dot(transposed, slab, precision=highest), ("row", "col"))
    return (basis, projection)


def solution(mesh):
    placed = (P(("row", "col"), None), P())
    return jax.shard_map(
        per_device,
        mesh=mesh,
        in_specs=placed,
        out_specs=(P(("row", "col"), None), P()),
        check_vma=False,
    )
```

profile of v0, /device:TPU:1, one launch (start us, length us, event | category | flops | bytes accessed | tf_op | source)
XLA Modules:
  0.0 357.7 jit_solution(3353322843451358239)
XLA Ops:
  7.2 16.2 %fusion.25 = f32[512,128]{1,0:T(8,128)S(1)} fusion(f32[512,8192]{1,0:T(8,128)} %param.3, f32[8192,128]{1,0:T(8,128)} %param.4), kind=kOutput, calls=%fused_computation.60 | convolution fusion | flops 6442450944 | bytes 21233664 | tf_op jit(solution)/shard_map/dot_general | solution.py:37
  24.1 11.7 %cholesky.134 = f32[128,128]{1,0:T(8,128)S(1)} custom-call(f32[128,128]{1,0:T(8,128)S(1)} %fusion.10), custom_call_target="Cholesky" | custom-call | tf_op jit(solution)/shard_map/jit(cholesky)/cholesky | solution.py:39
  37.2 2.0 collective-permute-start
  40.4 11.7 %cholesky.145 = f32[128,128]{1,0:T(8,128)S(1)} custom-call(f32[128,128]{1,0:T(8,128)S(1)} %fusion.9), custom_call_target="Cholesky" | custom-call | tf_op jit(solution)/shard_map/jit(cholesky)/cholesky | solution.py:20
  53.5 1.5 collective-permute-start.1
  55.2 1.5 collective-permute-done.1
  57.1 11.7 %cholesky.156 = f32[128,128]{1,0:T(8,128)S(1)} custom-call(f32[128,128]{1,0:T(8,128)S(1)} %fusion.8), custom_call_target="Cholesky" | custom-call | tf_op jit(solution)/shard_map/jit(cholesky)/cholesky | solution.py:20
  70.1 3.3 collective-permute-start.2
  73.6 1.4 collective-permute-done.2
  75.4 11.7 %cholesky.167 = f32[128,128]{1,0:T(8,128)S(1)} custom-call(f32[128,128]{1,0:T(8,128)S(1)} %fusion.7), custom_call_target="Cholesky" | custom-call | tf_op jit(solution)/shard_map/jit(cholesky)/cholesky | solution.py:20
  88.5 1.8 collective-permute-start.3
  92.3 11.7 %cholesky.178 = f32[128,128]{1,0:T(8,128)S(1)} custom-call(f32[128,128]{1,0:T(8,128)S(1)} %fusion.6), custom_call_target="Cholesky" | custom-call | tf_op jit(solution)/shard_map/jit(cholesky)/cholesky | solution.py:20
  105.3 3.7 %collective-permute-start.4 = (f32[128,128]{1,0:T(8,128)S(1)}, f32[128,128]{1,0:T(8,128)S(1)}, u32[]{:S(2)}, u32[]{:S(2)}) collective-permute-start(f32[128,128]{1,0:T(8,128)S(1)} %select_select_fusion.3), channel_id=1, source_target_pairs={{0,2},{1,3},{2,0},{3,1},{4,6},{5,7},{6,4},{7,5},{8,10},{9,11},{10,... | collective-permute-start | bytes 196616 | tf_op jit(solution)/shard_map/ppermute | solution.py:12
  109.3 1.4 collective-permute-done.4
  111.1 11.7 %cholesky.189 = f32[128,128]{1,0:T(8,128)S(1)} custom-call(f32[128,128]{1,0:T(8,128)S(1)} %fusion.5), custom_call_target="Cholesky" | custom-call | tf_op jit(solution)/shard_map/jit(cholesky)/cholesky | solution.py:20
  125.7 1.6 collective-permute-done.5
  127.7 11.7 %cholesky.200 = f32[128,128]{1,0:T(8,128)S(1)} custom-call(f32[128,128]{1,0:T(8,128)S(1)} %fusion.4), custom_call_target="Cholesky" | custom-call | tf_op jit(solution)/shard_map/jit(cholesky)/cholesky | solution.py:20
  140.8 3.1 collective-permute-start.6
  144.1 1.6 collective-permute-done.6
  146.1 11.7 %cholesky.211 = f32[128,128]{1,0:T(8,128)S(1)} custom-call(f32[128,128]{1,0:T(8,128)S(1)} %fusion.3), custom_call_target="Cholesky" | custom-call | tf_op jit(solution)/shard_map/jit(cholesky)/cholesky | solution.py:20
  159.2 9.8 %custom-call.6 = f32[1,128,128]{1,2,0:T(8,128)S(1)} custom-call(f32[1,128,128]{2,1,0:T(8,128)S(1)} %fusion), custom_call_target="InvertDiagBlocksLowerTriangular" | custom-call | tf_op jit(solution)/shard_map/jit(_solve_triangular)/triangular_solve | solution.py:41
  169.4 13.8 %fusion.34 = f32[128,8192]{1,0:T(8,128)} fusion(f32[128,512]{1,0:T(8,128)S(1)} %fusion.1, f32[512,8192]{1,0:T(8,128)} %param.3), kind=kOutput, calls=%fused_computation.69 | convolution fusion | flops 6442450944 | bytes 21233664 | tf_op jit(solution)/shard_map/dot_general | solution.py:44
  184.1 161.8 %all-reduce.2.cloned.1.call-done = f32[128,8192]{1,0:T(8,128)} async-done(((f32[128,8192]{1,0:T(8,128)}), f32[128,8192]{1,0:T(8,128)}) %all-reduce.2.cloned.1.call-update) | async-done | bytes 4194320 | tf_op jit(solution)/shard_map/psum | solution.py:44
  345.9 4.6 %copy.42 = f32[128,8192]{1,0:T(8,128)} copy(f32[128,8192]{1,0:T(8,128)} %all-reduce.2.cloned.1.call-done) | data formatting | bytes 8388608
  (63 shorter events, 20.4 us)
Async XLA Ops:
  7.2 338.7 %all-reduce.2.cloned.1.call-start = ((), (), s32[]{:S(2)}) async-start(), calls=%async_computation | async-start | bytes 8388608 | tf_op jit(solution)/shard_map/psum | solution.py:44
  37.2 2.9 collective-permute-start
  53.5 3.2 collective-permute-start.1
  70.1 4.9 %collective-permute-start.2 = (f32[128,128]{1,0:T(8,128)S(1)}, f32[128,128]{1,0:T(8,128)S(1)}, u32[]{:S(2)}, u32[]{:S(2)}) collective-permute-start(f32[128,128]{1,0:T(8,128)S(1)} %select_select_fusion.5), channel_id=1, source_target_pairs={{0,64},{16,80},{32,96},{48,112},{64,0},{80,16},{96,32},{112,48},{1... | collective-permute-start | bytes 196616 | tf_op jit(solution)/shard_map/ppermute | solution.py:12
  88.5 3.4 collective-permute-start.3
  105.3 5.4 %collective-permute-start.4 = (f32[128,128]{1,0:T(8,128)S(1)}, f32[128,128]{1,0:T(8,128)S(1)}, u32[]{:S(2)}, u32[]{:S(2)}) collective-permute-start(f32[128,128]{1,0:T(8,128)S(1)} %select_select_fusion.3), channel_id=1, source_target_pairs={{0,2},{1,3},{2,0},{3,1},{4,6},{5,7},{6,4},{7,5},{8,10},{9,11},{10,... | collective-permute-start | bytes 196616 | tf_op jit(solution)/shard_map/ppermute | solution.py:12
  124.1 3.2 collective-permute-start.5
  140.8 5.0 %collective-permute-start.6 = (f32[128,128]{1,0:T(8,128)S(1)}, f32[128,128]{1,0:T(8,128)S(1)}, u32[]{:S(2)}, u32[]{:S(2)}) collective-permute-start(f32[128,128]{1,0:T(8,128)S(1)} %select_select_fusion.1), channel_id=1, source_target_pairs={{0,8},{1,9},{2,10},{3,11},{4,12},{5,13},{6,14},{7,15},{8,0},{9,1},... | collective-permute-start | bytes 196616 | tf_op jit(solution)/shard_map/ppermute | solution.py:12
Sparse Core Ops, SparseCore 0:
  183.3 162.4 all-reduce.1
where the time goes:
time: 364 us; the launch traced here: 358 us
  waiting for transfers between devices  171 us (47%)
  other arithmetic  114 us (31%)
  matrix products  34.7 us (10%)
  starting transfers between devices  16.6 us (5%)
  between operations  14.7 us (4%)
  local copies, waits for them, and re-layouts  6.18 us (2%)
    psum x1, waiting for transfers between devices, per_device(): lax.psum(jnp.dot(transposed, slab, precision=highest), ('row', 'col'))  162 us
    another operation x21, other arithmetic, merge_level(): return jnp.linalg.cholesky(combined)  86.7 us
    ppermute x7, starting transfers between devices, from_partner(): return lax.ppermute(value, axis, pairs)  16.5 us
    dot_general x1, matrix products, per_device(): jnp.dot(slab, sketch, precision=highest, preferred_element_type=jnp.float32)  16.2 us
    dot_general x1, matrix products, per_device(): jnp.dot(transposed, slab, precision=highest)  13.8 us
    another operation x3, other arithmetic, per_device(): lower = jnp.linalg.cholesky(local_gram)  12.4 us
    another operation x2, other arithmetic, per_device(): transposed = jax.scipy.linalg.solve_triangular(lower, sampled.T, lower=True)  10.5 us
    ppermute x7, waiting for transfers between devices, from_partner(): return lax.ppermute(value, axis, pairs)  9.55 us
  transfers between devices with their start and end apart: 8, of which 8 were waited for; matrix products, arithmetic and copies ran while one was open for 1% of the time, Pallas kernels for 0%

commit v1 on v0

v1 whole, which is shorter than its diff:
```python
import math

import jax
import jax.numpy as jnp
import numpy as np
from jax import lax
from jax.experimental import pallas as pl
from jax.experimental.pallas import tpu as pltpu
from jax.sharding import PartitionSpec as P

AXES = ("row", "col")
RING = 4
K = 128
CHUNK = 1024
SPLIT = (48, 40, 40)
STARTS = (0, 48, 88)
MIB = 2**20
F32 = jnp.float32
BF16 = jnp.bfloat16
HIGHEST = lax.Precision.HIGHEST


def places():
    return [
        (x, y, z, c) for y in range(RING) for c in range(2) for x in range(RING) for z in range(RING)
    ]


def linear(x, y, z, c):
    return (y * 2 + c) * RING * RING + x * RING + z


def beside(place, step, core):
    return place ^ 1 if (step ^ core) == 0 else RING - 1 - place


def ring_pairs(axis, step):
    pairs = []
    for x, y, z, c in places():
        to = [x, y, z]
        to[axis] = beside(to[axis], step, c)
        pairs.append((linear(x, y, z, c), linear(*to, c)))
    return pairs


CORE_PAIRS = [(linear(x, y, z, c), linear(x, y, z, 1 - c)) for x, y, z, c in places()]


def ring_order(place, core):
    first = beside(place, 0, core)
    return [place, beside(place, 1, core), first, beside(first, 1, core)]


def order_table():
    table = np.zeros((len(places()), 3, 8), np.int32)
    for x, y, z, c in places():
        here = linear(x, y, z, c)
        for half, core in enumerate((1 - c, c)):
            orders = [ring_order(p, core) for p in (x, y, z)]
            for slot, quarter in enumerate(orders[0]):
                step = half * 4 + slot
                table[here, 0, step] = core * 4 + quarter
                table[here, 1, step] = orders[1].index(quarter)
                table[here, 2, step] = orders[2].index(quarter)
    return table


def halves(value):
    high = value.astype(BF16)
    return high, (value - high.astype(F32)).astype(BF16)


def mul(a, b):
    return jnp.dot(a, b, preferred_element_type=F32)


def front_kernel(table, slab, sketch, sampled, gram, xs, ys, zs, xk, yk, zk, high, low, total, turned):
    step = pl.program_id(0)

    @pl.when(step < 8)
    def _():
        slab_high, slab_low = halves(slab[...])
        high[step] = slab_high
        low[step] = slab_low
        sketch_high, sketch_low = halves(sketch[...])
        both = mul(slab_high, jnp.concatenate([sketch_high, sketch_low], axis=1))
        part = both[:, :K] + (both[:, K:] + mul(slab_low, sketch_high))

        @pl.when(step == 0)
        def _():
            total[...] = part

        @pl.when(step > 0)
        def _():
            total[...] += part

    @pl.when(step == 7)
    def _():
        value = total[...]
        sampled[...] = value
        across = value.T
        product = jnp.dot(across, value, precision=HIGHEST, preferred_element_type=F32)
        gram[...] = jnp.concatenate([product[16 * t : 16 * t + 16] for t in range(8)], axis=1)
        across_high, across_low = halves(across)
        turned[...] = jnp.concatenate([across_high, across_low], axis=0)

    def products():
        chunk = table[0, step - 8]
        left = turned[...]
        both = mul(left, high[chunk])
        return both[:K] + (both[K:] + mul(left[:K], low[chunk]))

    @pl.when((step >= 8) & (step < 12))
    def _():
        value = products()
        for out, start, rows in zip((xs, ys, zs), STARTS, SPLIT):
            out[0] = value[start : start + rows]

    @pl.when(step >= 12)
    def _():
        value = products()
        for out, start, rows in zip((xk, yk, zk), STARTS, SPLIT):
            out[0] = value[start : start + rows]


def front(table, slab, sketch):
    rows = slab.shape[0]

    def sent(line):
        def index(i, t):
            at = jnp.clip(i - 8, 0, 3)
            return (at if line == 0 else t[line, at]), 0, 0

        return index

    def kept(line):
        def index(i, t):
            at = jnp.clip(i - 8, 4, 7)
            return (at - 4 if line == 0 else t[line, at]), 0, 0

        return index

    blocks = [pl.BlockSpec((1, SPLIT[a], CHUNK), sent(a)) for a in range(3)]
    blocks += [pl.BlockSpec((1, SPLIT[a], CHUNK), kept(a)) for a in range(3)]
    return pl.pallas_call(
        front_kernel,
        grid_spec=pltpu.PrefetchScalarGridSpec(
            num_scalar_prefetch=1,
            grid=(16,),
            in_specs=[
                pl.BlockSpec((rows, CHUNK), lambda i, t: (0, jnp.minimum(i, 7))),
                pl.BlockSpec((CHUNK, K), lambda i, t: (jnp.minimum(i, 7), 0)),
            ],
            out_specs=[
                pl.BlockSpec((rows, K), lambda i, t: (0, 0)),
                pl.BlockSpec((16, CHUNK), lambda i, t: (0, 0)),
                *blocks,
            ],
            scratch_shapes=[
                pltpu.VMEM((8, rows, CHUNK), BF16),
                pltpu.VMEM((8, rows, CHUNK), BF16),
                pltpu.VMEM((rows, K), F32),
                pltpu.VMEM((2 * K, rows), BF16),
            ],
        ),
        out_shape=[
            jax.ShapeDtypeStruct((rows, K), F32),
            jax.ShapeDtypeStruct((16, CHUNK), F32),
            *[jax.ShapeDtypeStruct((4, SPLIT[a % 3], CHUNK), F32) for a in range(6)],
        ],
        compiler_params=pltpu.CompilerParams(vmem_limit_bytes=36 * MIB),
        name="sample_and_product",
    )(table, slab, sketch)


def factor_kernel(scale, low_rows, high_rows, sampled, inverse, basis):
    folded = jnp.concatenate([low_rows[...], high_rows[...]], axis=0)
    left = jnp.concatenate([folded[:, K * t : K * t + K] for t in range(8)], axis=0)
    row = lax.broadcasted_iota(jnp.int32, (K, K), 0)
    col = lax.broadcasted_iota(jnp.int32, (K, K), 1)
    right = jnp.where(row == col, 1.0, 0.0).astype(F32)
    lefts = [left[8 * t : 8 * t + 8] for t in range(16)]
    rights = [right[8 * t : 8 * t + 8] for t in range(16)]
    sub = lax.broadcasted_iota(jnp.int32, (8, 1), 0)
    for j in range(K):
        tile, at = divmod(j, 8)
        pivot_row = lefts[tile][at : at + 1]
        down = 1.0 / pivot_row[:, j : j + 1]
        left_row = pivot_row * down
        right_row = rights[tile][at : at + 1] * down
        for t in range(tile, 16):
            factor = lefts[t][:, j : j + 1]
            if t == tile:
                factor = jnp.where(sub > at, factor, 0.0)
            lefts[t] = lefts[t] - factor * left_row
            rights[t] = rights[t] - factor * right_row
    left = jnp.concatenate(lefts, axis=0)
    right = jnp.concatenate(rights, axis=0)
    diagonal = jnp.sum(jnp.where(row == col, left, 0.0), axis=1, keepdims=True)
    value = right * lax.rsqrt(diagonal)
    inverse[...] = value
    basis[...] = scale * jnp.dot(sampled[...], value.T, precision=HIGHEST, preferred_element_type=F32)


def factor(low_rows, high_rows, sampled, scale):
    rows = sampled.shape[0]
    return pl.pallas_call(
        lambda *refs: factor_kernel(scale, *refs),
        out_shape=[jax.ShapeDtypeStruct((K, K), F32), jax.ShapeDtypeStruct((rows, K), F32)],
        cost_estimate=pl.CostEstimate(flops=8 * 10**9, bytes_accessed=MIB, transcendentals=0),
        compiler_params=pltpu.CompilerParams(vmem_limit_bytes=8 * MIB),
        name="factor_and_basis",
    )(low_rows, high_rows, sampled)


def apply_kernel(table, inverse, x, y, z, *rest):
    out = rest[-1]
    value = jnp.concatenate([x[0], y[0], z[0]], axis=0)
    out[...] = jnp.dot(inverse[...], value, precision=HIGHEST, preferred_element_type=F32)


def apply(table, inverse, parts, half, before=None):
    def slot(line):
        return lambda i, t: ((i if line == 0 else t[line, half * 4 + i]), 0, 0)

    in_specs = [pl.BlockSpec((K, K), lambda i, t: (0, 0))]
    in_specs += [pl.BlockSpec((1, SPLIT[a], CHUNK), slot(a)) for a in range(3)]
    args = [table, inverse, *parts]
    aliases = {}
    if before is not None:
        in_specs.append(pl.BlockSpec(memory_space=pl.ANY))
        args.append(before)
        aliases = {5: 0}
    return pl.pallas_call(
        apply_kernel,
        grid_spec=pltpu.PrefetchScalarGridSpec(
            num_scalar_prefetch=1,
            grid=(4,),
            in_specs=in_specs,
            out_specs=pl.BlockSpec((K, CHUNK), lambda i, t: (0, t[0, half * 4 + i])),
        ),
        out_shape=jax.ShapeDtypeStruct((K, 8 * CHUNK), F32),
        input_output_aliases=aliases,
        compiler_params=pltpu.CompilerParams(vmem_limit_bytes=12 * MIB),
        cost_estimate=pl.CostEstimate(flops=10**9, bytes_accessed=4 * MIB, transcendentals=0),
        name=f"apply_{half}",
    )(*args)


def send(value, pairs):
    return lax.ppermute(value, AXES, pairs)


def scatter_step(state, half, pairs):
    got = send(state[half:], pairs)
    return jnp.concatenate([state[:half], state[2 * half :]], axis=0) + got


def total_over_devices(kept, sent, extra):
    states = []
    for chain in range(3):
        rows = 4 * SPLIT[chain]
        own, other = kept[chain].reshape(rows, CHUNK), sent[chain].reshape(rows, CHUNK)
        if extra[chain] is not None:
            own = jnp.concatenate([own, extra[chain]], axis=0)
            other = jnp.concatenate([other, extra[chain]], axis=0)
        states.append(own + send(other, CORE_PAIRS))
    for step in range(2):
        for chain in range(3):
            half = SPLIT[chain] * (2 >> step)
            states[chain] = scatter_step(states[chain], half, ring_pairs(chain, step))
    for turn in (1, 2):
        for step in range(2):
            for chain in range(3):
                axis = (chain + turn) % 3
                states[chain] = states[chain] + send(states[chain], ring_pairs(axis, step))
    sums = [states[chain][SPLIT[chain] :] for chain in range(3)]
    parts = [states[chain][: SPLIT[chain]] for chain in range(3)]
    for step in (1, 0):
        for chain in range(3):
            got = send(parts[chain], ring_pairs(chain, step))
            parts[chain] = jnp.concatenate([parts[chain], got], axis=0)
    others = [send(part, CORE_PAIRS) for part in parts]

    def fold(arrays):
        return [a.reshape(4, SPLIT[chain], CHUNK) for chain, a in enumerate(arrays)]

    return fold(parts), fold(others), sums


def per_device(slab, sketch):
    total_rows = slab.shape[0] * lax.axis_size("row") * lax.axis_size("col")
    here = lax.axis_index("row") * lax.axis_size("col") + lax.axis_index("col")
    table = lax.dynamic_index_in_dim(jnp.asarray(order_table()), here, 0, keepdims=False)
    sampled, gram, *chunks = front(table, slab, sketch)
    own, other, sums = total_over_devices(chunks[3:], chunks[:3], (None, gram[:8], gram[8:]))
    inverse, basis = factor(sums[1], sums[2], sampled, math.sqrt(total_rows))
    projection = apply(table, inverse, own, 1)
    projection = apply(table, inverse, other, 0, projection)
    return basis, projection


def solution(mesh):
    return jax.shard_map(
        per_device,
        mesh=mesh,
        in_specs=(P(AXES, None), P()),
        out_specs=(P(AXES, None), P()),
        check_vma=False,
    )
```

time: 364 us -> 113 us (0.31); the launches traced: 358 us -> 113 us
  waiting for transfers between devices: 171 us -> 28.4 us
  other arithmetic: 114 us -> 1.15 us
  Pallas kernels: 0 us -> 36.5 us
  matrix products: 34.7 us -> 0 us
  starting transfers between devices: 16.6 us -> 42.7 us
  between operations: 14.7 us -> 1.04 us
    psum x1 -> x0, waiting for transfers between devices: 162 us -> none  [per_device(): lax.psum(jnp.dot(transposed, slab, precision=highest), ('row', 'col'))]
    another operation x26 -> x0, other arithmetic: 110 us -> none  [the longest x21 86.7 us: merge_level(): return jnp.linalg.cholesky(combined)]
    pallas_call x0 -> x4, Pallas kernels: none -> 36.5 us  [the longest x1 16.8 us: front(): pl.pallas_call(front_kernel, grid_spec=pltpu.PrefetchScalarGridSpec(num_s...]
    dot_general x17 -> x0, matrix products: 34.2 us -> none  [the longest x1 16.2 us: per_device(): jnp.dot(slab, sketch, precision=highest, preferred_element_type=jnp.float32)]
    ppermute x7 -> x30, starting transfers between devices: 16.5 us -> 42.7 us  [send(): return lax.ppermute(value, AXES, pairs)]
    ppermute x7 -> x30, waiting for transfers between devices: 9.55 us -> 28.4 us  [send(): return lax.ppermute(value, AXES, pairs)]
    select_n x7 -> x0, other arithmetic: 4.59 us -> none  [the longest x6 3.94 us: merge_level(): return jnp.linalg.cholesky(combined)]
  transfers between devices with their start and end apart: 8 -> 30, of which waited for: 8 -> 16; matrix products, arithmetic and copies ran while one was open for 1% -> 1% of each run, Pallas kernels for 0% -> 14%
where the time goes in v1:
time: 113 us
  starting transfers between devices  42.7 us (38%)
  Pallas kernels  36.5 us (32%)
  waiting for transfers between devices  28.4 us (25%)
  local copies, waits for them, and re-layouts  3.13 us (3%)
  other arithmetic  1.15 us (1%)
    ppermute x30, starting transfers between devices, send(): return lax.ppermute(value, AXES, pairs)  42.7 us
    ppermute x30, waiting for transfers between devices, send(): return lax.ppermute(value, AXES, pairs)  28.4 us
    pallas_call x1, Pallas kernels, front(): pl.pallas_call(front_kernel, grid_spec=pltpu.PrefetchScalarGridSpec(num_s...  16.8 us
    pallas_call x1, Pallas kernels, factor(): pl.pallas_call(lambda *refs: factor_kernel(scale, *refs), out_shape=[jax....  11.9 us
    pallas_call x2, Pallas kernels, apply(): pl.pallas_call(apply_kernel, grid_spec=pltpu.PrefetchScalarGridSpec(num_s...  7.83 us
  transfers between devices with their start and end apart: 30, of which 16 were waited for; matrix products, arithmetic and copies ran while one was open for 1% of the time, Pallas kernels for 14%

profile of v1, /device:TPU:1, one launch (start us, length us, event | category | flops | bytes accessed | tf_op | source)
XLA Modules:
  0.0 112.9 jit_solution(2024739123310613399)
XLA Ops:
  1.3 2.2 %copy-done = f32[8192,128]{1,0:T(8,128)S(1)} copy-done((f32[8192,128]{1,0:T(8,128)S(1)}, f32[8192,128]{1,0:T(8,128)}, u32[]{:S(2)}) %copy-start) | copy-done | bytes 4194328
  3.5 16.8 %sample_and_product.1 = (f32[512,128]{1,0:T(8,128)S(1)}, f32[16,1024]{1,0:T(8,128)S(1)}, f32[4,48,1024]{2,1,0:T(8,128)S(1)}, f32[4,40,1024]{2,1,0:T(8,128)S(1)},...) custom-call(s32[3,8]{1,0:T(4,128)S(1)} %dynamic-slice_bitcast_fusion, ...), custom_call_target="tpu_custom_call" | custom-call | tf_op jit(solution)/shard_map/sample_and_product/pallas_call | solution.py:145
  23.8 2.9 %collective-permute-start.1 = (f32[88,1024]{1,0:T(8,128)S(1)}, f32[88,1024]{1,0:T(8,128)S(1)}, u32[]{:S(2)}, u32[]{:S(2)}) collective-permute-start(f32[88,1024]{1,0:T(8,128)S(1)} %slice.90), channel_id=1, source_target_pairs={{0,32},{1,33},{2,34},{3,35},{4,36},{5,37},{6,38},{7,39},{8,40},{9,... | collective-permute-start | bytes 1081352 | tf_op jit(solution)/shard_map/ppermute | solution.py:251
  26.9 3.8 %collective-permute-start.8 = (f32[88,1024]{1,0:T(8,128)S(1)}, f32[88,1024]{1,0:T(8,128)S(1)}, u32[]{:S(2)}, u32[]{:S(2)}) collective-permute-start(f32[88,1024]{1,0:T(8,128)S(1)} %slice.97), channel_id=1, source_target_pairs={{0,1},{1,0},{2,3},{3,2},{4,5},{5,4},{6,7},{7,6},{8,9},{9,8},{10,11... | collective-permute-start | bytes 1081352 | tf_op jit(solution)/shard_map/ppermute | solution.py:251
  30.9 2.6 %collective-permute-start.15 = (f32[96,1024]{1,0:T(8,128)S(1)}, f32[96,1024]{1,0:T(8,128)S(1)}, u32[]{:S(2)}, u32[]{:S(2)}) collective-permute-start(f32[96,1024]{1,0:T(8,128)S(1)} %slice.103), channel_id=1, source_target_pairs={{0,4},{1,5},{2,6},{3,7},{4,0},{5,1},{6,2},{7,3},{8,12},{9,13},{10,... | collective-permute-start | bytes 1179656 | tf_op jit(solution)/shard_map/ppermute | solution.py:251
  33.6 2.0 %collective-permute-done.8 = f32[88,1024]{1,0:T(8,128)S(1)} collective-permute-done((f32[88,1024]{1,0:T(8,128)S(1)}, f32[88,1024]{1,0:T(8,128)S(1)}, u32[]{:S(2)}, u32[]{:S(2)}) %collective-permute-start.8) | collective-permute-done | bytes 360480 | tf_op jit(solution)/shard_map/ppermute | solution.py:251
  35.9 3.3 %collective-permute-done.15 = f32[96,1024]{1,0:T(8,128)S(1)} collective-permute-done((f32[96,1024]{1,0:T(8,128)S(1)}, f32[96,1024]{1,0:T(8,128)S(1)}, u32[]{:S(2)}, u32[]{:S(2)}) %collective-permute-start.15) | collective-permute-done | bytes 393248 | tf_op jit(solution)/shard_map/ppermute | solution.py:251
  40.3 3.0 %collective-permute-start.3 = (f32[48,1024]{1,0:T(8,128)S(1)}, f32[48,1024]{1,0:T(8,128)S(1)}, u32[]{:S(2)}, u32[]{:S(2)}) collective-permute-start(f32[48,1024]{1,0:T(8,128)S(1)} %maximum_add_fusion.2), channel_id=1, source_target_pairs={{0,1},{1,0},{2,3},{3,2},{4,5},{5,4},{6,7},{7,6},{8,9},{9,8},{10,11... | collective-permute-start | bytes 589832 | tf_op jit(solution)/shard_map/ppermute | solution.py:251
  43.4 2.6 %collective-permute-start.10 = (f32[48,1024]{1,0:T(8,128)S(1)}, f32[48,1024]{1,0:T(8,128)S(1)}, u32[]{:S(2)}, u32[]{:S(2)}) collective-permute-start(f32[48,1024]{1,0:T(8,128)S(1)} %maximum_add_fusion.3), channel_id=1, source_target_pairs={{0,4},{1,5},{2,6},{3,7},{4,0},{5,1},{6,2},{7,3},{8,12},{9,13},{10,... | collective-permute-start | bytes 589832 | tf_op jit(solution)/shard_map/ppermute | solution.py:251
  47.0 2.3 %collective-permute-done.10 = f32[48,1024]{1,0:T(8,128)S(1)} collective-permute-done((f32[48,1024]{1,0:T(8,128)S(1)}, f32[48,1024]{1,0:T(8,128)S(1)}, u32[]{:S(2)}, u32[]{:S(2)}) %collective-permute-start.10) | collective-permute-done | bytes 196640 | tf_op jit(solution)/shard_map/ppermute | solution.py:251
  49.6 2.2 %collective-permute-done.17 = f32[48,1024]{1,0:T(8,128)S(1)} collective-permute-done((f32[48,1024]{1,0:T(8,128)S(1)}, f32[48,1024]{1,0:T(8,128)S(1)}, u32[]{:S(2)}, u32[]{:S(2)}) %collective-permute-start.17) | collective-permute-done | bytes 196640 | tf_op jit(solution)/shard_map/ppermute | solution.py:251
  52.0 2.3 %collective-permute-start.5 = (f32[48,1024]{1,0:T(8,128)S(1)}, f32[48,1024]{1,0:T(8,128)S(1)}, u32[]{:S(2)}, u32[]{:S(2)}) collective-permute-start(f32[48,1024]{1,0:T(8,128)S(1)} %add.76), channel_id=1, source_target_pairs={{0,4},{1,5},{2,6},{3,7},{4,0},{5,1},{6,2},{7,3},{8,12},{9,13},{10,... | collective-permute-start | bytes 589832 | tf_op jit(solution)/shard_map/ppermute | solution.py:251
  57.3 2.0 %collective-permute-done.5 = f32[48,1024]{1,0:T(8,128)S(1)} collective-permute-done((f32[48,1024]{1,0:T(8,128)S(1)}, f32[48,1024]{1,0:T(8,128)S(1)}, u32[]{:S(2)}, u32[]{:S(2)}) %collective-permute-start.5) | collective-permute-done | bytes 196640 | tf_op jit(solution)/shard_map/ppermute | solution.py:251
  59.5 2.5 %collective-permute-done.12 = f32[48,1024]{1,0:T(8,128)S(1)} collective-permute-done((f32[48,1024]{1,0:T(8,128)S(1)}, f32[48,1024]{1,0:T(8,128)S(1)}, u32[]{:S(2)}, u32[]{:S(2)}) %collective-permute-start.12) | collective-permute-done | bytes 196640 | tf_op jit(solution)/shard_map/ppermute | solution.py:251
  64.4 2.5 %collective-permute-done.13 = f32[48,1024]{1,0:T(8,128)S(1)} collective-permute-done((f32[48,1024]{1,0:T(8,128)S(1)}, f32[48,1024]{1,0:T(8,128)S(1)}, u32[]{:S(2)}, u32[]{:S(2)}) %collective-permute-start.13) | collective-permute-done | bytes 196640 | tf_op jit(solution)/shard_map/ppermute | solution.py:251
  67.0 2.3 %collective-permute-done.20 = f32[48,1024]{1,0:T(8,128)S(1)} collective-permute-done((f32[48,1024]{1,0:T(8,128)S(1)}, f32[48,1024]{1,0:T(8,128)S(1)}, u32[]{:S(2)}, u32[]{:S(2)}) %collective-permute-start.20) | collective-permute-done | bytes 196640 | tf_op jit(solution)/shard_map/ppermute | solution.py:251
  71.5 1.8 %collective-permute-start.28 = (f32[80,1024]{1,0:T(8,128)S(1)}, f32[80,1024]{1,0:T(8,128)S(1)}, u32[]{:S(2)}, u32[]{:S(2)}) collective-permute-start(f32[80,1024]{1,0:T(8,128)S(1)} %pad_maximum_fusion.9), channel_id=1, source_target_pairs={{0,1},{1,0},{2,3},{3,2},{4,5},{5,4},{6,7},{7,6},{8,9},{9,8},{10,11... | collective-permute-start | bytes 983048 | tf_op jit(solution)/shard_map/ppermute | solution.py:251
  75.6 2.3 %collective-permute-done.25 = f32[80,1024]{1,0:T(8,128)S(1)} collective-permute-done((f32[80,1024]{1,0:T(8,128)S(1)}, f32[80,1024]{1,0:T(8,128)S(1)}, u32[]{:S(2)}, u32[]{:S(2)}) %collective-permute-start.25) | collective-permute-done | bytes 327712 | tf_op jit(solution)/shard_map/ppermute | solution.py:251
  78.0 8.6 %collective-permute-start.26 = (f32[160,1024]{1,0:T(8,128)S(1)}, f32[160,1024]{1,0:T(8,128)S(1)}, u32[]{:S(2)}, u32[]{:S(2)}) collective-permute-start(f32[160,1024]{1,0:T(8,128)S(1)} %pad_maximum_fusion.5), channel_id=1, source_target_pairs={{0,16},{1,17},{2,18},{3,19},{4,20},{5,21},{6,22},{7,23},{8,24},{9,... | collective-permute-start | bytes 1966088 | tf_op jit(solution)/shard_map/ppermute | solution.py:251
  86.6 2.3 %collective-permute-start.29 = (f32[160,1024]{1,0:T(8,128)S(1)}, f32[160,1024]{1,0:T(8,128)S(1)}, u32[]{:S(2)}, u32[]{:S(2)}) collective-permute-start(f32[160,1024]{1,0:T(8,128)S(1)} %pad_maximum_fusion.6), channel_id=1, source_target_pairs={{0,16},{1,17},{2,18},{3,19},{4,20},{5,21},{6,22},{7,23},{8,24},{9,... | collective-permute-start | bytes 1966088 | tf_op jit(solution)/shard_map/ppermute | solution.py:251
  89.0 4.2 %collective-permute-start.23 = (f32[192,1024]{1,0:T(8,128)S(1)}, f32[192,1024]{1,0:T(8,128)S(1)}, u32[]{:S(2)}, u32[]{:S(2)}) collective-permute-start(f32[192,1024]{1,0:T(8,128)S(1)} %pad_maximum_fusion.4), channel_id=1, source_target_pairs={{0,16},{1,17},{2,18},{3,19},{4,20},{5,21},{6,22},{7,23},{8,24},{9,... | collective-permute-start | bytes 2359304 | tf_op jit(solution)/shard_map/ppermute | solution.py:251
  93.2 11.9 %factor_and_basis.1 = (f32[128,128]{1,0:T(8,128)S(1)}, f32[512,128]{1,0:T(8,128)}) custom-call(f32[8,1024]{1,0:T(8,128)S(1)} %slice.94.refs_0_, f32[8,1024]{1,0:T(8,128)S(1)} %slice.101.refs_1_, f32[512,128]{1,0:T(8,128)S(1)} %get-tuple-element.17.refs_2_), custom_call_target="tpu_custom_call" | custom-call | flops 8000000000 | bytes 1048576 | tf_op jit(solution)/shard_map/factor_and_basis/pallas_call | solution.py:207
  105.1 3.9 %apply_1.1.rest_0_ = f32[128,8192]{1,0:T(8,128)} custom-call(s32[3,8]{1,0:T(4,128)S(1)} %dynamic-slice_bitcast_fusion.table, f32[128,128]{1,0:T(8,128)S(1)} %get-tuple-element.19.inverse, f32[4,48,1024]{2,1,0:T(8,128)S(1)} %bitcast.15, f32[4,40,1024]{2,1,0:T(8,128)S(1)} %bitcast.16, f32[4,40,1024]{2,1,0:T(8,128)S(1)} %bitcast.17), custom_call_target="tpu_custom_call" | custom-call | flops 1000000000 | bytes 4194304 | tf_op jit(solution)/shard_map/apply_1/pallas_call | solution.py:234
  109.0 3.9 %apply_0.1 = f32[128,8192]{1,0:T(8,128)} custom-call(s32[3,8]{1,0:T(4,128)S(1)} %dynamic-slice_bitcast_fusion.table, f32[128,128]{1,0:T(8,128)S(1)} %get-tuple-element.19.inverse, f32[4,48,1024]{2,1,0:T(8,128)S(1)} %bitcast.18, f32[4,40,1024]{2,1,0:T(8,128)S(1)} %bitcast.19, f32[4,40,1024]{2,1,0:T(8,128)S(1)} %bitcast.20, ...), custom_call_target="tpu_custom_call", output_to_operand_aliasing={{}: (5, {})} | custom-call | flops 1000000000 | bytes 4194304 | tf_op jit(solution)/shard_map/apply_0/pallas_call | solution.py:234
  (91 shorter events, 17.9 us)
Async XLA Ops:
  22.1 8.7 %collective-permute-start.14 = (f32[192,1024]{1,0:T(8,128)S(1)}, f32[192,1024]{1,0:T(8,128)S(1)}, u32[]{:S(2)}, u32[]{:S(2)}) collective-permute-start(f32[192,1024]{1,0:T(8,128)S(1)} %bitcast.25), channel_id=1, source_target_pairs={{0,16},{1,17},{2,18},{3,19},{4,20},{5,21},{6,22},{7,23},{8,24},{9,... | collective-permute-start | bytes 2359304 | tf_op jit(solution)/shard_map/ppermute | solution.py:251
  23.8 9.7 %collective-permute-start.1 = (f32[88,1024]{1,0:T(8,128)S(1)}, f32[88,1024]{1,0:T(8,128)S(1)}, u32[]{:S(2)}, u32[]{:S(2)}) collective-permute-start(f32[88,1024]{1,0:T(8,128)S(1)} %slice.90), channel_id=1, source_target_pairs={{0,32},{1,33},{2,34},{3,35},{4,36},{5,37},{6,38},{7,39},{8,40},{9,... | collective-permute-start | bytes 1081352 | tf_op jit(solution)/shard_map/ppermute | solution.py:251
  26.9 8.7 %collective-permute-start.8 = (f32[88,1024]{1,0:T(8,128)S(1)}, f32[88,1024]{1,0:T(8,128)S(1)}, u32[]{:S(2)}, u32[]{:S(2)}) collective-permute-start(f32[88,1024]{1,0:T(8,128)S(1)} %slice.97), channel_id=1, source_target_pairs={{0,1},{1,0},{2,3},{3,2},{4,5},{5,4},{6,7},{7,6},{8,9},{9,8},{10,11... | collective-permute-start | bytes 1081352 | tf_op jit(solution)/shard_map/ppermute | solution.py:251
  30.9 8.2 %collective-permute-start.15 = (f32[96,1024]{1,0:T(8,128)S(1)}, f32[96,1024]{1,0:T(8,128)S(1)}, u32[]{:S(2)}, u32[]{:S(2)}) collective-permute-start(f32[96,1024]{1,0:T(8,128)S(1)} %slice.103), channel_id=1, source_target_pairs={{0,4},{1,5},{2,6},{3,7},{4,0},{5,1},{6,2},{7,3},{8,12},{9,13},{10,... | collective-permute-start | bytes 1179656 | tf_op jit(solution)/shard_map/ppermute | solution.py:251
  35.8 7.6 %collective-permute-start.9 = (f32[48,1024]{1,0:T(8,128)S(1)}, f32[48,1024]{1,0:T(8,128)S(1)}, u32[]{:S(2)}, u32[]{:S(2)}) collective-permute-start(f32[48,1024]{1,0:T(8,128)S(1)} %slice.100), channel_id=1, source_target_pairs={{0,3},{1,2},{2,1},{3,0},{4,7},{5,6},{6,5},{7,4},{8,11},{9,10},{10,... | collective-permute-start | bytes 589832 | tf_op jit(solution)/shard_map/ppermute | solution.py:251
  39.2 6.7 %collective-permute-start.16 = (f32[48,1024]{1,0:T(8,128)S(1)}, f32[48,1024]{1,0:T(8,128)S(1)}, u32[]{:S(2)}, u32[]{:S(2)}) collective-permute-start(f32[48,1024]{1,0:T(8,128)S(1)} %slice.105), channel_id=1, source_target_pairs={{0,12},{1,13},{2,14},{3,15},{4,8},{5,9},{6,10},{7,11},{8,4},{9,5},... | collective-permute-start | bytes 589832 | tf_op jit(solution)/shard_map/ppermute | solution.py:251
  40.3 6.5 %collective-permute-start.3 = (f32[48,1024]{1,0:T(8,128)S(1)}, f32[48,1024]{1,0:T(8,128)S(1)}, u32[]{:S(2)}, u32[]{:S(2)}) collective-permute-start(f32[48,1024]{1,0:T(8,128)S(1)} %maximum_add_fusion.2), channel_id=1, source_target_pairs={{0,1},{1,0},{2,3},{3,2},{4,5},{5,4},{6,7},{7,6},{8,9},{9,8},{10,11... | collective-permute-start | bytes 589832 | tf_op jit(solution)/shard_map/ppermute | solution.py:251
  43.4 5.8 %collective-permute-start.10 = (f32[48,1024]{1,0:T(8,128)S(1)}, f32[48,1024]{1,0:T(8,128)S(1)}, u32[]{:S(2)}, u32[]{:S(2)}) collective-permute-start(f32[48,1024]{1,0:T(8,128)S(1)} %maximum_add_fusion.3), channel_id=1, source_target_pairs={{0,4},{1,5},{2,6},{3,7},{4,0},{5,1},{6,2},{7,3},{8,12},{9,13},{10,... | collective-permute-start | bytes 589832 | tf_op jit(solution)/shard_map/ppermute | solution.py:251
  46.0 5.8 %collective-permute-start.17 = (f32[48,1024]{1,0:T(8,128)S(1)}, f32[48,1024]{1,0:T(8,128)S(1)}, u32[]{:S(2)}, u32[]{:S(2)}) collective-permute-start(f32[48,1024]{1,0:T(8,128)S(1)} %slice_add_fusion.1), channel_id=1, source_target_pairs={{0,32},{1,33},{2,34},{3,35},{4,36},{5,37},{6,38},{7,39},{8,40},{9,... | collective-permute-start | bytes 589832 | tf_op jit(solution)/shard_map/ppermute | solution.py:251
  46.9 5.1 %collective-permute-start.4 = (f32[48,1024]{1,0:T(8,128)S(1)}, f32[48,1024]{1,0:T(8,128)S(1)}, u32[]{:S(2)}, u32[]{:S(2)}) collective-permute-start(f32[48,1024]{1,0:T(8,128)S(1)} %add.75), channel_id=1, source_target_pairs={{0,3},{1,2},{2,1},{3,0},{4,7},{5,6},{6,5},{7,4},{8,11},{9,10},{10,... | collective-permute-start | bytes 589832 | tf_op jit(solution)/shard_map/ppermute | solution.py:251
  49.2 5.0 %collective-permute-start.11 = (f32[48,1024]{1,0:T(8,128)S(1)}, f32[48,1024]{1,0:T(8,128)S(1)}, u32[]{:S(2)}, u32[]{:S(2)}) collective-permute-start(f32[48,1024]{1,0:T(8,128)S(1)} %add.82), channel_id=1, source_target_pairs={{0,12},{1,13},{2,14},{3,15},{4,8},{5,9},{6,10},{7,11},{8,4},{9,5},... | collective-permute-start | bytes 589832 | tf_op jit(solution)/shard_map/ppermute | solution.py:251
  52.0 7.4 %collective-permute-start.5 = (f32[48,1024]{1,0:T(8,128)S(1)}, f32[48,1024]{1,0:T(8,128)S(1)}, u32[]{:S(2)}, u32[]{:S(2)}) collective-permute-start(f32[48,1024]{1,0:T(8,128)S(1)} %add.76), channel_id=1, source_target_pairs={{0,4},{1,5},{2,6},{3,7},{4,0},{5,1},{6,2},{7,3},{8,12},{9,13},{10,... | collective-permute-start | bytes 589832 | tf_op jit(solution)/shard_map/ppermute | solution.py:251
  54.3 7.7 %collective-permute-start.12 = (f32[48,1024]{1,0:T(8,128)S(1)}, f32[48,1024]{1,0:T(8,128)S(1)}, u32[]{:S(2)}, u32[]{:S(2)}) collective-permute-start(f32[48,1024]{1,0:T(8,128)S(1)} %add.83), channel_id=1, source_target_pairs={{0,32},{1,33},{2,34},{3,35},{4,36},{5,37},{6,38},{7,39},{8,40},{9,... | collective-permute-start | bytes 589832 | tf_op jit(solution)/shard_map/ppermute | solution.py:251
  56.7 5.8 %collective-permute-start.19 = (f32[48,1024]{1,0:T(8,128)S(1)}, f32[48,1024]{1,0:T(8,128)S(1)}, u32[]{:S(2)}, u32[]{:S(2)}) collective-permute-start(f32[48,1024]{1,0:T(8,128)S(1)} %add.90), channel_id=1, source_target_pairs={{0,1},{1,0},{2,3},{3,2},{4,5},{5,4},{6,7},{7,6},{8,9},{9,8},{10,11... | collective-permute-start | bytes 589832 | tf_op jit(solution)/shard_map/ppermute | solution.py:251
  59.4 4.9 %collective-permute-start.6 = (f32[48,1024]{1,0:T(8,128)S(1)}, f32[48,1024]{1,0:T(8,128)S(1)}, u32[]{:S(2)}, u32[]{:S(2)}) collective-permute-start(f32[48,1024]{1,0:T(8,128)S(1)} %add.77), channel_id=1, source_target_pairs={{0,12},{1,13},{2,14},{3,15},{4,8},{5,9},{6,10},{7,11},{8,4},{9,5},... | collective-permute-start | bytes 589832 | tf_op jit(solution)/shard_map/ppermute | solution.py:251
  62.0 4.9 %collective-permute-start.13 = (f32[48,1024]{1,0:T(8,128)S(1)}, f32[48,1024]{1,0:T(8,128)S(1)}, u32[]{:S(2)}, u32[]{:S(2)}) collective-permute-start(f32[48,1024]{1,0:T(8,128)S(1)} %add.84), channel_id=1, source_target_pairs={{0,96},{1,97},{2,98},{3,99},{4,100},{5,101},{6,102},{7,103},{8,104... | collective-permute-start | bytes 589832 | tf_op jit(solution)/shard_map/ppermute | solution.py:251
  62.6 6.7 %collective-permute-start.20 = (f32[48,1024]{1,0:T(8,128)S(1)}, f32[48,1024]{1,0:T(8,128)S(1)}, u32[]{:S(2)}, u32[]{:S(2)}) collective-permute-start(f32[48,1024]{1,0:T(8,128)S(1)} %add.91), channel_id=1, source_target_pairs={{0,3},{1,2},{2,1},{3,0},{4,7},{5,6},{6,5},{7,4},{8,11},{9,10},{10,... | collective-permute-start | bytes 589832 | tf_op jit(solution)/shard_map/ppermute | solution.py:251
  64.3 5.2 %collective-permute-start.24 = (f32[40,1024]{1,0:T(8,128)S(1)}, f32[40,1024]{1,0:T(8,128)S(1)}, u32[]{:S(2)}, u32[]{:S(2)}) collective-permute-start(f32[40,1024]{1,0:T(8,128)S(1)} %slice.106), channel_id=1, source_target_pairs={{0,96},{1,97},{2,98},{3,99},{4,100},{5,101},{6,102},{7,103},{8,104... | collective-permute-start | bytes 491528 | tf_op jit(solution)/shard_map/ppermute | solution.py:251
  69.6 8.3 %collective-permute-start.25 = (f32[80,1024]{1,0:T(8,128)S(1)}, f32[80,1024]{1,0:T(8,128)S(1)}, u32[]{:S(2)}, u32[]{:S(2)}) collective-permute-start(f32[80,1024]{1,0:T(8,128)S(1)} %pad_maximum_fusion.8), channel_id=1, source_target_pairs={{0,32},{1,33},{2,34},{3,35},{4,36},{5,37},{6,38},{7,39},{8,40},{9,... | collective-permute-start | bytes 983048 | tf_op jit(solution)/shard_map/ppermute | solution.py:251
  71.5 15.1 %collective-permute-start.28 = (f32[80,1024]{1,0:T(8,128)S(1)}, f32[80,1024]{1,0:T(8,128)S(1)}, u32[]{:S(2)}, u32[]{:S(2)}) collective-permute-start(f32[80,1024]{1,0:T(8,128)S(1)} %pad_maximum_fusion.9), channel_id=1, source_target_pairs={{0,1},{1,0},{2,3},{3,2},{4,5},{5,4},{6,7},{7,6},{8,9},{9,8},{10,11... | collective-permute-start | bytes 983048 | tf_op jit(solution)/shard_map/ppermute | solution.py:251
  74.0 15.0 %collective-permute-start.22 = (f32[96,1024]{1,0:T(8,128)S(1)}, f32[96,1024]{1,0:T(8,128)S(1)}, u32[]{:S(2)}, u32[]{:S(2)}) collective-permute-start(f32[96,1024]{1,0:T(8,128)S(1)} %pad_maximum_fusion.7), channel_id=1, source_target_pairs={{0,4},{1,5},{2,6},{3,7},{4,0},{5,1},{6,2},{7,3},{8,12},{9,13},{10,... | collective-permute-start | bytes 1179656 | tf_op jit(solution)/shard_map/ppermute | solution.py:251
  78.0 31.1 %collective-permute-start.26 = (f32[160,1024]{1,0:T(8,128)S(1)}, f32[160,1024]{1,0:T(8,128)S(1)}, u32[]{:S(2)}, u32[]{:S(2)}) collective-permute-start(f32[160,1024]{1,0:T(8,128)S(1)} %pad_maximum_fusion.5), channel_id=1, source_target_pairs={{0,16},{1,17},{2,18},{3,19},{4,20},{5,21},{6,22},{7,23},{8,24},{9,... | collective-permute-start | bytes 1966088 | tf_op jit(solution)/shard_map/ppermute | solution.py:251
  86.6 22.4 %collective-permute-start.29 = (f32[160,1024]{1,0:T(8,128)S(1)}, f32[160,1024]{1,0:T(8,128)S(1)}, u32[]{:S(2)}, u32[]{:S(2)}) collective-permute-start(f32[160,1024]{1,0:T(8,128)S(1)} %pad_maximum_fusion.6), channel_id=1, source_target_pairs={{0,16},{1,17},{2,18},{3,19},{4,20},{5,21},{6,22},{7,23},{8,24},{9,... | collective-permute-start | bytes 1966088 | tf_op jit(solution)/shard_map/ppermute | solution.py:251
  89.0 20.0 %collective-permute-start.23 = (f32[192,1024]{1,0:T(8,128)S(1)}, f32[192,1024]{1,0:T(8,128)S(1)}, u32[]{:S(2)}, u32[]{:S(2)}) collective-permute-start(f32[192,1024]{1,0:T(8,128)S(1)} %pad_maximum_fusion.4), channel_id=1, source_target_pairs={{0,16},{1,17},{2,18},{3,19},{4,20},{5,21},{6,22},{7,23},{8,24},{9,... | collective-permute-start | bytes 2359304 | tf_op jit(solution)/shard_map/ppermute | solution.py:251
  (7 other events, 28.9 us)

commit v2 on v0

v2 whole, which is shorter than its diff:
```python
import math

import jax
import jax.numpy as jnp
from jax import lax
from jax.experimental import pallas as pl
from jax.experimental.pallas import tpu as pltpu
from jax.sharding import PartitionSpec as P

AXES = ("row", "col")
RING = 4
K = 128
CHUNK = 1024
HALF = 4096
WIDTH = (384, 384, 256)
STARTS = (0, 1536, 3072)
GRAM = 64
AHEAD = 8
QUARTERS = (156, 180)
SLOTS = (120, 180)
MIB = 2**20
F32 = jnp.float32
BF16 = jnp.bfloat16
HIGHEST = lax.Precision.HIGHEST
VMEM = pl.BlockSpec(memory_space=pltpu.VMEM)
HBM = pl.BlockSpec(memory_space=pltpu.HBM)


def places():
    return [
        (x, y, z, c) for y in range(RING) for c in range(2) for x in range(RING) for z in range(RING)
    ]


def linear(x, y, z, c):
    return (y * 2 + c) * RING * RING + x * RING + z


def side_of(x, y, z, core):
    return core ^ ((x + y + z) & 1)


def beside(place, step, side):
    return place ^ 1 if (step ^ side) == 0 else place ^ 3


def ring_pairs(axis, step):
    pairs = []
    for x, y, z, c in places():
        to = [x, y, z]
        to[axis] = beside(to[axis], step, side_of(x, y, z, c))
        pairs.append((linear(x, y, z, c), linear(*to, 1 - c)))
    return pairs


CORE_PAIRS = [(linear(x, y, z, c), linear(x, y, z, 1 - c)) for x, y, z, c in places()]


def here():
    row, col = lax.axis_index("row"), lax.axis_index("col")
    place = (col // RING, row // 2, col % RING)
    return place, side_of(*place, row % 2)


def two_bits(choices, side, at):
    return (jnp.where(side == 0, choices[0], choices[1]) >> (2 * at)) & 3


def halves(value):
    high = value.astype(BF16)
    return high, (value - high.astype(F32)).astype(BF16)


def mul(a, b):
    return jnp.dot(a, b, preferred_element_type=F32)


def products(left, high, low, outs, side):
    place, _ = here()
    for chain in range(3):
        width = WIDTH[chain]
        for pair in range(2):
            at = pl.ds(STARTS[chain] + 2 * pair * width, 2 * width)
            both = mul(left[...], high[:, at])
            value = both[:K] + (both[K:] + mul(left[:K], low[:, at]))
            for part in range(2):
                slot = two_bits(SLOTS, side, (2 * pair + part) ^ place[chain])
                rows = pl.ds(pl.multiple_of(slot * K, K), K)
                outs[chain][rows] = value[:, part * width : (part + 1) * width]


def sample_kernel(
    slab, sketch, sampled, left, high, low, xs, ys, zs,
    slab_here, sketch_here, sent_high, sent_low, slab_done, sketch_done,
):
    _, side = here()
    depth = slab_here.shape[0]

    def column(k):
        half = 1 - side if k < 4 else side
        return pl.multiple_of(half * HALF + (k % 4) * CHUNK, CHUNK)

    def slab_copy(k):
        return pltpu.make_async_copy(
            slab.at[:, pl.ds(column(k), CHUNK)], slab_here.at[k % depth], slab_done.at[k % depth]
        )

    def sketch_copy(k):
        return pltpu.make_async_copy(sketch.at[pl.ds(column(k), CHUNK)], sketch_here.at[k], sketch_done.at[k])

    for k in range(8):
        sketch_copy(k).start()
        if k < depth:
            slab_copy(k).start()
    for k in range(8):
        slab_copy(k).wait()
        slab_high, slab_low = halves(slab_here[k % depth])
        at = pl.ds((k % 4) * CHUNK, CHUNK)
        if k < 4:
            sent_high[:, at], sent_low[:, at] = slab_high, slab_low
        else:
            high[:, at], low[:, at] = slab_high, slab_low
        if k + depth < 8:
            slab_copy(k + depth).start()
        sketch_copy(k).wait()
        sketch_high, sketch_low = halves(sketch_here[k])
        both = mul(slab_high, jnp.concatenate([sketch_high, sketch_low], axis=1))
        value = both[:, :K] + (both[:, K:] + mul(slab_low, sketch_high))
        if k == 0:
            sampled[...] = value
        else:
            sampled[...] += value
    left[...] = jnp.concatenate(halves(sampled[...].T), axis=0)
    square = lax.dot_general(left[...], left[...], (((1,), (1,)), ((), ())), preferred_element_type=F32)
    gram = (square[:K, :K] + square[K:, K:]) + (square[:K, K:] + square[K:, :K])
    zs[4 * K :] = jnp.concatenate([gram[:GRAM], gram[GRAM:]], axis=1)
    products(left, sent_high, sent_low, (xs, ys, zs), 1 - side)


def sample(slab, sketch):
    rows = slab.shape[0]
    depth = 5
    return pl.pallas_call(
        sample_kernel,
        in_specs=[HBM, HBM],
        out_specs=[VMEM] * 7,
        out_shape=[
            jax.ShapeDtypeStruct((rows, K), F32),
            jax.ShapeDtypeStruct((2 * K, rows), BF16),
            jax.ShapeDtypeStruct((rows, HALF), BF16),
            jax.ShapeDtypeStruct((rows, HALF), BF16),
            jax.ShapeDtypeStruct((4 * K, WIDTH[0]), F32),
            jax.ShapeDtypeStruct((4 * K, WIDTH[1]), F32),
            jax.ShapeDtypeStruct((4 * K + GRAM, WIDTH[2]), F32),
        ],
        scratch_shapes=[
            pltpu.VMEM((depth, rows, CHUNK), F32),
            pltpu.VMEM((8, CHUNK, K), F32),
            pltpu.VMEM((rows, HALF), BF16),
            pltpu.VMEM((rows, HALF), BF16),
            pltpu.SemaphoreType.DMA((depth,)),
            pltpu.SemaphoreType.DMA((8,)),
        ],
        compiler_params=pltpu.CompilerParams(vmem_limit_bytes=40 * MIB),
        cost_estimate=pl.CostEstimate(flops=8 * 10**9, bytes_accessed=21 * MIB, transcendentals=0),
        name="sample",
    )(slab, sketch)


def keep_kernel(left, high, low, sent, x, y, z):
    _, side = here()
    z[4 * K :] = sent[4 * K :]
    products(left, high, low, (x, y, z), side)


def keep(left, high, low, sent):
    return pl.pallas_call(
        keep_kernel,
        in_specs=[VMEM] * 4,
        out_specs=[VMEM] * 3,
        out_shape=[
            jax.ShapeDtypeStruct((4 * K, WIDTH[0]), F32),
            jax.ShapeDtypeStruct((4 * K, WIDTH[1]), F32),
            jax.ShapeDtypeStruct((4 * K + GRAM, WIDTH[2]), F32),
        ],
        compiler_params=pltpu.CompilerParams(vmem_limit_bytes=20 * MIB),
        cost_estimate=pl.CostEstimate(flops=2 * 10**9, bytes_accessed=MIB, transcendentals=0),
        name="keep",
    )(left, high, low, sent)


def factor_kernel(folded, inverse):
    left = jnp.concatenate([folded[:, :K], folded[:, K:]], axis=0)
    row = lax.broadcasted_iota(jnp.int32, (K, K), 0)
    col = lax.broadcasted_iota(jnp.int32, (K, K), 1)
    right = jnp.where(row == col, 1.0, 0.0).astype(F32)
    lefts = [left[8 * t : 8 * t + 8] for t in range(16)]
    rights = [right[8 * t : 8 * t + 8] for t in range(16)]
    sub = lax.broadcasted_iota(jnp.int32, (8, K), 0)
    for start in range(0, K, AHEAD):
        tile, at = divmod(start, 8)
        columns = [
            [jnp.broadcast_to(lefts[t][:, start + k : start + k + 1], (8, K)) for t in range(tile, 16)]
            for k in range(AHEAD)
        ]
        rows_left = [jnp.broadcast_to(lefts[tile][at + k : at + k + 1], (8, K)) for k in range(AHEAD)]
        rows_right = [jnp.broadcast_to(rights[tile][at + k : at + k + 1], (8, K)) for k in range(AHEAD)]

        def entry(r, c):
            return jnp.broadcast_to(columns[c][0][at + r : at + r + 1], (8, K))

        for k in range(AHEAD):
            down = 1.0 / entry(k, k)
            below = [entry(m, k) for m in range(k + 1, AHEAD)]
            rows_left[k] = rows_left[k] * down
            rows_right[k] = rows_right[k] * down
            for m in range(k + 1, AHEAD):
                rows_left[m] = rows_left[m] - below[m - k - 1] * rows_left[k]
                rows_right[m] = rows_right[m] - below[m - k - 1] * rows_right[k]
                share = below[m - k - 1] * down
                columns[m] = [own - other * share for own, other in zip(columns[m], columns[k])]
        for k in range(AHEAD):
            columns[k][0] = jnp.where(sub > at + k, columns[k][0], 0.0)
        for t in range(tile, 16):
            for k in range(AHEAD):
                lefts[t] = lefts[t] - columns[k][t - tile] * rows_left[k]
                rights[t] = rights[t] - columns[k][t - tile] * rows_right[k]
    left = jnp.concatenate(lefts, axis=0)
    right = jnp.concatenate(rights, axis=0)
    diagonal = jnp.sum(jnp.where(row == col, left, 0.0), axis=1, keepdims=True)
    inverse[...] = right * lax.rsqrt(diagonal)


def factor(folded):
    return pl.pallas_call(
        factor_kernel,
        in_specs=[VMEM],
        out_specs=VMEM,
        out_shape=jax.ShapeDtypeStruct((K, K), F32),
        cost_estimate=pl.CostEstimate(flops=6 * 10**9, bytes_accessed=MIB, transcendentals=0),
        compiler_params=pltpu.CompilerParams(vmem_limit_bytes=8 * MIB),
        name="factor",
    )(folded)


def basis_kernel(scale, inverse, sampled, out):
    out[...] = scale * jnp.dot(sampled[...], inverse[...].T, precision=HIGHEST, preferred_element_type=F32)


def basis(inverse, sampled, scale):
    return pl.pallas_call(
        lambda *refs: basis_kernel(scale, *refs),
        in_specs=[VMEM, VMEM],
        out_specs=VMEM,
        out_shape=jax.ShapeDtypeStruct(sampled.shape, F32),
        cost_estimate=pl.CostEstimate(flops=10**9, bytes_accessed=MIB, transcendentals=0),
        compiler_params=pltpu.CompilerParams(vmem_limit_bytes=8 * MIB),
        name="basis",
    )(inverse, sampled)


def call_in_turn(body, args, shapes, after, name):
    extra = [] if after is None else [after]
    any_space = pl.BlockSpec(memory_space=pl.ANY)

    def kernel(*refs):
        body(*refs[: len(args)], *refs[len(args) + len(extra) :])

    return pl.pallas_call(
        kernel,
        in_specs=[VMEM] * len(args) + [any_space] * len(extra),
        out_specs=[VMEM] * len(shapes),
        out_shape=[jax.ShapeDtypeStruct(shape, F32) for shape in shapes],
        compiler_params=pltpu.CompilerParams(vmem_limit_bytes=MIB),
        cost_estimate=pl.CostEstimate(flops=10**8, bytes_accessed=MIB // 4, transcendentals=0),
        name=name,
    )(*args, *extra)


def split(total, rest, keep, hand):
    half = keep.shape[0]
    keep[...] = total[:half]
    hand[:half] = total[half:]
    if rest is not None:
        hand[half:] = rest


def sum_cores(kept, got, after):
    rows, width = kept.shape

    def body(kept_ref, got_ref, keep, hand):
        rest = kept_ref[4 * K :] + got_ref[4 * K :] if rows > 4 * K else None
        split(kept_ref[: 4 * K] + got_ref[: 4 * K], rest, keep, hand)

    return call_in_turn(body, [kept, got], [(2 * K, width), (rows - 2 * K, width)], after, "sum_cores")


def sum_half(kept, handed, got, after):
    half, width = kept.shape
    rest = handed.shape[0] - half

    def total(kept_ref, handed_ref, got_ref):
        more = handed_ref[half:] + got_ref[half:] if rest else None
        return kept_ref[...] + got_ref[:half], more

    def halve(kept_ref, handed_ref, got_ref, keep, hand):
        split(*total(kept_ref, handed_ref, got_ref), keep, hand)

    def finish(kept_ref, handed_ref, got_ref, out):
        value, more = total(kept_ref, handed_ref, got_ref)
        out[:half] = value
        if rest:
            out[half:] = more

    args = [kept, handed, got]
    if half == K:
        return call_in_turn(finish, args, [(half + rest, width)], after, "sum_quarter")[0]
    return call_in_turn(halve, args, [(half // 2, width), (half // 2 + rest, width)], after, "sum_half")


def sum_whole(state, got, after):
    def body(state_ref, got_ref, out):
        out[...] = state_ref[...] + got_ref[...]

    return call_in_turn(body, [state, got], [state.shape], after, "sum_whole")[0]


def sum_last(state, got, after):
    rows, width = state.shape

    def body(state_ref, got_ref, own, *rest):
        own[...] = state_ref[:K] + got_ref[:K]
        if rest:
            rest[0][...] = state_ref[K:] + got_ref[K:]

    shapes = [(K, width)] + ([(rows - K, width)] if rows > K else [])
    return call_in_turn(body, [state, got], shapes, after, "sum_last")


def join(own, got, after):
    rows, width = own.shape

    def body(own_ref, got_ref, out):
        out[:rows] = own_ref[...]
        out[rows:] = got_ref[...]

    return call_in_turn(body, [own, got], [(2 * rows, width)], after, "join")[0]


def pass_on(value, after):
    any_space = pl.BlockSpec(memory_space=pl.ANY)
    return pl.pallas_call(
        lambda *refs: None,
        in_specs=[any_space] * 2,
        out_specs=any_space,
        out_shape=jax.ShapeDtypeStruct(value.shape, value.dtype),
        input_output_aliases={0: 0},
        compiler_params=pltpu.CompilerParams(vmem_limit_bytes=MIB),
        name="pass_on",
    )(value, after)


def apply_kernel(pieces, inverse, *rest):
    arrays, (out, *ready, done) = rest[: len(pieces)], rest[-5:]
    place, side = here()
    high, low = halves(inverse[...])
    wide = jnp.concatenate([high, high], axis=1)
    copies = []
    filled = [0, 0, 0]
    for array, (chain, other, first) in zip(arrays, pieces):
        owner = 1 - side if other else side
        width = WIDTH[chain]
        for i in range(2):
            value_high, value_low = halves(array[K * i : K * i + K])
            at = filled[chain]
            filled[chain] += 1
            stacked = jnp.concatenate([value_high, value_low], axis=0)
            ready[chain][at] = mul(wide, stacked) + mul(low, value_high)
            quarter = place[chain] ^ two_bits(QUARTERS, owner, first + i)
            column = pl.multiple_of(owner * HALF + STARTS[chain] + quarter * width, K)
            copies.append(
                pltpu.make_async_copy(ready[chain].at[at], out.at[:, pl.ds(column, width)], done.at[len(copies)])
            )
            copies[-1].start()
    for copy in copies:
        copy.wait()


def apply(inverse, parts, pieces, before, name):
    aliases = {} if before is None else {1 + len(parts): 0}
    args = [inverse, *parts] + ([] if before is None else [before])
    most = [2 * sum(piece[0] == chain for piece in pieces) for chain in range(3)]
    return pl.pallas_call(
        lambda *refs: apply_kernel(pieces, *refs),
        in_specs=[VMEM] * (1 + len(parts)) + [HBM] * len(aliases),
        out_specs=HBM,
        out_shape=jax.ShapeDtypeStruct((K, 2 * HALF), F32),
        scratch_shapes=[
            *[pltpu.VMEM((max(most[chain], 1), K, WIDTH[chain]), F32) for chain in range(3)],
            pltpu.SemaphoreType.DMA((2 * len(pieces),)),
        ],
        input_output_aliases=aliases,
        compiler_params=pltpu.CompilerParams(vmem_limit_bytes=12 * MIB),
        cost_estimate=pl.CostEstimate(flops=10**9, bytes_accessed=2 * MIB, transcendentals=0),
        name=name,
    )(*args)


def send(value, pairs):
    return lax.ppermute(value, AXES, pairs)


def per_device(slab, sketch):
    total_rows = slab.shape[0] * lax.axis_size("row") * lax.axis_size("col")
    turns = (0, 1, 2)
    sampled, left, high, low, *sent = sample(slab, sketch)
    kept = keep(left, high, low, sent[2])
    after = None
    kept, handed, states, near, far = list(kept), [None] * 3, [None] * 3, [None] * 3, [None] * 3
    for chain in turns:
        got = send(sent[chain], CORE_PAIRS)
        kept[chain], handed[chain] = sum_cores(kept[chain], got, after)
        after = kept[chain]
    for chain in turns:
        got = send(handed[chain], ring_pairs(chain, 0))
        kept[chain], handed[chain] = sum_half(kept[chain], handed[chain], got, after)
        after = kept[chain]
    for chain in turns:
        got = send(handed[chain], ring_pairs(chain, 1))
        states[chain] = after = sum_half(kept[chain], handed[chain], got, after)
    for turn, step in ((1, 0), (1, 1), (2, 0)):
        for chain in turns:
            got = send(states[chain], ring_pairs((chain + turn) % 3, step))
            states[chain] = after = sum_whole(states[chain], got, after)
    gram = None
    for chain in turns:
        got = send(states[chain], ring_pairs((chain + 2) % 3, 1))
        states[chain], *rest = sum_last(states[chain], got, after)
        after = states[chain]
        gram = rest[0] if rest else gram
    for chain in turns:
        near[chain] = after = join(states[chain], send(states[chain], ring_pairs(chain, 1)), after)
    inverse = factor(pass_on(gram, after))
    for chain in turns:
        far[chain] = pass_on(send(near[chain], ring_pairs(chain, 0)), inverse)
    near_other = [send(pass_on(part, later), CORE_PAIRS) for part, later in zip(near, far)]
    far_other = [send(part, CORE_PAIRS) for part in far]
    out = apply(inverse, near + far, [(a, 0, first) for first in (0, 2) for a in range(3)], None, "apply_own")
    out = apply(inverse, near_other, [(a, 1, 0) for a in range(3)], out, "apply_near")
    out = apply(inverse, far_other, [(a, 1, 2) for a in range(3)], out, "apply_far")
    return basis(inverse, sampled, math.sqrt(total_rows)), out


def solution(mesh):
    return jax.shard_map(
        per_device,
        mesh=mesh,
        in_specs=(P(AXES, None), P()),
        out_specs=(P(AXES, None), P()),
        check_vma=False,
    )
```

time: 364 us -> 84.6 us (0.23); the launches traced: 358 us -> 84.5 us
  waiting for transfers between devices: 171 us -> 18.4 us
  other arithmetic: 114 us -> 0 us
  matrix products: 34.7 us -> 0 us
  Pallas kernels: 0 us -> 24.9 us
  starting transfers between devices: 16.6 us -> 40.2 us
  between operations: 14.7 us -> 1.05 us
  local copies, waits for them, and re-layouts: 6.18 us -> 0 us
    psum x1 -> x0, waiting for transfers between devices: 162 us -> none  [per_device(): lax.psum(jnp.dot(transposed, slab, precision=highest), ('row', 'col'))]
    another operation x26 -> x0, other arithmetic: 110 us -> none  [the longest x21 86.7 us: merge_level(): return jnp.linalg.cholesky(combined)]
    dot_general x17 -> x0, matrix products: 34.2 us -> none  [the longest x1 16.2 us: per_device(): jnp.dot(slab, sketch, precision=highest, preferred_element_type=jnp.float32)]
    pallas_call x0 -> x38, Pallas kernels: none -> 24.9 us  [the longest x1 13.1 us: sample(): pl.pallas_call(sample_kernel, in_specs=[HBM, HBM], out_specs=[VMEM] * 7,...]
    ppermute x7 -> x33, starting transfers between devices: 16.5 us -> 40.2 us  [send(): return lax.ppermute(value, AXES, pairs)]
    ppermute x7 -> x33, waiting for transfers between devices: 9.55 us -> 18.4 us  [send(): return lax.ppermute(value, AXES, pairs)]
    unnamed x2 -> x0, local copies, waits for them, and re-layouts: 5.44 us -> none
    select_n x7 -> x0, other arithmetic: 4.59 us -> none  [the longest x6 3.94 us: merge_level(): return jnp.linalg.cholesky(combined)]
  transfers between devices with their start and end apart: 8 -> 33, of which waited for: 8 -> 15; matrix products, arithmetic and copies ran while one was open for 1% -> 0% of each run, Pallas kernels for 0% -> 10%
where the time goes in v2:
time: 84.6 us; the launch traced here: 84.5 us
  starting transfers between devices  40.2 us (48%)
  Pallas kernels  24.9 us (29%)
  waiting for transfers between devices  18.4 us (22%)
  between operations  1.05 us (1%)
    ppermute x33, starting transfers between devices, send(): return lax.ppermute(value, AXES, pairs)  40.2 us
    ppermute x33, waiting for transfers between devices, send(): return lax.ppermute(value, AXES, pairs)  18.4 us
    pallas_call x1, Pallas kernels, sample(): pl.pallas_call(sample_kernel, in_specs=[HBM, HBM], out_specs=[VMEM] * 7,...  13.1 us
    pallas_call x3, Pallas kernels, apply(): pl.pallas_call(lambda *refs: apply_kernel(pieces, *refs), in_specs=[VMEM]...  4.11 us
    pallas_call x1, Pallas kernels, factor(): pl.pallas_call(factor_kernel, in_specs=[VMEM], out_specs=VMEM, out_shape=...  4.01 us
    pallas_call x1, Pallas kernels, keep(): pl.pallas_call(keep_kernel, in_specs=[VMEM] * 4, out_specs=[VMEM] * 3, ou...  1.79 us
  transfers between devices with their start and end apart: 33, of which 15 were waited for; matrix products, arithmetic and copies ran while one was open for 0% of the time, Pallas kernels for 10%

profile of v2, /device:TPU:1, one launch (start us, length us, event | category | flops | bytes accessed | tf_op | source)
XLA Modules:
  0.0 84.5 jit_solution(16921577656920972938)
XLA Ops:
  0.6 13.1 %sample.1 = (f32[512,128]{1,0:T(8,128)S(1)}, bf16[256,512]{1,0:T(8,128)(2,1)S(1)}, bf16[512,4096]{1,0:T(8,128)(2,1)S(1)}, bf16[512,4096]{1,0:T(8,128)(2,1)S(1)},...) custom-call(f32[512,8192]{1,0:T(8,128)} %slab.1, f32[8192,128]{1,0:T(8,128)} %sketch.1), custom_call_target="tpu_custom_call" | custom-call | flops 8000000000 | bytes 22020096 | tf_op jit(solution)/shard_map/sample/pallas_call | solution.py:143
  13.8 1.5 %collective-permute-start.2 = (f32[512,384]{1,0:T(8,128)S(1)}, f32[512,384]{1,0:T(8,128)S(1)}, u32[]{:S(2)}, u32[]{:S(2)}) collective-permute-start(f32[512,384]{1,0:T(8,128)S(1)} %get-tuple-element.34), channel_id=1, source_target_pairs={{0,16},{1,17},{2,18},{3,19},{4,20},{5,21},{6,22},{7,23},{8,24},{9,... | collective-permute-start | bytes 2359304 | tf_op jit(solution)/shard_map/ppermute | solution.py:410
  15.8 1.8 %keep.1 = (f32[512,384]{1,0:T(8,128)S(1)}, f32[512,384]{1,0:T(8,128)S(1)}, f32[576,256]{1,0:T(8,128)S(1)}) custom-call(bf16[256,512]{1,0:T(8,128)(2,1)S(1)} %get-tuple-element.26.left, bf16[512,4096]{1,0:T(8,128)(2,1)S(1)} %get-tuple-element.27.high, bf16[512,4096]{1,0:T(8,128)(2,1)S(1)} %get-tuple-element.28.low, f32[576,256]{1,0:T(8,128)S(1)} %get-tuple-element.29.sent), custom_call_target="tpu_custom_call" | custom-call | flops 2000000000 | bytes 1048576 | tf_op jit(solution)/shard_map/keep/pallas_call | solution.py:177
  17.7 2.6 %collective-permute-start.5 = (f32[256,384]{1,0:T(8,128)S(1)}, f32[256,384]{1,0:T(8,128)S(1)}, u32[]{:S(2)}, u32[]{:S(2)}) collective-permute-start(f32[256,384]{1,0:T(8,128)S(1)} %get-tuple-element.40.refs_1_), channel_id=1, source_target_pairs={{0,20},{1,29},{2,22},{3,31},{4,24},{5,17},{6,26},{7,19},{8,28},{9,... | collective-permute-start | bytes 1179656 | tf_op jit(solution)/shard_map/ppermute | solution.py:410
  20.4 3.3 %collective-permute-start.4 = (f32[256,384]{1,0:T(8,128)S(1)}, f32[256,384]{1,0:T(8,128)S(1)}, u32[]{:S(2)}, u32[]{:S(2)}) collective-permute-start(f32[256,384]{1,0:T(8,128)S(1)} %get-tuple-element.39.refs_1_), channel_id=1, source_target_pairs={{0,48},{1,113},{2,50},{3,115},{4,116},{5,53},{6,118},{7,55},{8,56}... | collective-permute-start | bytes 1179656 | tf_op jit(solution)/shard_map/ppermute | solution.py:410
  23.8 3.8 %collective-permute-start.3 = (f32[320,256]{1,0:T(8,128)S(1)}, f32[320,256]{1,0:T(8,128)S(1)}, u32[]{:S(2)}, u32[]{:S(2)}) collective-permute-start(f32[320,256]{1,0:T(8,128)S(1)} %get-tuple-element.38.refs_1_), channel_id=1, source_target_pairs={{0,17},{1,18},{2,19},{3,16},{4,23},{5,20},{6,21},{7,22},{8,25},{9,... | collective-permute-start | bytes 983048 | tf_op jit(solution)/shard_map/ppermute | solution.py:410
  28.0 1.5 %collective-permute-done.4.refs_2_ = f32[256,384]{1,0:T(8,128)S(1)} collective-permute-done((f32[256,384]{1,0:T(8,128)S(1)}, f32[256,384]{1,0:T(8,128)S(1)}, u32[]{:S(2)}, u32[]{:S(2)}) %collective-permute-start.4) | collective-permute-done | bytes 393248 | tf_op jit(solution)/shard_map/ppermute | solution.py:410
  29.6 3.0 %collective-permute-done.3.refs_2_ = f32[320,256]{1,0:T(8,128)S(1)} collective-permute-done((f32[320,256]{1,0:T(8,128)S(1)}, f32[320,256]{1,0:T(8,128)S(1)}, u32[]{:S(2)}, u32[]{:S(2)}) %collective-permute-start.3) | collective-permute-done | bytes 327712 | tf_op jit(solution)/shard_map/ppermute | solution.py:410
  33.1 1.3 %collective-permute-start.11 = (f32[128,384]{1,0:T(8,128)S(1)}, f32[128,384]{1,0:T(8,128)S(1)}, u32[]{:S(2)}, u32[]{:S(2)}) collective-permute-start(f32[128,384]{1,0:T(8,128)S(1)} %sum_quarter.3.refs_3_.refs_0_), channel_id=1, source_target_pairs={{0,48},{1,113},{2,50},{3,115},{4,116},{5,53},{6,118},{7,55},{8,56}... | collective-permute-start | bytes 589832 | tf_op jit(solution)/shard_map/ppermute | solution.py:410
  34.7 3.8 %collective-permute-start.10 = (f32[128,384]{1,0:T(8,128)S(1)}, f32[128,384]{1,0:T(8,128)S(1)}, u32[]{:S(2)}, u32[]{:S(2)}) collective-permute-start(f32[128,384]{1,0:T(8,128)S(1)} %sum_quarter.4.refs_3_.refs_0_), channel_id=1, source_target_pairs={{0,17},{1,18},{2,19},{3,16},{4,23},{5,20},{6,21},{7,22},{8,25},{9,... | collective-permute-start | bytes 589832 | tf_op jit(solution)/shard_map/ppermute | solution.py:410
  38.5 2.5 %collective-permute-start.9 = (f32[192,256]{1,0:T(8,128)S(1)}, f32[192,256]{1,0:T(8,128)S(1)}, u32[]{:S(2)}, u32[]{:S(2)}) collective-permute-start(f32[192,256]{1,0:T(8,128)S(1)} %sum_quarter.5.refs_2_.refs_0_), channel_id=1, source_target_pairs={{0,20},{1,29},{2,22},{3,31},{4,24},{5,17},{6,26},{7,19},{8,28},{9,... | collective-permute-start | bytes 589832 | tf_op jit(solution)/shard_map/ppermute | solution.py:410
  42.5 2.6 %collective-permute-done.9.refs_1_ = f32[192,256]{1,0:T(8,128)S(1)} collective-permute-done((f32[192,256]{1,0:T(8,128)S(1)}, f32[192,256]{1,0:T(8,128)S(1)}, u32[]{:S(2)}, u32[]{:S(2)}) %collective-permute-start.9) | collective-permute-done | bytes 196640 | tf_op jit(solution)/shard_map/ppermute | solution.py:410
  45.3 1.2 %collective-permute-done.14.refs_1_ = f32[128,384]{1,0:T(8,128)S(1)} collective-permute-done((f32[128,384]{1,0:T(8,128)S(1)}, f32[128,384]{1,0:T(8,128)S(1)}, u32[]{:S(2)}, u32[]{:S(2)}) %collective-permute-start.14) | collective-permute-done | bytes 196640 | tf_op jit(solution)/shard_map/ppermute | solution.py:410
  47.3 2.8 %collective-permute-start.16 = (f32[128,384]{1,0:T(8,128)S(1)}, f32[128,384]{1,0:T(8,128)S(1)}, u32[]{:S(2)}, u32[]{:S(2)}) collective-permute-start(f32[128,384]{1,0:T(8,128)S(1)} %sum_whole.13.refs_2_.refs_0_), channel_id=1, source_target_pairs={{0,20},{1,29},{2,22},{3,31},{4,24},{5,17},{6,26},{7,19},{8,28},{9,... | collective-permute-start | bytes 589832 | tf_op jit(solution)/shard_map/ppermute | solution.py:410
  50.9 3.2 %collective-permute-start.15 = (f32[192,256]{1,0:T(8,128)S(1)}, f32[192,256]{1,0:T(8,128)S(1)}, u32[]{:S(2)}, u32[]{:S(2)}) collective-permute-start(f32[192,256]{1,0:T(8,128)S(1)} %sum_whole.14.refs_2_.refs_0_), channel_id=1, source_target_pairs={{0,48},{1,113},{2,50},{3,115},{4,116},{5,53},{6,118},{7,55},{8,56}... | collective-permute-start | bytes 589832 | tf_op jit(solution)/shard_map/ppermute | solution.py:410
  55.5 2.3 %collective-permute-done.15.refs_1_ = f32[192,256]{1,0:T(8,128)S(1)} collective-permute-done((f32[192,256]{1,0:T(8,128)S(1)}, f32[192,256]{1,0:T(8,128)S(1)}, u32[]{:S(2)}, u32[]{:S(2)}) %collective-permute-start.15) | collective-permute-done | bytes 196640 | tf_op jit(solution)/shard_map/ppermute | solution.py:410
  60.9 2.3 %collective-permute-done.18.refs_1_ = f32[192,256]{1,0:T(8,128)S(1)} collective-permute-done((f32[192,256]{1,0:T(8,128)S(1)}, f32[192,256]{1,0:T(8,128)S(1)}, u32[]{:S(2)}, u32[]{:S(2)}) %collective-permute-start.18) | collective-permute-done | bytes 196640 | tf_op jit(solution)/shard_map/ppermute | solution.py:410
  63.4 1.7 %collective-permute-done.23.refs_1_ = f32[128,384]{1,0:T(8,128)S(1)} collective-permute-done((f32[128,384]{1,0:T(8,128)S(1)}, f32[128,384]{1,0:T(8,128)S(1)}, u32[]{:S(2)}, u32[]{:S(2)}) %collective-permute-start.23) | collective-permute-done | bytes 196640 | tf_op jit(solution)/shard_map/ppermute | solution.py:410
  66.1 2.0 %collective-permute-start.26 = (f32[256,384]{1,0:T(8,128)S(1)}, f32[256,384]{1,0:T(8,128)S(1)}, u32[]{:S(2)}, u32[]{:S(2)}) collective-permute-start(f32[256,384]{1,0:T(8,128)S(1)} %join.4.refs_2_.refs_0_), channel_id=1, source_target_pairs={{0,48},{1,113},{2,50},{3,115},{4,116},{5,53},{6,118},{7,55},{8,56}... | collective-permute-start | bytes 1179656 | tf_op jit(solution)/shard_map/ppermute | solution.py:410
  68.1 5.1 %collective-permute-start.28 = (f32[256,256]{1,0:T(8,128)S(1)}, f32[256,256]{1,0:T(8,128)S(1)}, u32[]{:S(2)}, u32[]{:S(2)}) collective-permute-start(f32[256,256]{1,0:T(8,128)S(1)} %join.5.refs_1_.refs_0_.refs_3_), channel_id=1, source_target_pairs={{0,17},{1,18},{2,19},{3,16},{4,23},{5,20},{6,21},{7,22},{8,25},{9,... | collective-permute-start | bytes 786440 | tf_op jit(solution)/shard_map/ppermute | solution.py:410
  73.2 4.0 %factor.1.refs_0_.refs_1_ = f32[128,128]{1,0:T(8,128)S(1)} custom-call(f32[64,256]{1,0:T(8,128)S(1)} %pass_on.7.folded), custom_call_target="tpu_custom_call" | custom-call | flops 6000000000 | bytes 1048576 | tf_op jit(solution)/shard_map/factor/pallas_call | solution.py:235
  77.2 1.6 %apply_own.1.refs_4_ = f32[128,8192]{1,0:T(8,128)} custom-call(f32[128,128]{1,0:T(8,128)S(1)} %factor.1.refs_0_.refs_1_, f32[256,384]{1,0:T(8,128)S(1)} %join.3.refs_2_.refs_0_.refs_1_, f32[256,384]{1,0:T(8,128)S(1)} %join.4.refs_2_.refs_0_, f32[256,256]{1,0:T(8,128)S(1)} %join.5.refs_1_.refs_0_.refs_3_, f32[256,384]{1,0:T(8,128)S(1)} %pass_on.8.refs_1_.refs_4_, ...), custom_call_target="tpu_custom_call" | custom-call | flops 1000000000 | bytes 2097152 | tf_op jit(solution)/shard_map/apply_own/pallas_call | solution.py:393
  81.7 1.2 %apply_near.1.refs_4_ = f32[128,8192]{1,0:T(8,128)} custom-call(f32[128,128]{1,0:T(8,128)S(1)} %factor.1.refs_0_.refs_1_, f32[256,384]{1,0:T(8,128)S(1)} %collective-permute-done.30.refs_1_, f32[256,384]{1,0:T(8,128)S(1)} %collective-permute-done.31.refs_2_, f32[256,256]{1,0:T(8,128)S(1)} %collective-permute-done.32.refs_3_, ...), custom_call_target="tpu_custom_call", output_to_operand_aliasing={{}: (4, {})} | custom-call | flops 1000000000 | bytes 2097152 | tf_op jit(solution)/shard_map/apply_near/pallas_call | solution.py:393
  83.1 1.2 %apply_far.1 = f32[128,8192]{1,0:T(8,128)} custom-call(f32[128,128]{1,0:T(8,128)S(1)} %factor.1.refs_0_.refs_1_, f32[256,384]{1,0:T(8,128)S(1)} %collective-permute-done.25.refs_1_, f32[256,384]{1,0:T(8,128)S(1)} %collective-permute-done.27.refs_2_, f32[256,256]{1,0:T(8,128)S(1)} %collective-permute-done.29.refs_3_, ...), custom_call_target="tpu_custom_call", output_to_operand_aliasing={{}: (4, {})} | custom-call | flops 1000000000 | bytes 2097152 | tf_op jit(solution)/shard_map/apply_far/pallas_call | solution.py:393
  (80 shorter events, 13.7 us)
Async XLA Ops:
  15.4 8.3 %collective-permute-start = (f32[576,256]{1,0:T(8,128)S(1)}, f32[576,256]{1,0:T(8,128)S(1)}, u32[]{:S(2)}, u32[]{:S(2)}) collective-permute-start(f32[576,256]{1,0:T(8,128)S(1)} %get-tuple-element.29.sent), channel_id=1, source_target_pairs={{0,16},{1,17},{2,18},{3,19},{4,20},{5,21},{6,22},{7,23},{8,24},{9,... | collective-permute-start | bytes 1769480 | tf_op jit(solution)/shard_map/ppermute | solution.py:410
  17.7 9.9 %collective-permute-start.5 = (f32[256,384]{1,0:T(8,128)S(1)}, f32[256,384]{1,0:T(8,128)S(1)}, u32[]{:S(2)}, u32[]{:S(2)}) collective-permute-start(f32[256,384]{1,0:T(8,128)S(1)} %get-tuple-element.40.refs_1_), channel_id=1, source_target_pairs={{0,20},{1,29},{2,22},{3,31},{4,24},{5,17},{6,26},{7,19},{8,28},{9,... | collective-permute-start | bytes 1179656 | tf_op jit(solution)/shard_map/ppermute | solution.py:410
  20.4 9.1 %collective-permute-start.4 = (f32[256,384]{1,0:T(8,128)S(1)}, f32[256,384]{1,0:T(8,128)S(1)}, u32[]{:S(2)}, u32[]{:S(2)}) collective-permute-start(f32[256,384]{1,0:T(8,128)S(1)} %get-tuple-element.39.refs_1_), channel_id=1, source_target_pairs={{0,48},{1,113},{2,50},{3,115},{4,116},{5,53},{6,118},{7,55},{8,56}... | collective-permute-start | bytes 1179656 | tf_op jit(solution)/shard_map/ppermute | solution.py:410
  23.8 8.9 %collective-permute-start.3 = (f32[320,256]{1,0:T(8,128)S(1)}, f32[320,256]{1,0:T(8,128)S(1)}, u32[]{:S(2)}, u32[]{:S(2)}) collective-permute-start(f32[320,256]{1,0:T(8,128)S(1)} %get-tuple-element.38.refs_1_), channel_id=1, source_target_pairs={{0,17},{1,18},{2,19},{3,16},{4,23},{5,20},{6,21},{7,22},{8,25},{9,... | collective-permute-start | bytes 983048 | tf_op jit(solution)/shard_map/ppermute | solution.py:410
  27.6 5.5 %collective-permute-start.8 = (f32[128,384]{1,0:T(8,128)S(1)}, f32[128,384]{1,0:T(8,128)S(1)}, u32[]{:S(2)}, u32[]{:S(2)}) collective-permute-start(f32[128,384]{1,0:T(8,128)S(1)} %get-tuple-element.46.refs_1_), channel_id=1, source_target_pairs={{0,28},{1,21},{2,30},{3,23},{4,16},{5,25},{6,18},{7,27},{8,20},{9,... | collective-permute-start | bytes 589832 | tf_op jit(solution)/shard_map/ppermute | solution.py:410
  29.5 5.2 %collective-permute-start.7 = (f32[128,384]{1,0:T(8,128)S(1)}, f32[128,384]{1,0:T(8,128)S(1)}, u32[]{:S(2)}, u32[]{:S(2)}) collective-permute-start(f32[128,384]{1,0:T(8,128)S(1)} %get-tuple-element.45.refs_1_), channel_id=1, source_target_pairs={{0,112},{1,49},{2,114},{3,51},{4,52},{5,117},{6,54},{7,119},{8,120... | collective-permute-start | bytes 589832 | tf_op jit(solution)/shard_map/ppermute | solution.py:410
  32.7 5.8 %collective-permute-start.6 = (f32[192,256]{1,0:T(8,128)S(1)}, f32[192,256]{1,0:T(8,128)S(1)}, u32[]{:S(2)}, u32[]{:S(2)}) collective-permute-start(f32[192,256]{1,0:T(8,128)S(1)} %get-tuple-element.44.refs_1_), channel_id=1, source_target_pairs={{0,19},{1,16},{2,17},{3,18},{4,21},{5,22},{6,23},{7,20},{8,27},{9,... | collective-permute-start | bytes 589832 | tf_op jit(solution)/shard_map/ppermute | solution.py:410
  33.1 7.9 %collective-permute-start.11 = (f32[128,384]{1,0:T(8,128)S(1)}, f32[128,384]{1,0:T(8,128)S(1)}, u32[]{:S(2)}, u32[]{:S(2)}) collective-permute-start(f32[128,384]{1,0:T(8,128)S(1)} %sum_quarter.3.refs_3_.refs_0_), channel_id=1, source_target_pairs={{0,48},{1,113},{2,50},{3,115},{4,116},{5,53},{6,118},{7,55},{8,56}... | collective-permute-start | bytes 589832 | tf_op jit(solution)/shard_map/ppermute | solution.py:410
  34.7 7.1 %collective-permute-start.10 = (f32[128,384]{1,0:T(8,128)S(1)}, f32[128,384]{1,0:T(8,128)S(1)}, u32[]{:S(2)}, u32[]{:S(2)}) collective-permute-start(f32[128,384]{1,0:T(8,128)S(1)} %sum_quarter.4.refs_3_.refs_0_), channel_id=1, source_target_pairs={{0,17},{1,18},{2,19},{3,16},{4,23},{5,20},{6,21},{7,22},{8,25},{9,... | collective-permute-start | bytes 589832 | tf_op jit(solution)/shard_map/ppermute | solution.py:410
  38.5 6.7 %collective-permute-start.9 = (f32[192,256]{1,0:T(8,128)S(1)}, f32[192,256]{1,0:T(8,128)S(1)}, u32[]{:S(2)}, u32[]{:S(2)}) collective-permute-start(f32[192,256]{1,0:T(8,128)S(1)} %sum_quarter.5.refs_2_.refs_0_), channel_id=1, source_target_pairs={{0,20},{1,29},{2,22},{3,31},{4,24},{5,17},{6,26},{7,19},{8,28},{9,... | collective-permute-start | bytes 589832 | tf_op jit(solution)/shard_map/ppermute | solution.py:410
  41.1 5.5 %collective-permute-start.14 = (f32[128,384]{1,0:T(8,128)S(1)}, f32[128,384]{1,0:T(8,128)S(1)}, u32[]{:S(2)}, u32[]{:S(2)}) collective-permute-start(f32[128,384]{1,0:T(8,128)S(1)} %sum_whole.9.refs_2_.refs_0_), channel_id=1, source_target_pairs={{0,112},{1,49},{2,114},{3,51},{4,52},{5,117},{6,54},{7,119},{8,120... | collective-permute-start | bytes 589832 | tf_op jit(solution)/shard_map/ppermute | solution.py:410
  41.8 5.5 %collective-permute-start.13 = (f32[128,384]{1,0:T(8,128)S(1)}, f32[128,384]{1,0:T(8,128)S(1)}, u32[]{:S(2)}, u32[]{:S(2)}) collective-permute-start(f32[128,384]{1,0:T(8,128)S(1)} %sum_whole.10.refs_2_.refs_0_), channel_id=1, source_target_pairs={{0,19},{1,16},{2,17},{3,18},{4,21},{5,22},{6,23},{7,20},{8,27},{9,... | collective-permute-start | bytes 589832 | tf_op jit(solution)/shard_map/ppermute | solution.py:410
  45.2 5.7 %collective-permute-start.12 = (f32[192,256]{1,0:T(8,128)S(1)}, f32[192,256]{1,0:T(8,128)S(1)}, u32[]{:S(2)}, u32[]{:S(2)}) collective-permute-start(f32[192,256]{1,0:T(8,128)S(1)} %sum_whole.11.refs_2_.refs_0_), channel_id=1, source_target_pairs={{0,28},{1,21},{2,30},{3,23},{4,16},{5,25},{6,18},{7,27},{8,20},{9,... | collective-permute-start | bytes 589832 | tf_op jit(solution)/shard_map/ppermute | solution.py:410
  46.6 7.6 %collective-permute-start.17 = (f32[128,384]{1,0:T(8,128)S(1)}, f32[128,384]{1,0:T(8,128)S(1)}, u32[]{:S(2)}, u32[]{:S(2)}) collective-permute-start(f32[128,384]{1,0:T(8,128)S(1)} %sum_whole.12.refs_2_.refs_0_), channel_id=1, source_target_pairs={{0,17},{1,18},{2,19},{3,16},{4,23},{5,20},{6,21},{7,22},{8,25},{9,... | collective-permute-start | bytes 589832 | tf_op jit(solution)/shard_map/ppermute | solution.py:410
  47.3 6.9 %collective-permute-start.16 = (f32[128,384]{1,0:T(8,128)S(1)}, f32[128,384]{1,0:T(8,128)S(1)}, u32[]{:S(2)}, u32[]{:S(2)}) collective-permute-start(f32[128,384]{1,0:T(8,128)S(1)} %sum_whole.13.refs_2_.refs_0_), channel_id=1, source_target_pairs={{0,20},{1,29},{2,22},{3,31},{4,24},{5,17},{6,26},{7,19},{8,28},{9,... | collective-permute-start | bytes 589832 | tf_op jit(solution)/shard_map/ppermute | solution.py:410
  50.9 6.9 %collective-permute-start.15 = (f32[192,256]{1,0:T(8,128)S(1)}, f32[192,256]{1,0:T(8,128)S(1)}, u32[]{:S(2)}, u32[]{:S(2)}) collective-permute-start(f32[192,256]{1,0:T(8,128)S(1)} %sum_whole.14.refs_2_.refs_0_), channel_id=1, source_target_pairs={{0,48},{1,113},{2,50},{3,115},{4,116},{5,53},{6,118},{7,55},{8,56}... | collective-permute-start | bytes 589832 | tf_op jit(solution)/shard_map/ppermute | solution.py:410
  54.1 5.5 %collective-permute-start.20 = (f32[128,384]{1,0:T(8,128)S(1)}, f32[128,384]{1,0:T(8,128)S(1)}, u32[]{:S(2)}, u32[]{:S(2)}) collective-permute-start(f32[128,384]{1,0:T(8,128)S(1)} %sum_whole.15.refs_2_.refs_0_), channel_id=1, source_target_pairs={{0,19},{1,16},{2,17},{3,18},{4,21},{5,22},{6,23},{7,20},{8,27},{9,... | collective-permute-start | bytes 589832 | tf_op jit(solution)/shard_map/ppermute | solution.py:410
  54.3 6.3 %collective-permute-start.19 = (f32[128,384]{1,0:T(8,128)S(1)}, f32[128,384]{1,0:T(8,128)S(1)}, u32[]{:S(2)}, u32[]{:S(2)}) collective-permute-start(f32[128,384]{1,0:T(8,128)S(1)} %sum_whole.16.refs_2_.refs_0_), channel_id=1, source_target_pairs={{0,28},{1,21},{2,30},{3,23},{4,16},{5,25},{6,18},{7,27},{8,20},{9,... | collective-permute-start | bytes 589832 | tf_op jit(solution)/shard_map/ppermute | solution.py:410
  57.8 5.5 %collective-permute-start.18 = (f32[192,256]{1,0:T(8,128)S(1)}, f32[192,256]{1,0:T(8,128)S(1)}, u32[]{:S(2)}, u32[]{:S(2)}) collective-permute-start(f32[192,256]{1,0:T(8,128)S(1)} %sum_whole.17.refs_2_.refs_0_), channel_id=1, source_target_pairs={{0,112},{1,49},{2,114},{3,51},{4,52},{5,117},{6,54},{7,119},{8,120... | collective-permute-start | bytes 589832 | tf_op jit(solution)/shard_map/ppermute | solution.py:410
  59.6 5.5 %collective-permute-start.23 = (f32[128,384]{1,0:T(8,128)S(1)}, f32[128,384]{1,0:T(8,128)S(1)}, u32[]{:S(2)}, u32[]{:S(2)}) collective-permute-start(f32[128,384]{1,0:T(8,128)S(1)} %sum_last.3.refs_2_.refs_0_), channel_id=1, source_target_pairs={{0,28},{1,21},{2,30},{3,23},{4,16},{5,25},{6,18},{7,27},{8,20},{9,... | collective-permute-start | bytes 589832 | tf_op jit(solution)/shard_map/ppermute | solution.py:410
  60.6 5.5 %collective-permute-start.22 = (f32[128,384]{1,0:T(8,128)S(1)}, f32[128,384]{1,0:T(8,128)S(1)}, u32[]{:S(2)}, u32[]{:S(2)}) collective-permute-start(f32[128,384]{1,0:T(8,128)S(1)} %sum_last.4.refs_2_.refs_0_), channel_id=1, source_target_pairs={{0,112},{1,49},{2,114},{3,51},{4,52},{5,117},{6,54},{7,119},{8,120... | collective-permute-start | bytes 589832 | tf_op jit(solution)/shard_map/ppermute | solution.py:410
  65.1 12.1 %collective-permute-start.24 = (f32[256,384]{1,0:T(8,128)S(1)}, f32[256,384]{1,0:T(8,128)S(1)}, u32[]{:S(2)}, u32[]{:S(2)}) collective-permute-start(f32[256,384]{1,0:T(8,128)S(1)} %join.3.refs_2_.refs_0_.refs_1_), channel_id=1, source_target_pairs={{0,20},{1,29},{2,22},{3,31},{4,24},{5,17},{6,26},{7,19},{8,28},{9,... | collective-permute-start | bytes 1179656 | tf_op jit(solution)/shard_map/ppermute | solution.py:410
  66.1 11.2 %collective-permute-start.26 = (f32[256,384]{1,0:T(8,128)S(1)}, f32[256,384]{1,0:T(8,128)S(1)}, u32[]{:S(2)}, u32[]{:S(2)}) collective-permute-start(f32[256,384]{1,0:T(8,128)S(1)} %join.4.refs_2_.refs_0_), channel_id=1, source_target_pairs={{0,48},{1,113},{2,50},{3,115},{4,116},{5,53},{6,118},{7,55},{8,56}... | collective-permute-start | bytes 1179656 | tf_op jit(solution)/shard_map/ppermute | solution.py:410
  68.1 9.1 %collective-permute-start.28 = (f32[256,256]{1,0:T(8,128)S(1)}, f32[256,256]{1,0:T(8,128)S(1)}, u32[]{:S(2)}, u32[]{:S(2)}) collective-permute-start(f32[256,256]{1,0:T(8,128)S(1)} %join.5.refs_1_.refs_0_.refs_3_), channel_id=1, source_target_pairs={{0,17},{1,18},{2,19},{3,16},{4,23},{5,20},{6,21},{7,22},{8,25},{9,... | collective-permute-start | bytes 786440 | tf_op jit(solution)/shard_map/ppermute | solution.py:410
  (9 other events, 29.5 us)

commit v3 on v2

--- a/solution.py
+++ b/solution.py
@@ -15,6 +15,7 @@
 WIDTH = (384, 384, 256)
 STARTS = (0, 1536, 3072)
 GRAM = 64
+FLIP = (0, 1, 0)
 AHEAD = 8
 QUARTERS = (156, 180)
 SLOTS = (120, 180)
@@ -44,11 +45,11 @@
     return place ^ 1 if (step ^ side) == 0 else place ^ 3
 
 
-def ring_pairs(axis, step):
+def ring_pairs(axis, step, flip=0):
     pairs = []
     for x, y, z, c in places():
         to = [x, y, z]
-        to[axis] = beside(to[axis], step, side_of(x, y, z, c))
+        to[axis] = beside(to[axis], step ^ flip, side_of(x, y, z, c))
         pairs.append((linear(x, y, z, c), linear(*to, 1 - c)))
     return pairs
 
@@ -75,23 +76,30 @@
     return jnp.dot(a, b, preferred_element_type=F32)
 
 
-def products(left, high, low, outs, side):
+def product(chain, side, left, high, low, out):
     place, _ = here()
-    for chain in range(3):
-        width = WIDTH[chain]
-        for pair in range(2):
-            at = pl.ds(STARTS[chain] + 2 * pair * width, 2 * width)
-            both = mul(left[...], high[:, at])
-            value = both[:K] + (both[K:] + mul(left[:K], low[:, at]))
-            for part in range(2):
-                slot = two_bits(SLOTS, side, (2 * pair + part) ^ place[chain])
-                rows = pl.ds(pl.multiple_of(slot * K, K), K)
-                outs[chain][rows] = value[:, part * width : (part + 1) * width]
+    width = WIDTH[chain]
+    for i in range(4):
+        first = max(STARTS[chain], i * CHUNK)
+        last = min(STARTS[chain] + 4 * width, (i + 1) * CHUNK)
+        if first >= last:
+            continue
+        at = slice(first - i * CHUNK, last - i * CHUNK)
+        both = mul(left[...], high[i, :, at])
+        value = both[:K] + (both[K:] + mul(left[:K], low[i, :, at]))
+        begin = first
+        while begin < last:
+            quarter, within = divmod(begin - STARTS[chain], width)
+            size = min(width - within, last - begin)
+            slot = two_bits(SLOTS, side ^ FLIP[chain], quarter ^ place[chain])
+            rows = pl.ds(pl.multiple_of(slot * K, K), K)
+            out[rows, within : within + size] = value[:, begin - first : begin - first + size]
+            begin += size
 
 
 def sample_kernel(
-    slab, sketch, sampled, left, high, low, xs, ys, zs,
-    slab_here, sketch_here, sent_high, sent_low, slab_done, sketch_done,
+    slab, sketch, sampled, left, sent_high, sent_low, high, low, xs,
+    slab_here, sketch_here, slab_done, sketch_done,
 ):
     _, side = here()
     depth = slab_here.shape[0]
@@ -114,15 +122,12 @@
             slab_copy(k).start()
     for k in range(8):
         slab_copy(k).wait()
+        sketch_copy(k).wait()
         slab_high, slab_low = halves(slab_here[k % depth])
-        at = pl.ds((k % 4) * CHUNK, CHUNK)
         if k < 4:
-            sent_high[:, at], sent_low[:, at] = slab_high, slab_low
+            sent_high[k], sent_low[k] = slab_high, slab_low
         else:
-            high[:, at], low[:, at] = slab_high, slab_low
-        if k + depth < 8:
-            slab_copy(k + depth).start()
-        sketch_copy(k).wait()
+            high[k - 4], low[k - 4] = slab_high, slab_low
         sketch_high, sketch_low = halves(sketch_here[k])
         both = mul(slab_high, jnp.concatenate([sketch_high, sketch_low], axis=1))
         value = both[:, :K] + (both[:, K:] + mul(slab_low, sketch_high))
@@ -130,11 +135,10 @@
             sampled[...] = value
         else:
             sampled[...] += value
+        if k + depth < 8:
+            slab_copy(k + depth).start()
     left[...] = jnp.concatenate(halves(sampled[...].T), axis=0)
-    square = lax.dot_general(left[...], left[...], (((1,), (1,)), ((), ())), preferred_element_type=F32)
-    gram = (square[:K, :K] + square[K:, K:]) + (square[:K, K:] + square[K:, :K])
-    zs[4 * K :] = jnp.concatenate([gram[:GRAM], gram[GRAM:]], axis=1)
-    products(left, sent_high, sent_low, (xs, ys, zs), 1 - side)
+    product(0, 1 - side, left, sent_high, sent_low, xs)
 
 
 def sample(slab, sketch):
@@ -147,46 +151,65 @@
         out_shape=[
             jax.ShapeDtypeStruct((rows, K), F32),
             jax.ShapeDtypeStruct((2 * K, rows), BF16),
-            jax.ShapeDtypeStruct((rows, HALF), BF16),
-            jax.ShapeDtypeStruct((rows, HALF), BF16),
+            *[jax.ShapeDtypeStruct((4, rows, CHUNK), BF16)] * 4,
             jax.ShapeDtypeStruct((4 * K, WIDTH[0]), F32),
-            jax.ShapeDtypeStruct((4 * K, WIDTH[1]), F32),
-            jax.ShapeDtypeStruct((4 * K + GRAM, WIDTH[2]), F32),
         ],
         scratch_shapes=[
             pltpu.VMEM((depth, rows, CHUNK), F32),
             pltpu.VMEM((8, CHUNK, K), F32),
-            pltpu.VMEM((rows, HALF), BF16),
-            pltpu.VMEM((rows, HALF), BF16),
             pltpu.SemaphoreType.DMA((depth,)),
             pltpu.SemaphoreType.DMA((8,)),
         ],
-        compiler_params=pltpu.CompilerParams(vmem_limit_bytes=40 * MIB),
+        compiler_params=pltpu.CompilerParams(vmem_limit_bytes=34 * MIB),
         cost_estimate=pl.CostEstimate(flops=8 * 10**9, bytes_accessed=21 * MIB, transcendentals=0),
         name="sample",
     )(slab, sketch)
 
 
-def keep_kernel(left, high, low, sent, x, y, z):
+def rest_kernel(left, high, low, after, y, z):
     _, side = here()
-    z[4 * K :] = sent[4 * K :]
-    products(left, high, low, (x, y, z), side)
-
-
-def keep(left, high, low, sent):
-    return pl.pallas_call(
-        keep_kernel,
-        in_specs=[VMEM] * 4,
-        out_specs=[VMEM] * 3,
+    product(1, 1 - side, left, high, low, y)
+    square = lax.dot_general(left[...], left[...], (((1,), (1,)), ((), ())), preferred_element_type=F32)
+    gram = (square[:K, :K] + square[K:, K:]) + (square[:K, K:] + square[K:, :K])
+    z[4 * K :] = jnp.concatenate([gram[:GRAM], gram[GRAM:]], axis=1)
+    product(2, 1 - side, left, high, low, z)
+
+
+def rest_to_send(left, high, low, after):
+    return pl.pallas_call(
+        rest_kernel,
+        in_specs=[VMEM] * 3 + [pl.BlockSpec(memory_space=pl.ANY)],
+        out_specs=[VMEM] * 2,
         out_shape=[
-            jax.ShapeDtypeStruct((4 * K, WIDTH[0]), F32),
             jax.ShapeDtypeStruct((4 * K, WIDTH[1]), F32),
             jax.ShapeDtypeStruct((4 * K + GRAM, WIDTH[2]), F32),
         ],
         compiler_params=pltpu.CompilerParams(vmem_limit_bytes=20 * MIB),
-        cost_estimate=pl.CostEstimate(flops=2 * 10**9, bytes_accessed=MIB, transcendentals=0),
+        cost_estimate=pl.CostEstimate(flops=15 * 10**8, bytes_accessed=MIB, transcendentals=0),
+        name="rest_to_send",
+    )(left, high, low, after)
+
+
+def keep_kernel(chain, left, high, low, *rest):
+    _, side = here()
+    out = rest[-1]
+    if len(rest) > 2:
+        out[4 * K :] = rest[0][4 * K :]
+    product(chain, side, left, high, low, out)
+
+
+def keep(chain, left, high, low, sent, after):
+    rows, width = sent.shape
+    args = [left, high, low] + ([sent] if rows > 4 * K else []) + [after]
+    return pl.pallas_call(
+        lambda *refs: keep_kernel(chain, *refs),
+        in_specs=[VMEM] * (len(args) - 1) + [pl.BlockSpec(memory_space=pl.ANY)],
+        out_specs=VMEM,
+        out_shape=jax.ShapeDtypeStruct((rows, width), F32),
+        compiler_params=pltpu.CompilerParams(vmem_limit_bytes=20 * MIB),
+        cost_estimate=pl.CostEstimate(flops=7 * 10**8, bytes_accessed=MIB, transcendentals=0),
         name="keep",
-    )(left, high, low, sent)
+    )(*args)
 
 
 def factor_kernel(folded, inverse):
@@ -243,22 +266,6 @@
     )(folded)
 
 
-def basis_kernel(scale, inverse, sampled, out):
-    out[...] = scale * jnp.dot(sampled[...], inverse[...].T, precision=HIGHEST, preferred_element_type=F32)
-
-
-def basis(inverse, sampled, scale):
-    return pl.pallas_call(
-        lambda *refs: basis_kernel(scale, *refs),
-        in_specs=[VMEM, VMEM],
-        out_specs=VMEM,
-        out_shape=jax.ShapeDtypeStruct(sampled.shape, F32),
-        cost_estimate=pl.CostEstimate(flops=10**9, bytes_accessed=MIB, transcendentals=0),
-        compiler_params=pltpu.CompilerParams(vmem_limit_bytes=8 * MIB),
-        name="basis",
-    )(inverse, sampled)
-
-
 def call_in_turn(body, args, shapes, after, name):
     extra = [] if after is None else [after]
     any_space = pl.BlockSpec(memory_space=pl.ANY)
@@ -360,8 +367,7 @@
     )(value, after)
 
 
-def apply_kernel(pieces, inverse, *rest):
-    arrays, (out, *ready, done) = rest[: len(pieces)], rest[-5:]
+def put_products(pieces, arrays, inverse, out, ready, done):
     place, side = here()
     high, low = halves(inverse[...])
     wide = jnp.concatenate([high, high], axis=1)
@@ -376,34 +382,74 @@
             filled[chain] += 1
             stacked = jnp.concatenate([value_high, value_low], axis=0)
             ready[chain][at] = mul(wide, stacked) + mul(low, value_high)
-            quarter = place[chain] ^ two_bits(QUARTERS, owner, first + i)
+            quarter = place[chain] ^ two_bits(QUARTERS, owner ^ FLIP[chain], first + i)
             column = pl.multiple_of(owner * HALF + STARTS[chain] + quarter * width, K)
             copies.append(
                 pltpu.make_async_copy(ready[chain].at[at], out.at[:, pl.ds(column, width)], done.at[len(copies)])
             )
             copies[-1].start()
+    return copies
+
+
+def apply_first_kernel(pieces, scale, inverse, sampled, *rest):
+    arrays, (out, basis, mark, *ready, basis_ready, done, basis_done) = rest[: len(pieces)], rest[len(pieces) :]
+    mark[...] = jnp.zeros_like(mark)
+    copies = put_products(pieces, arrays, inverse, out, ready, done)
+    across_high, across_low = halves(inverse[...].T)
+    high, low = halves(sampled[...])
+    wide = jnp.concatenate([across_high, across_high], axis=0)
+    basis_ready[...] = scale * (mul(jnp.concatenate([high, low], axis=1), wide) + mul(high, across_low))
+    copies.append(pltpu.make_async_copy(basis_ready, basis, basis_done))
+    copies[-1].start()
     for copy in copies:
         copy.wait()
 
 
-def apply(inverse, parts, pieces, before, name):
-    aliases = {} if before is None else {1 + len(parts): 0}
-    args = [inverse, *parts] + ([] if before is None else [before])
+def apply_next_kernel(pieces, inverse, *rest):
+    arrays, (_, out, *ready, done) = rest[: len(pieces)], rest[len(pieces) :]
+    for copy in put_products(pieces, arrays, inverse, out, ready, done):
+        copy.wait()
+
+
+def apply_scratch(pieces):
     most = [2 * sum(piece[0] == chain for piece in pieces) for chain in range(3)]
-    return pl.pallas_call(
-        lambda *refs: apply_kernel(pieces, *refs),
-        in_specs=[VMEM] * (1 + len(parts)) + [HBM] * len(aliases),
+    return [pltpu.VMEM((most[chain], K, WIDTH[chain]), F32) for chain in range(3)]
+
+
+def apply_first(inverse, parts, pieces, sampled, scale):
+    return pl.pallas_call(
+        lambda *refs: apply_first_kernel(pieces, scale, *refs),
+        in_specs=[VMEM] * (2 + len(parts)),
+        out_specs=[HBM, HBM, VMEM],
+        out_shape=[
+            jax.ShapeDtypeStruct((K, 2 * HALF), F32),
+            jax.ShapeDtypeStruct(sampled.shape, F32),
+            jax.ShapeDtypeStruct((8, K), F32),
+        ],
+        scratch_shapes=[
+            *apply_scratch(pieces),
+            pltpu.VMEM(sampled.shape, F32),
+            pltpu.SemaphoreType.DMA((2 * len(pieces),)),
+            pltpu.SemaphoreType.DMA,
+        ],
+        compiler_params=pltpu.CompilerParams(vmem_limit_bytes=12 * MIB),
+        cost_estimate=pl.CostEstimate(flops=10**9, bytes_accessed=2 * MIB, transcendentals=0),
+        name="apply_first",
+    )(inverse, sampled, *parts)
+
+
+def apply_next(inverse, parts, pieces, before):
+    return pl.pallas_call(
+        lambda *refs: apply_next_kernel(pieces, *refs),
+        in_specs=[VMEM] * (1 + len(parts)) + [HBM],
         out_specs=HBM,
         out_shape=jax.ShapeDtypeStruct((K, 2 * HALF), F32),
-        scratch_shapes=[
-            *[pltpu.VMEM((max(most[chain], 1), K, WIDTH[chain]), F32) for chain in range(3)],
-            pltpu.SemaphoreType.DMA((2 * len(pieces),)),
-        ],
-        input_output_aliases=aliases,
+        scratch_shapes=[*apply_scratch(pieces), pltpu.SemaphoreType.DMA((2 * len(pieces),))],
+        input_output_aliases={1 + len(parts): 0},
         compiler_params=pltpu.CompilerParams(vmem_limit_bytes=12 * MIB),
         cost_estimate=pl.CostEstimate(flops=10**9, bytes_accessed=2 * MIB, transcendentals=0),
-        name=name,
-    )(*args)
+        name="apply_next",
+    )(inverse, *parts, before)
 
 
 def send(value, pairs):
@@ -413,42 +459,45 @@
 def per_device(slab, sketch):
     total_rows = slab.shape[0] * lax.axis_size("row") * lax.axis_size("col")
     turns = (0, 1, 2)
-    sampled, left, high, low, *sent = sample(slab, sketch)
-    kept = keep(left, high, low, sent[2])
-    after = None
-    kept, handed, states, near, far = list(kept), [None] * 3, [None] * 3, [None] * 3, [None] * 3
+    sampled, left, sent_high, sent_low, high, low, first = sample(slab, sketch)
+    sent = [first, *rest_to_send(left, sent_high, sent_low, first)]
+    after = sent[2]
+    kept, handed, states, near, far = [None] * 3, [None] * 3, [None] * 3, [None] * 3, [None] * 3
     for chain in turns:
         got = send(sent[chain], CORE_PAIRS)
-        kept[chain], handed[chain] = sum_cores(kept[chain], got, after)
+        own = keep(chain, left, high, low, sent[chain], after)
+        kept[chain], handed[chain] = sum_cores(own, got, None)
         after = kept[chain]
     for chain in turns:
-        got = send(handed[chain], ring_pairs(chain, 0))
+        got = send(handed[chain], ring_pairs(chain, 0, FLIP[chain]))
         kept[chain], handed[chain] = sum_half(kept[chain], handed[chain], got, after)
         after = kept[chain]
     for chain in turns:
-        got = send(handed[chain], ring_pairs(chain, 1))
+        got = send(handed[chain], ring_pairs(chain, 1, FLIP[chain]))
         states[chain] = after = sum_half(kept[chain], handed[chain], got, after)
     for turn, step in ((1, 0), (1, 1), (2, 0)):
         for chain in turns:
-            got = send(states[chain], ring_pairs((chain + turn) % 3, step))
+            got = send(states[chain], ring_pairs((chain + turn) % 3, step, FLIP[chain]))
             states[chain] = after = sum_whole(states[chain], got, after)
     gram = None
     for chain in turns:
-        got = send(states[chain], ring_pairs((chain + 2) % 3, 1))
+        got = send(states[chain], ring_pairs((chain + 2) % 3, 1, FLIP[chain]))
         states[chain], *rest = sum_last(states[chain], got, after)
         after = states[chain]
         gram = rest[0] if rest else gram
     for chain in turns:
-        near[chain] = after = join(states[chain], send(states[chain], ring_pairs(chain, 1)), after)
+        near[chain] = after = join(states[chain], send(states[chain], ring_pairs(chain, 1, FLIP[chain])), after)
     inverse = factor(pass_on(gram, after))
+    scale = math.sqrt(total_rows)
+    out, basis, mark = apply_first(inverse, near, [(a, 0, 0) for a in range(3)], sampled, scale)
     for chain in turns:
-        far[chain] = pass_on(send(near[chain], ring_pairs(chain, 0)), inverse)
+        far[chain] = pass_on(send(near[chain], ring_pairs(chain, 0, FLIP[chain])), mark)
     near_other = [send(pass_on(part, later), CORE_PAIRS) for part, later in zip(near, far)]
     far_other = [send(part, CORE_PAIRS) for part in far]
-    out = apply(inverse, near + far, [(a, 0, first) for first in (0, 2) for a in range(3)], None, "apply_own")
-    out = apply(inverse, near_other, [(a, 1, 0) for a in range(3)], out, "apply_near")
-    out = apply(inverse, far_other, [(a, 1, 2) for a in range(3)], out, "apply_far")
-    return basis(inverse, sampled, math.sqrt(total_rows)), out
+    middle = [(a, 0, 2) for a in range(3)] + [(a, 1, 0) for a in range(3)]
+    out = apply_next(inverse, far + near_other, middle, out)
+    out = apply_next(inverse, far_other, [(a, 1, 2) for a in range(3)], out)
+    return basis, out
 
 
 def solution(mesh):

time: 84.6 us -> 78.1 us (0.923)
  waiting for transfers between devices: 18.4 us -> 13.4 us
  Pallas kernels: 24.9 us -> 21.6 us
  starting transfers between devices: 40.2 us -> 41.8 us
    ppermute x33, waiting for transfers between devices: 18.4 us -> 13.4 us  [send(): return lax.ppermute(value, AXES, pairs)]
    pallas_call x1, Pallas kernels: 13.1 us -> 9.2 us  [sample(): pl.pallas_call(sample_kernel, in_specs=[HBM, HBM], out_specs=[VMEM] * 7,...]
    ppermute x33, starting transfers between devices: 40.2 us -> 41.8 us  [send(): return lax.ppermute(value, AXES, pairs)]
    pallas_call x5 -> x7, Pallas kernels: 6.98 us -> 7.68 us  [the longest x2 2.87 us: apply_next(): pl.pallas_call(lambda *refs: apply_next_kernel(pieces, *refs), in_specs=[...]
  transfers between devices with their start and end apart: 33 -> 33, of which waited for: 15 -> 19; matrix products, arithmetic and copies ran while one was open for 0% -> 0% of each run, Pallas kernels for 10% -> 14%
where the time goes in v3:
time: 78.1 us; the launch traced here: 78 us
  starting transfers between devices  41.8 us (54%)
  Pallas kernels  21.6 us (28%)
  waiting for transfers between devices  13.4 us (17%)
  between operations  1.13 us (1%)
    ppermute x33, starting transfers between devices, send(): return lax.ppermute(value, AXES, pairs)  41.8 us
    ppermute x33, waiting for transfers between devices, send(): return lax.ppermute(value, AXES, pairs)  13.4 us
    pallas_call x1, Pallas kernels, sample(): pl.pallas_call(sample_kernel, in_specs=[HBM, HBM], out_specs=[VMEM] * 7,...  9.2 us
    pallas_call x1, Pallas kernels, factor(): pl.pallas_call(factor_kernel, in_specs=[VMEM], out_specs=VMEM, out_shape=...  4.01 us
    pallas_call x2, Pallas kernels, apply_next(): pl.pallas_call(lambda *refs: apply_next_kernel(pieces, *refs), in_specs=[...  2.87 us
    pallas_call x3, Pallas kernels, keep(): pl.pallas_call(lambda *refs: keep_kernel(chain, *refs), in_specs=[VMEM] *...  2.11 us
  transfers between devices with their start and end apart: 33, of which 19 were waited for; matrix products, arithmetic and copies ran while one was open for 0% of the time, Pallas kernels for 14%

profile of v3, /device:TPU:1, one launch (start us, length us, event | category | flops | bytes accessed | tf_op | source)
XLA Modules:
  0.0 78.0 jit_solution(8214737133693647909)
XLA Ops:
  0.6 9.2 %sample.1 = (f32[512,128]{1,0:T(8,128)S(1)}, bf16[256,512]{1,0:T(8,128)(2,1)S(1)}, bf16[4,512,1024]{2,1,0:T(8,128)(2,1)S(1)}, bf16[4,512,1024]{2,1,0:T(8,128)(2,...) custom-call(f32[512,8192]{1,0:T(8,128)} %slab.1, ...), custom_call_target="tpu_custom_call" | custom-call | flops 8000000000 | bytes 22020096 | tf_op jit(solution)/shard_map/sample/pallas_call | solution.py:147
  9.8 1.5 %collective-permute-start = (f32[512,384]{1,0:T(8,128)S(1)}, f32[512,384]{1,0:T(8,128)S(1)}, u32[]{:S(2)}, u32[]{:S(2)}) collective-permute-start(f32[512,384]{1,0:T(8,128)S(1)} %get-tuple-element.33.after), channel_id=1, source_target_pairs={{0,16},{1,17},{2,18},{3,19},{4,20},{5,21},{6,22},{7,23},{8,24},{9,... | collective-permute-start | bytes 2359304 | tf_op jit(solution)/shard_map/ppermute | solution.py:456
  11.3 1.3 %rest_to_send.1 = (f32[512,384]{1,0:T(8,128)S(1)}, f32[576,256]{1,0:T(8,128)S(1)}) custom-call(bf16[256,512]{1,0:T(8,128)(2,1)S(1)} %get-tuple-element.28.left.refs_0_, bf16[4,512,1024]{2,1,0:T(8,128)(2,1)S(1)} %get-tuple-element.31.high, bf16[4,512,1024]{2,1,0:T(8,128)(2,1)S(1)} %get-tuple-element.32.low, f32[512,384]{1,0:T(8,128)S(1)} %get-tuple-element.33.after), custom_call_target="tpu_custom_call" | custom-call | flops 1500000000 | bytes 1048576 | tf_op jit(solution)/shard_map/rest_to_send/pallas_call | solution.py:179
  14.1 2.6 %collective-permute-start.5 = (f32[256,384]{1,0:T(8,128)S(1)}, f32[256,384]{1,0:T(8,128)S(1)}, u32[]{:S(2)}, u32[]{:S(2)}) collective-permute-start(f32[256,384]{1,0:T(8,128)S(1)} %get-tuple-element.41.refs_1_), channel_id=1, source_target_pairs={{0,20},{1,29},{2,22},{3,31},{4,24},{5,17},{6,26},{7,19},{8,28},{9,... | collective-permute-start | bytes 1179656 | tf_op jit(solution)/shard_map/ppermute | solution.py:456
  17.6 1.7 %collective-permute-start.4 = (f32[256,384]{1,0:T(8,128)S(1)}, f32[256,384]{1,0:T(8,128)S(1)}, u32[]{:S(2)}, u32[]{:S(2)}) collective-permute-start(f32[256,384]{1,0:T(8,128)S(1)} %get-tuple-element.40.refs_1_), channel_id=1, source_target_pairs={{0,112},{1,49},{2,114},{3,51},{4,52},{5,117},{6,54},{7,119},{8,120... | collective-permute-start | bytes 1179656 | tf_op jit(solution)/shard_map/ppermute | solution.py:456
  19.9 3.8 %collective-permute-start.3 = (f32[320,256]{1,0:T(8,128)S(1)}, f32[320,256]{1,0:T(8,128)S(1)}, u32[]{:S(2)}, u32[]{:S(2)}) collective-permute-start(f32[320,256]{1,0:T(8,128)S(1)} %get-tuple-element.39.refs_1_), channel_id=1, source_target_pairs={{0,17},{1,18},{2,19},{3,16},{4,23},{5,20},{6,21},{7,22},{8,25},{9,... | collective-permute-start | bytes 983048 | tf_op jit(solution)/shard_map/ppermute | solution.py:456
  25.2 2.8 %collective-permute-start.7 = (f32[128,384]{1,0:T(8,128)S(1)}, f32[128,384]{1,0:T(8,128)S(1)}, u32[]{:S(2)}, u32[]{:S(2)}) collective-permute-start(f32[128,384]{1,0:T(8,128)S(1)} %get-tuple-element.46.refs_1_), channel_id=1, source_target_pairs={{0,48},{1,113},{2,50},{3,115},{4,116},{5,53},{6,118},{7,55},{8,56}... | collective-permute-start | bytes 589832 | tf_op jit(solution)/shard_map/ppermute | solution.py:456
  28.6 1.2 %collective-permute-start.6 = (f32[192,256]{1,0:T(8,128)S(1)}, f32[192,256]{1,0:T(8,128)S(1)}, u32[]{:S(2)}, u32[]{:S(2)}) collective-permute-start(f32[192,256]{1,0:T(8,128)S(1)} %get-tuple-element.45.refs_1_), channel_id=1, source_target_pairs={{0,19},{1,16},{2,17},{3,18},{4,21},{5,22},{6,23},{7,20},{8,27},{9,... | collective-permute-start | bytes 589832 | tf_op jit(solution)/shard_map/ppermute | solution.py:456
  29.8 1.7 %collective-permute-start.11 = (f32[128,384]{1,0:T(8,128)S(1)}, f32[128,384]{1,0:T(8,128)S(1)}, u32[]{:S(2)}, u32[]{:S(2)}) collective-permute-start(f32[128,384]{1,0:T(8,128)S(1)} %sum_quarter.3.refs_3_.refs_0_), channel_id=1, source_target_pairs={{0,48},{1,113},{2,50},{3,115},{4,116},{5,53},{6,118},{7,55},{8,56}... | collective-permute-start | bytes 589832 | tf_op jit(solution)/shard_map/ppermute | solution.py:456
  31.6 1.9 %collective-permute-start.10 = (f32[128,384]{1,0:T(8,128)S(1)}, f32[128,384]{1,0:T(8,128)S(1)}, u32[]{:S(2)}, u32[]{:S(2)}) collective-permute-start(f32[128,384]{1,0:T(8,128)S(1)} %sum_quarter.4.refs_3_.refs_0_), channel_id=1, source_target_pairs={{0,19},{1,16},{2,17},{3,18},{4,21},{5,22},{6,23},{7,20},{8,27},{9,... | collective-permute-start | bytes 589832 | tf_op jit(solution)/shard_map/ppermute | solution.py:456
  34.1 1.5 %collective-permute-start.9 = (f32[192,256]{1,0:T(8,128)S(1)}, f32[192,256]{1,0:T(8,128)S(1)}, u32[]{:S(2)}, u32[]{:S(2)}) collective-permute-start(f32[192,256]{1,0:T(8,128)S(1)} %sum_quarter.5.refs_2_.refs_0_), channel_id=1, source_target_pairs={{0,20},{1,29},{2,22},{3,31},{4,24},{5,17},{6,26},{7,19},{8,28},{9,... | collective-permute-start | bytes 589832 | tf_op jit(solution)/shard_map/ppermute | solution.py:456
  37.2 3.6 %collective-permute-start.13 = (f32[128,384]{1,0:T(8,128)S(1)}, f32[128,384]{1,0:T(8,128)S(1)}, u32[]{:S(2)}, u32[]{:S(2)}) collective-permute-start(f32[128,384]{1,0:T(8,128)S(1)} %sum_whole.10.refs_2_.refs_0_), channel_id=1, source_target_pairs={{0,17},{1,18},{2,19},{3,16},{4,23},{5,20},{6,21},{7,22},{8,25},{9,... | collective-permute-start | bytes 589832 | tf_op jit(solution)/shard_map/ppermute | solution.py:456
  42.2 2.0 %collective-permute-start.17 = (f32[128,384]{1,0:T(8,128)S(1)}, f32[128,384]{1,0:T(8,128)S(1)}, u32[]{:S(2)}, u32[]{:S(2)}) collective-permute-start(f32[128,384]{1,0:T(8,128)S(1)} %sum_whole.12.refs_2_.refs_0_), channel_id=1, source_target_pairs={{0,17},{1,18},{2,19},{3,16},{4,23},{5,20},{6,21},{7,22},{8,25},{9,... | collective-permute-start | bytes 589832 | tf_op jit(solution)/shard_map/ppermute | solution.py:456
  46.4 2.4 %collective-permute-start.15 = (f32[192,256]{1,0:T(8,128)S(1)}, f32[192,256]{1,0:T(8,128)S(1)}, u32[]{:S(2)}, u32[]{:S(2)}) collective-permute-start(f32[192,256]{1,0:T(8,128)S(1)} %sum_whole.14.refs_2_.refs_0_), channel_id=1, source_target_pairs={{0,48},{1,113},{2,50},{3,115},{4,116},{5,53},{6,118},{7,55},{8,56}... | collective-permute-start | bytes 589832 | tf_op jit(solution)/shard_map/ppermute | solution.py:456
  50.0 2.8 %collective-permute-start.19 = (f32[128,384]{1,0:T(8,128)S(1)}, f32[128,384]{1,0:T(8,128)S(1)}, u32[]{:S(2)}, u32[]{:S(2)}) collective-permute-start(f32[128,384]{1,0:T(8,128)S(1)} %sum_whole.16.refs_2_.refs_0_), channel_id=1, source_target_pairs={{0,20},{1,29},{2,22},{3,31},{4,24},{5,17},{6,26},{7,19},{8,28},{9,... | collective-permute-start | bytes 589832 | tf_op jit(solution)/shard_map/ppermute | solution.py:456
  55.0 1.7 %collective-permute-done.19.refs_1_ = f32[128,384]{1,0:T(8,128)S(1)} collective-permute-done((f32[128,384]{1,0:T(8,128)S(1)}, f32[128,384]{1,0:T(8,128)S(1)}, u32[]{:S(2)}, u32[]{:S(2)}) %collective-permute-start.19) | collective-permute-done | bytes 196640 | tf_op jit(solution)/shard_map/ppermute | solution.py:456
  56.7 2.7 %collective-permute-start.22 = (f32[128,384]{1,0:T(8,128)S(1)}, f32[128,384]{1,0:T(8,128)S(1)}, u32[]{:S(2)}, u32[]{:S(2)}) collective-permute-start(f32[128,384]{1,0:T(8,128)S(1)} %sum_last.4.refs_2_.refs_0_), channel_id=1, source_target_pairs={{0,48},{1,113},{2,50},{3,115},{4,116},{5,53},{6,118},{7,55},{8,56}... | collective-permute-start | bytes 589832 | tf_op jit(solution)/shard_map/ppermute | solution.py:456
  59.9 1.8 %collective-permute-start.24 = (f32[256,384]{1,0:T(8,128)S(1)}, f32[256,384]{1,0:T(8,128)S(1)}, u32[]{:S(2)}, u32[]{:S(2)}) collective-permute-start(f32[256,384]{1,0:T(8,128)S(1)} %join.3.refs_2_.refs_0_), channel_id=1, source_target_pairs={{0,20},{1,29},{2,22},{3,31},{4,24},{5,17},{6,26},{7,19},{8,28},{9,... | collective-permute-start | bytes 1179656 | tf_op jit(solution)/shard_map/ppermute | solution.py:456
  61.7 1.7 %collective-permute-done.22.refs_1_ = f32[128,384]{1,0:T(8,128)S(1)} collective-permute-done((f32[128,384]{1,0:T(8,128)S(1)}, f32[128,384]{1,0:T(8,128)S(1)}, u32[]{:S(2)}, u32[]{:S(2)}) %collective-permute-start.22) | collective-permute-done | bytes 196640 | tf_op jit(solution)/shard_map/ppermute | solution.py:456
  64.3 2.4 %collective-permute-start.28 = (f32[256,256]{1,0:T(8,128)S(1)}, f32[256,256]{1,0:T(8,128)S(1)}, u32[]{:S(2)}, u32[]{:S(2)}) collective-permute-start(f32[256,256]{1,0:T(8,128)S(1)} %join.5.refs_1_.refs_4_.refs_0_), channel_id=1, source_target_pairs={{0,17},{1,18},{2,19},{3,16},{4,23},{5,20},{6,21},{7,22},{8,25},{9,... | collective-permute-start | bytes 786440 | tf_op jit(solution)/shard_map/ppermute | solution.py:456
  66.7 4.0 %factor.1.refs_0_ = f32[128,128]{1,0:T(8,128)S(1)} custom-call(f32[64,256]{1,0:T(8,128)S(1)} %pass_on.7.folded), custom_call_target="tpu_custom_call" | custom-call | flops 6000000000 | bytes 1048576 | tf_op jit(solution)/shard_map/factor/pallas_call | solution.py:258
  70.7 1.4 %apply_first.1 = (f32[128,8192]{1,0:T(8,128)}, f32[512,128]{1,0:T(8,128)}, f32[8,128]{1,0:T(8,128)S(1)}) custom-call(f32[128,128]{1,0:T(8,128)S(1)} %factor.1.refs_0_, f32[512,128]{1,0:T(8,128)S(1)} %get-tuple-element.50.refs_1_, f32[256,384]{1,0:T(8,128)S(1)} %join.3.refs_2_.refs_0_, f32[256,384]{1,0:T(8,128)S(1)} %join.4.refs_2_.refs_3_.refs_0_, ...), custom_call_target="tpu_custom_call" | custom-call | flops 1000000000 | bytes 2097152 | tf_op jit(solution)/shard_map/apply_first/pallas_call | solution.py:420
  74.9 1.6 %apply_next.2.refs_4_ = f32[128,8192]{1,0:T(8,128)} custom-call(f32[128,128]{1,0:T(8,128)S(1)} %factor.1.refs_0_, f32[256,384]{1,0:T(8,128)S(1)} %pass_on.8.refs_1_, f32[256,384]{1,0:T(8,128)S(1)} %pass_on.9.refs_1_.refs_2_, f32[256,256]{1,0:T(8,128)S(1)} %pass_on.10.refs_1_.refs_3_, ...), custom_call_target="tpu_custom_call", output_to_operand_aliasing={{}: (7, {})} | custom-call | flops 1000000000 | bytes 2097152 | tf_op jit(solution)/shard_map/apply_next/pallas_call | solution.py:442
  76.6 1.2 %apply_next.3 = f32[128,8192]{1,0:T(8,128)} custom-call(f32[128,128]{1,0:T(8,128)S(1)} %factor.1.refs_0_, f32[256,384]{1,0:T(8,128)S(1)} %collective-permute-done.25.refs_1_, f32[256,384]{1,0:T(8,128)S(1)} %collective-permute-done.27.refs_2_, f32[256,256]{1,0:T(8,128)S(1)} %collective-permute-done.29.refs_3_, ...), custom_call_target="tpu_custom_call", output_to_operand_aliasing={{}: (4, {})} | custom-call | flops 1000000000 | bytes 2097152 | tf_op jit(solution)/shard_map/apply_next/pallas_call | solution.py:442
  (82 shorter events, 18.2 us)
Async XLA Ops:
  12.7 7.1 %collective-permute-start.2 = (f32[576,256]{1,0:T(8,128)S(1)}, f32[576,256]{1,0:T(8,128)S(1)}, u32[]{:S(2)}, u32[]{:S(2)}) collective-permute-start(f32[576,256]{1,0:T(8,128)S(1)} %get-tuple-element.34.refs_3_), channel_id=1, source_target_pairs={{0,16},{1,17},{2,18},{3,19},{4,20},{5,21},{6,22},{7,23},{8,24},{9,... | collective-permute-start | bytes 1769480 | tf_op jit(solution)/shard_map/ppermute | solution.py:456
  14.1 9.7 %collective-permute-start.5 = (f32[256,384]{1,0:T(8,128)S(1)}, f32[256,384]{1,0:T(8,128)S(1)}, u32[]{:S(2)}, u32[]{:S(2)}) collective-permute-start(f32[256,384]{1,0:T(8,128)S(1)} %get-tuple-element.41.refs_1_), channel_id=1, source_target_pairs={{0,20},{1,29},{2,22},{3,31},{4,24},{5,17},{6,26},{7,19},{8,28},{9,... | collective-permute-start | bytes 1179656 | tf_op jit(solution)/shard_map/ppermute | solution.py:456
  17.6 7.6 %collective-permute-start.4 = (f32[256,384]{1,0:T(8,128)S(1)}, f32[256,384]{1,0:T(8,128)S(1)}, u32[]{:S(2)}, u32[]{:S(2)}) collective-permute-start(f32[256,384]{1,0:T(8,128)S(1)} %get-tuple-element.40.refs_1_), channel_id=1, source_target_pairs={{0,112},{1,49},{2,114},{3,51},{4,52},{5,117},{6,54},{7,119},{8,120... | collective-permute-start | bytes 1179656 | tf_op jit(solution)/shard_map/ppermute | solution.py:456
  19.9 8.6 %collective-permute-start.3 = (f32[320,256]{1,0:T(8,128)S(1)}, f32[320,256]{1,0:T(8,128)S(1)}, u32[]{:S(2)}, u32[]{:S(2)}) collective-permute-start(f32[320,256]{1,0:T(8,128)S(1)} %get-tuple-element.39.refs_1_), channel_id=1, source_target_pairs={{0,17},{1,18},{2,19},{3,16},{4,23},{5,20},{6,21},{7,22},{8,25},{9,... | collective-permute-start | bytes 983048 | tf_op jit(solution)/shard_map/ppermute | solution.py:456
  23.8 6.0 %collective-permute-start.8 = (f32[128,384]{1,0:T(8,128)S(1)}, f32[128,384]{1,0:T(8,128)S(1)}, u32[]{:S(2)}, u32[]{:S(2)}) collective-permute-start(f32[128,384]{1,0:T(8,128)S(1)} %get-tuple-element.47.refs_1_), channel_id=1, source_target_pairs={{0,28},{1,21},{2,30},{3,23},{4,16},{5,25},{6,18},{7,27},{8,20},{9,... | collective-permute-start | bytes 589832 | tf_op jit(solution)/shard_map/ppermute | solution.py:456
  25.2 6.4 %collective-permute-start.7 = (f32[128,384]{1,0:T(8,128)S(1)}, f32[128,384]{1,0:T(8,128)S(1)}, u32[]{:S(2)}, u32[]{:S(2)}) collective-permute-start(f32[128,384]{1,0:T(8,128)S(1)} %get-tuple-element.46.refs_1_), channel_id=1, source_target_pairs={{0,48},{1,113},{2,50},{3,115},{4,116},{5,53},{6,118},{7,55},{8,56}... | collective-permute-start | bytes 589832 | tf_op jit(solution)/shard_map/ppermute | solution.py:456
  28.6 5.5 %collective-permute-start.6 = (f32[192,256]{1,0:T(8,128)S(1)}, f32[192,256]{1,0:T(8,128)S(1)}, u32[]{:S(2)}, u32[]{:S(2)}) collective-permute-start(f32[192,256]{1,0:T(8,128)S(1)} %get-tuple-element.45.refs_1_), channel_id=1, source_target_pairs={{0,19},{1,16},{2,17},{3,18},{4,21},{5,22},{6,23},{7,20},{8,27},{9,... | collective-permute-start | bytes 589832 | tf_op jit(solution)/shard_map/ppermute | solution.py:456
  29.8 6.9 %collective-permute-start.11 = (f32[128,384]{1,0:T(8,128)S(1)}, f32[128,384]{1,0:T(8,128)S(1)}, u32[]{:S(2)}, u32[]{:S(2)}) collective-permute-start(f32[128,384]{1,0:T(8,128)S(1)} %sum_quarter.3.refs_3_.refs_0_), channel_id=1, source_target_pairs={{0,48},{1,113},{2,50},{3,115},{4,116},{5,53},{6,118},{7,55},{8,56}... | collective-permute-start | bytes 589832 | tf_op jit(solution)/shard_map/ppermute | solution.py:456
  31.6 5.5 %collective-permute-start.10 = (f32[128,384]{1,0:T(8,128)S(1)}, f32[128,384]{1,0:T(8,128)S(1)}, u32[]{:S(2)}, u32[]{:S(2)}) collective-permute-start(f32[128,384]{1,0:T(8,128)S(1)} %sum_quarter.4.refs_3_.refs_0_), channel_id=1, source_target_pairs={{0,19},{1,16},{2,17},{3,18},{4,21},{5,22},{6,23},{7,20},{8,27},{9,... | collective-permute-start | bytes 589832 | tf_op jit(solution)/shard_map/ppermute | solution.py:456
  34.1 6.8 %collective-permute-start.9 = (f32[192,256]{1,0:T(8,128)S(1)}, f32[192,256]{1,0:T(8,128)S(1)}, u32[]{:S(2)}, u32[]{:S(2)}) collective-permute-start(f32[192,256]{1,0:T(8,128)S(1)} %sum_quarter.5.refs_2_.refs_0_), channel_id=1, source_target_pairs={{0,20},{1,29},{2,22},{3,31},{4,24},{5,17},{6,26},{7,19},{8,28},{9,... | collective-permute-start | bytes 589832 | tf_op jit(solution)/shard_map/ppermute | solution.py:456
  36.7 5.5 %collective-permute-start.14 = (f32[128,384]{1,0:T(8,128)S(1)}, f32[128,384]{1,0:T(8,128)S(1)}, u32[]{:S(2)}, u32[]{:S(2)}) collective-permute-start(f32[128,384]{1,0:T(8,128)S(1)} %sum_whole.9.refs_2_.refs_0_), channel_id=1, source_target_pairs={{0,112},{1,49},{2,114},{3,51},{4,52},{5,117},{6,54},{7,119},{8,120... | collective-permute-start | bytes 589832 | tf_op jit(solution)/shard_map/ppermute | solution.py:456
  37.2 7.3 %collective-permute-start.13 = (f32[128,384]{1,0:T(8,128)S(1)}, f32[128,384]{1,0:T(8,128)S(1)}, u32[]{:S(2)}, u32[]{:S(2)}) collective-permute-start(f32[128,384]{1,0:T(8,128)S(1)} %sum_whole.10.refs_2_.refs_0_), channel_id=1, source_target_pairs={{0,17},{1,18},{2,19},{3,16},{4,23},{5,20},{6,21},{7,22},{8,25},{9,... | collective-permute-start | bytes 589832 | tf_op jit(solution)/shard_map/ppermute | solution.py:456
  40.9 5.5 %collective-permute-start.12 = (f32[192,256]{1,0:T(8,128)S(1)}, f32[192,256]{1,0:T(8,128)S(1)}, u32[]{:S(2)}, u32[]{:S(2)}) collective-permute-start(f32[192,256]{1,0:T(8,128)S(1)} %sum_whole.11.refs_2_.refs_0_), channel_id=1, source_target_pairs={{0,28},{1,21},{2,30},{3,23},{4,16},{5,25},{6,18},{7,27},{8,20},{9,... | collective-permute-start | bytes 589832 | tf_op jit(solution)/shard_map/ppermute | solution.py:456
  42.2 6.7 %collective-permute-start.17 = (f32[128,384]{1,0:T(8,128)S(1)}, f32[128,384]{1,0:T(8,128)S(1)}, u32[]{:S(2)}, u32[]{:S(2)}) collective-permute-start(f32[128,384]{1,0:T(8,128)S(1)} %sum_whole.12.refs_2_.refs_0_), channel_id=1, source_target_pairs={{0,17},{1,18},{2,19},{3,16},{4,23},{5,20},{6,21},{7,22},{8,25},{9,... | collective-permute-start | bytes 589832 | tf_op jit(solution)/shard_map/ppermute | solution.py:456
  44.5 5.5 %collective-permute-start.16 = (f32[128,384]{1,0:T(8,128)S(1)}, f32[128,384]{1,0:T(8,128)S(1)}, u32[]{:S(2)}, u32[]{:S(2)}) collective-permute-start(f32[128,384]{1,0:T(8,128)S(1)} %sum_whole.13.refs_2_.refs_0_), channel_id=1, source_target_pairs={{0,28},{1,21},{2,30},{3,23},{4,16},{5,25},{6,18},{7,27},{8,20},{9,... | collective-permute-start | bytes 589832 | tf_op jit(solution)/shard_map/ppermute | solution.py:456
  46.4 6.7 %collective-permute-start.15 = (f32[192,256]{1,0:T(8,128)S(1)}, f32[192,256]{1,0:T(8,128)S(1)}, u32[]{:S(2)}, u32[]{:S(2)}) collective-permute-start(f32[192,256]{1,0:T(8,128)S(1)} %sum_whole.14.refs_2_.refs_0_), channel_id=1, source_target_pairs={{0,48},{1,113},{2,50},{3,115},{4,116},{5,53},{6,118},{7,55},{8,56}... | collective-permute-start | bytes 589832 | tf_op jit(solution)/shard_map/ppermute | solution.py:456
  48.9 5.5 %collective-permute-start.20 = (f32[128,384]{1,0:T(8,128)S(1)}, f32[128,384]{1,0:T(8,128)S(1)}, u32[]{:S(2)}, u32[]{:S(2)}) collective-permute-start(f32[128,384]{1,0:T(8,128)S(1)} %sum_whole.15.refs_2_.refs_0_), channel_id=1, source_target_pairs={{0,19},{1,16},{2,17},{3,18},{4,21},{5,22},{6,23},{7,20},{8,27},{9,... | collective-permute-start | bytes 589832 | tf_op jit(solution)/shard_map/ppermute | solution.py:456
  50.0 6.7 %collective-permute-start.19 = (f32[128,384]{1,0:T(8,128)S(1)}, f32[128,384]{1,0:T(8,128)S(1)}, u32[]{:S(2)}, u32[]{:S(2)}) collective-permute-start(f32[128,384]{1,0:T(8,128)S(1)} %sum_whole.16.refs_2_.refs_0_), channel_id=1, source_target_pairs={{0,20},{1,29},{2,22},{3,31},{4,24},{5,17},{6,26},{7,19},{8,28},{9,... | collective-permute-start | bytes 589832 | tf_op jit(solution)/shard_map/ppermute | solution.py:456
  53.1 6.4 %collective-permute-start.18 = (f32[192,256]{1,0:T(8,128)S(1)}, f32[192,256]{1,0:T(8,128)S(1)}, u32[]{:S(2)}, u32[]{:S(2)}) collective-permute-start(f32[192,256]{1,0:T(8,128)S(1)} %sum_whole.17.refs_2_.refs_0_), channel_id=1, source_target_pairs={{0,112},{1,49},{2,114},{3,51},{4,52},{5,117},{6,54},{7,119},{8,120... | collective-permute-start | bytes 589832 | tf_op jit(solution)/shard_map/ppermute | solution.py:456
  54.4 5.5 %collective-permute-start.23 = (f32[128,384]{1,0:T(8,128)S(1)}, f32[128,384]{1,0:T(8,128)S(1)}, u32[]{:S(2)}, u32[]{:S(2)}) collective-permute-start(f32[128,384]{1,0:T(8,128)S(1)} %sum_last.3.refs_2_.refs_0_), channel_id=1, source_target_pairs={{0,28},{1,21},{2,30},{3,23},{4,16},{5,25},{6,18},{7,27},{8,20},{9,... | collective-permute-start | bytes 589832 | tf_op jit(solution)/shard_map/ppermute | solution.py:456
  56.7 6.7 %collective-permute-start.22 = (f32[128,384]{1,0:T(8,128)S(1)}, f32[128,384]{1,0:T(8,128)S(1)}, u32[]{:S(2)}, u32[]{:S(2)}) collective-permute-start(f32[128,384]{1,0:T(8,128)S(1)} %sum_last.4.refs_2_.refs_0_), channel_id=1, source_target_pairs={{0,48},{1,113},{2,50},{3,115},{4,116},{5,53},{6,118},{7,55},{8,56}... | collective-permute-start | bytes 589832 | tf_op jit(solution)/shard_map/ppermute | solution.py:456
  59.9 12.3 %collective-permute-start.24 = (f32[256,384]{1,0:T(8,128)S(1)}, f32[256,384]{1,0:T(8,128)S(1)}, u32[]{:S(2)}, u32[]{:S(2)}) collective-permute-start(f32[256,384]{1,0:T(8,128)S(1)} %join.3.refs_2_.refs_0_), channel_id=1, source_target_pairs={{0,20},{1,29},{2,22},{3,31},{4,24},{5,17},{6,26},{7,19},{8,28},{9,... | collective-permute-start | bytes 1179656 | tf_op jit(solution)/shard_map/ppermute | solution.py:456
  63.5 8.8 %collective-permute-start.26 = (f32[256,384]{1,0:T(8,128)S(1)}, f32[256,384]{1,0:T(8,128)S(1)}, u32[]{:S(2)}, u32[]{:S(2)}) collective-permute-start(f32[256,384]{1,0:T(8,128)S(1)} %join.4.refs_2_.refs_3_.refs_0_), channel_id=1, source_target_pairs={{0,112},{1,49},{2,114},{3,51},{4,52},{5,117},{6,54},{7,119},{8,120... | collective-permute-start | bytes 1179656 | tf_op jit(solution)/shard_map/ppermute | solution.py:456
  64.3 7.9 %collective-permute-start.28 = (f32[256,256]{1,0:T(8,128)S(1)}, f32[256,256]{1,0:T(8,128)S(1)}, u32[]{:S(2)}, u32[]{:S(2)}) collective-permute-start(f32[256,256]{1,0:T(8,128)S(1)} %join.5.refs_1_.refs_4_.refs_0_), channel_id=1, source_target_pairs={{0,17},{1,18},{2,19},{3,16},{4,23},{5,20},{6,21},{7,22},{8,25},{9,... | collective-permute-start | bytes 786440 | tf_op jit(solution)/shard_map/ppermute | solution.py:456
  (9 other events, 29.1 us)

commit v4 on v3

--- a/solution.py
+++ b/solution.py
@@ -212,15 +212,14 @@
     )(*args)
 
 
-def factor_kernel(folded, inverse):
-    left = jnp.concatenate([folded[:, :K], folded[:, K:]], axis=0)
+def diagonal_mask():
     row = lax.broadcasted_iota(jnp.int32, (K, K), 0)
-    col = lax.broadcasted_iota(jnp.int32, (K, K), 1)
-    right = jnp.where(row == col, 1.0, 0.0).astype(F32)
-    lefts = [left[8 * t : 8 * t + 8] for t in range(16)]
-    rights = [right[8 * t : 8 * t + 8] for t in range(16)]
+    return row == lax.broadcasted_iota(jnp.int32, (K, K), 1)
+
+
+def eliminate(lefts, rights, starts):
     sub = lax.broadcasted_iota(jnp.int32, (8, K), 0)
-    for start in range(0, K, AHEAD):
+    for start in starts:
         tile, at = divmod(start, 8)
         columns = [
             [jnp.broadcast_to(lefts[t][:, start + k : start + k + 1], (8, K)) for t in range(tile, 16)]
@@ -248,25 +247,37 @@
             for k in range(AHEAD):
                 lefts[t] = lefts[t] - columns[k][t - tile] * rows_left[k]
                 rights[t] = rights[t] - columns[k][t - tile] * rows_right[k]
-    left = jnp.concatenate(lefts, axis=0)
-    right = jnp.concatenate(rights, axis=0)
-    diagonal = jnp.sum(jnp.where(row == col, left, 0.0), axis=1, keepdims=True)
-    inverse[...] = right * lax.rsqrt(diagonal)
-
-
-def factor(folded):
-    return pl.pallas_call(
-        factor_kernel,
-        in_specs=[VMEM],
-        out_specs=VMEM,
-        out_shape=jax.ShapeDtypeStruct((K, K), F32),
-        cost_estimate=pl.CostEstimate(flops=6 * 10**9, bytes_accessed=MIB, transcendentals=0),
-        compiler_params=pltpu.CompilerParams(vmem_limit_bytes=8 * MIB),
-        name="factor",
-    )(folded)
-
-
-def call_in_turn(body, args, shapes, after, name):
+
+
+def tiles_of(value):
+    return [value[8 * t : 8 * t + 8] for t in range(16)]
+
+
+def factor_part(state, panels, after):
+    starts = range(panels[0] * AHEAD, panels[1] * AHEAD, AHEAD)
+    last = panels[1] * AHEAD == K
+
+    def body(*refs):
+        if len(state) == 1:
+            folded = refs[0]
+            left = jnp.concatenate([folded[:, :K], folded[:, K:]], axis=0)
+            right = jnp.where(diagonal_mask(), 1.0, 0.0).astype(F32)
+        else:
+            left, right = refs[0][...], refs[1][...]
+        lefts, rights = tiles_of(left), tiles_of(right)
+        eliminate(lefts, rights, starts)
+        left, right = jnp.concatenate(lefts, axis=0), jnp.concatenate(rights, axis=0)
+        if last:
+            diagonal = jnp.sum(jnp.where(diagonal_mask(), left, 0.0), axis=1, keepdims=True)
+            refs[-1][...] = right * lax.rsqrt(diagonal)
+        else:
+            refs[-2][...] = left
+            refs[-1][...] = right
+
+    return call_in_turn(body, list(state), [(K, K)] * (1 if last else 2), after, "factor_part", 4 * MIB, 10**9)
+
+
+def call_in_turn(body, args, shapes, after, name, limit=MIB, flops=10**8):
     extra = [] if after is None else [after]
     any_space = pl.BlockSpec(memory_space=pl.ANY)
 
@@ -278,8 +289,8 @@
         in_specs=[VMEM] * len(args) + [any_space] * len(extra),
         out_specs=[VMEM] * len(shapes),
         out_shape=[jax.ShapeDtypeStruct(shape, F32) for shape in shapes],
-        compiler_params=pltpu.CompilerParams(vmem_limit_bytes=MIB),
-        cost_estimate=pl.CostEstimate(flops=10**8, bytes_accessed=MIB // 4, transcendentals=0),
+        compiler_params=pltpu.CompilerParams(vmem_limit_bytes=limit),
+        cost_estimate=pl.CostEstimate(flops=flops, bytes_accessed=MIB // 4, transcendentals=0),
         name=name,
     )(*args, *extra)
 
@@ -485,14 +496,17 @@
         states[chain], *rest = sum_last(states[chain], got, after)
         after = states[chain]
         gram = rest[0] if rest else gram
-    for chain in turns:
-        near[chain] = after = join(states[chain], send(states[chain], ring_pairs(chain, 1, FLIP[chain])), after)
-    inverse = factor(pass_on(gram, after))
+    state = [gram]
+    for chain, panels in zip(turns, ((0, 2), (2, 4), (4, 6))):
+        state = factor_part(state, panels, after)
+        got = send(states[chain], ring_pairs(chain, 1, FLIP[chain]))
+        near[chain] = after = join(states[chain], got, state[0])
+    (inverse,) = factor_part(state, (6, 16), after)
     scale = math.sqrt(total_rows)
     out, basis, mark = apply_first(inverse, near, [(a, 0, 0) for a in range(3)], sampled, scale)
+    near_other = [send(pass_on(part, mark), CORE_PAIRS) for part in near]
     for chain in turns:
         far[chain] = pass_on(send(near[chain], ring_pairs(chain, 0, FLIP[chain])), mark)
-    near_other = [send(pass_on(part, later), CORE_PAIRS) for part, later in zip(near, far)]
     far_other = [send(part, CORE_PAIRS) for part in far]
     middle = [(a, 0, 2) for a in range(3)] + [(a, 1, 0) for a in range(3)]
     out = apply_next(inverse, far + near_other, middle, out)

time: 78.1 us -> 77.5 us (level)
  waiting for transfers between devices: 13.4 us -> 12.1 us
    pallas_call x24 -> x28, Pallas kernels: 0.74 us -> 5.19 us  [call_in_turn(): pl.pallas_call(kernel, in_specs=[VMEM] * len(args) + [any_space] * len(ex...]
    pallas_call x1 -> x0, Pallas kernels: 4.01 us -> none  [factor(): pl.pallas_call(factor_kernel, in_specs=[VMEM], out_specs=VMEM, out_shape=...]
    ppermute x33, waiting for transfers between devices: 13.4 us -> 12.1 us  [send(): return lax.ppermute(value, AXES, pairs)]
  transfers between devices with their start and end apart: 33 -> 33, of which waited for: 19 -> 20; matrix products, arithmetic and copies ran while one was open for 0% -> 0% of each run, Pallas kernels for 14% -> 15%
where the time goes in v4:
time: 77.5 us; the launch traced here: 77.4 us
  starting transfers between devices  42.1 us (54%)
  Pallas kernels  22.1 us (29%)
  waiting for transfers between devices  12.1 us (16%)
  between operations  1.09 us (1%)
    ppermute x33, starting transfers between devices, send(): return lax.ppermute(value, AXES, pairs)  42.1 us
    ppermute x33, waiting for transfers between devices, send(): return lax.ppermute(value, AXES, pairs)  12.1 us
    pallas_call x1, Pallas kernels, sample(): pl.pallas_call(sample_kernel, in_specs=[HBM, HBM], out_specs=[VMEM] * 7,...  9.2 us
    pallas_call x28, Pallas kernels, call_in_turn(): pl.pallas_call(kernel, in_specs=[VMEM] * len(args) + [any_space] * len(ex...  5.19 us
    pallas_call x2, Pallas kernels, apply_next(): pl.pallas_call(lambda *refs: apply_next_kernel(pieces, *refs), in_specs=[...  2.87 us
    pallas_call x3, Pallas kernels, keep(): pl.pallas_call(lambda *refs: keep_kernel(chain, *refs), in_specs=[VMEM] *...  2.11 us
  transfers between devices with their start and end apart: 33, of which 20 were waited for; matrix products, arithmetic and copies ran while one was open for 0% of the time, Pallas kernels for 15%

profile of v4, /device:TPU:1, one launch (start us, length us, event | category | flops | bytes accessed | tf_op | source)
XLA Modules:
  0.0 77.4 jit_solution(13877785657964062897)
XLA Ops:
  0.6 9.2 %sample.1 = (f32[512,128]{1,0:T(8,128)S(1)}, bf16[256,512]{1,0:T(8,128)(2,1)S(1)}, bf16[4,512,1024]{2,1,0:T(8,128)(2,1)S(1)}, bf16[4,512,1024]{2,1,0:T(8,128)(2,...) custom-call(f32[512,8192]{1,0:T(8,128)} %slab.1, ...), custom_call_target="tpu_custom_call" | custom-call | flops 8000000000 | bytes 22020096 | tf_op jit(solution)/shard_map/sample/pallas_call | solution.py:147
  9.8 1.5 %collective-permute-start = (f32[512,384]{1,0:T(8,128)S(1)}, f32[512,384]{1,0:T(8,128)S(1)}, u32[]{:S(2)}, u32[]{:S(2)}) collective-permute-start(f32[512,384]{1,0:T(8,128)S(1)} %get-tuple-element.39.after), channel_id=1, source_target_pairs={{0,16},{1,17},{2,18},{3,19},{4,20},{5,21},{6,22},{7,23},{8,24},{9,... | collective-permute-start | bytes 2359304 | tf_op jit(solution)/shard_map/ppermute | solution.py:467
  11.3 1.3 %rest_to_send.1 = (f32[512,384]{1,0:T(8,128)S(1)}, f32[576,256]{1,0:T(8,128)S(1)}) custom-call(bf16[256,512]{1,0:T(8,128)(2,1)S(1)} %get-tuple-element.34.left.refs_0_, bf16[4,512,1024]{2,1,0:T(8,128)(2,1)S(1)} %get-tuple-element.37.high, bf16[4,512,1024]{2,1,0:T(8,128)(2,1)S(1)} %get-tuple-element.38.low, f32[512,384]{1,0:T(8,128)S(1)} %get-tuple-element.39.after), custom_call_target="tpu_custom_call" | custom-call | flops 1500000000 | bytes 1048576 | tf_op jit(solution)/shard_map/rest_to_send/pallas_call | solution.py:179
  14.1 2.6 %collective-permute-start.5 = (f32[256,384]{1,0:T(8,128)S(1)}, f32[256,384]{1,0:T(8,128)S(1)}, u32[]{:S(2)}, u32[]{:S(2)}) collective-permute-start(f32[256,384]{1,0:T(8,128)S(1)} %get-tuple-element.47.refs_1_), channel_id=1, source_target_pairs={{0,20},{1,29},{2,22},{3,31},{4,24},{5,17},{6,26},{7,19},{8,28},{9,... | collective-permute-start | bytes 1179656 | tf_op jit(solution)/shard_map/ppermute | solution.py:467
  17.6 1.7 %collective-permute-start.4 = (f32[256,384]{1,0:T(8,128)S(1)}, f32[256,384]{1,0:T(8,128)S(1)}, u32[]{:S(2)}, u32[]{:S(2)}) collective-permute-start(f32[256,384]{1,0:T(8,128)S(1)} %get-tuple-element.46.refs_1_), channel_id=1, source_target_pairs={{0,112},{1,49},{2,114},{3,51},{4,52},{5,117},{6,54},{7,119},{8,120... | collective-permute-start | bytes 1179656 | tf_op jit(solution)/shard_map/ppermute | solution.py:467
  19.9 3.8 %collective-permute-start.3 = (f32[320,256]{1,0:T(8,128)S(1)}, f32[320,256]{1,0:T(8,128)S(1)}, u32[]{:S(2)}, u32[]{:S(2)}) collective-permute-start(f32[320,256]{1,0:T(8,128)S(1)} %get-tuple-element.45.refs_1_), channel_id=1, source_target_pairs={{0,17},{1,18},{2,19},{3,16},{4,23},{5,20},{6,21},{7,22},{8,25},{9,... | collective-permute-start | bytes 983048 | tf_op jit(solution)/shard_map/ppermute | solution.py:467
  25.2 2.8 %collective-permute-start.7 = (f32[128,384]{1,0:T(8,128)S(1)}, f32[128,384]{1,0:T(8,128)S(1)}, u32[]{:S(2)}, u32[]{:S(2)}) collective-permute-start(f32[128,384]{1,0:T(8,128)S(1)} %get-tuple-element.52.refs_1_), channel_id=1, source_target_pairs={{0,48},{1,113},{2,50},{3,115},{4,116},{5,53},{6,118},{7,55},{8,56}... | collective-permute-start | bytes 589832 | tf_op jit(solution)/shard_map/ppermute | solution.py:467
  28.6 1.2 %collective-permute-start.6 = (f32[192,256]{1,0:T(8,128)S(1)}, f32[192,256]{1,0:T(8,128)S(1)}, u32[]{:S(2)}, u32[]{:S(2)}) collective-permute-start(f32[192,256]{1,0:T(8,128)S(1)} %get-tuple-element.51.refs_1_), channel_id=1, source_target_pairs={{0,19},{1,16},{2,17},{3,18},{4,21},{5,22},{6,23},{7,20},{8,27},{9,... | collective-permute-start | bytes 589832 | tf_op jit(solution)/shard_map/ppermute | solution.py:467
  29.8 1.7 %collective-permute-start.11 = (f32[128,384]{1,0:T(8,128)S(1)}, f32[128,384]{1,0:T(8,128)S(1)}, u32[]{:S(2)}, u32[]{:S(2)}) collective-permute-start(f32[128,384]{1,0:T(8,128)S(1)} %sum_quarter.3.refs_3_.refs_0_), channel_id=1, source_target_pairs={{0,48},{1,113},{2,50},{3,115},{4,116},{5,53},{6,118},{7,55},{8,56}... | collective-permute-start | bytes 589832 | tf_op jit(solution)/shard_map/ppermute | solution.py:467
  31.6 1.9 %collective-permute-start.10 = (f32[128,384]{1,0:T(8,128)S(1)}, f32[128,384]{1,0:T(8,128)S(1)}, u32[]{:S(2)}, u32[]{:S(2)}) collective-permute-start(f32[128,384]{1,0:T(8,128)S(1)} %sum_quarter.4.refs_3_.refs_0_), channel_id=1, source_target_pairs={{0,19},{1,16},{2,17},{3,18},{4,21},{5,22},{6,23},{7,20},{8,27},{9,... | collective-permute-start | bytes 589832 | tf_op jit(solution)/shard_map/ppermute | solution.py:467
  34.1 1.5 %collective-permute-start.9 = (f32[192,256]{1,0:T(8,128)S(1)}, f32[192,256]{1,0:T(8,128)S(1)}, u32[]{:S(2)}, u32[]{:S(2)}) collective-permute-start(f32[192,256]{1,0:T(8,128)S(1)} %sum_quarter.5.refs_2_.refs_0_), channel_id=1, source_target_pairs={{0,20},{1,29},{2,22},{3,31},{4,24},{5,17},{6,26},{7,19},{8,28},{9,... | collective-permute-start | bytes 589832 | tf_op jit(solution)/shard_map/ppermute | solution.py:467
  35.5 1.2 %collective-permute-done.11.refs_1_ = f32[128,384]{1,0:T(8,128)S(1)} collective-permute-done((f32[128,384]{1,0:T(8,128)S(1)}, f32[128,384]{1,0:T(8,128)S(1)}, u32[]{:S(2)}, u32[]{:S(2)}) %collective-permute-start.11) | collective-permute-done | bytes 196640 | tf_op jit(solution)/shard_map/ppermute | solution.py:467
  37.2 3.6 %collective-permute-start.13 = (f32[128,384]{1,0:T(8,128)S(1)}, f32[128,384]{1,0:T(8,128)S(1)}, u32[]{:S(2)}, u32[]{:S(2)}) collective-permute-start(f32[128,384]{1,0:T(8,128)S(1)} %sum_whole.10.refs_2_.refs_0_), channel_id=1, source_target_pairs={{0,17},{1,18},{2,19},{3,16},{4,23},{5,20},{6,21},{7,22},{8,25},{9,... | collective-permute-start | bytes 589832 | tf_op jit(solution)/shard_map/ppermute | solution.py:467
  42.2 2.0 %collective-permute-start.17 = (f32[128,384]{1,0:T(8,128)S(1)}, f32[128,384]{1,0:T(8,128)S(1)}, u32[]{:S(2)}, u32[]{:S(2)}) collective-permute-start(f32[128,384]{1,0:T(8,128)S(1)} %sum_whole.12.refs_2_.refs_0_), channel_id=1, source_target_pairs={{0,17},{1,18},{2,19},{3,16},{4,23},{5,20},{6,21},{7,22},{8,25},{9,... | collective-permute-start | bytes 589832 | tf_op jit(solution)/shard_map/ppermute | solution.py:467
  46.4 2.4 %collective-permute-start.15 = (f32[192,256]{1,0:T(8,128)S(1)}, f32[192,256]{1,0:T(8,128)S(1)}, u32[]{:S(2)}, u32[]{:S(2)}) collective-permute-start(f32[192,256]{1,0:T(8,128)S(1)} %sum_whole.14.refs_2_.refs_0_), channel_id=1, source_target_pairs={{0,48},{1,113},{2,50},{3,115},{4,116},{5,53},{6,118},{7,55},{8,56}... | collective-permute-start | bytes 589832 | tf_op jit(solution)/shard_map/ppermute | solution.py:467
  50.0 2.8 %collective-permute-start.19 = (f32[128,384]{1,0:T(8,128)S(1)}, f32[128,384]{1,0:T(8,128)S(1)}, u32[]{:S(2)}, u32[]{:S(2)}) collective-permute-start(f32[128,384]{1,0:T(8,128)S(1)} %sum_whole.16.refs_2_.refs_0_), channel_id=1, source_target_pairs={{0,20},{1,29},{2,22},{3,31},{4,24},{5,17},{6,26},{7,19},{8,28},{9,... | collective-permute-start | bytes 589832 | tf_op jit(solution)/shard_map/ppermute | solution.py:467
  55.0 1.7 %collective-permute-done.19.refs_1_ = f32[128,384]{1,0:T(8,128)S(1)} collective-permute-done((f32[128,384]{1,0:T(8,128)S(1)}, f32[128,384]{1,0:T(8,128)S(1)}, u32[]{:S(2)}, u32[]{:S(2)}) %collective-permute-start.19) | collective-permute-done | bytes 196640 | tf_op jit(solution)/shard_map/ppermute | solution.py:467
  56.7 2.7 %collective-permute-start.22 = (f32[128,384]{1,0:T(8,128)S(1)}, f32[128,384]{1,0:T(8,128)S(1)}, u32[]{:S(2)}, u32[]{:S(2)}) collective-permute-start(f32[128,384]{1,0:T(8,128)S(1)} %sum_last.4.refs_2_.refs_0_), channel_id=1, source_target_pairs={{0,48},{1,113},{2,50},{3,115},{4,116},{5,53},{6,118},{7,55},{8,56}... | collective-permute-start | bytes 589832 | tf_op jit(solution)/shard_map/ppermute | solution.py:467
  60.6 1.8 %collective-permute-start.24 = (f32[256,384]{1,0:T(8,128)S(1)}, f32[256,384]{1,0:T(8,128)S(1)}, u32[]{:S(2)}, u32[]{:S(2)}) collective-permute-start(f32[256,384]{1,0:T(8,128)S(1)} %join.3.refs_2_.refs_0_), channel_id=1, source_target_pairs={{0,20},{1,29},{2,22},{3,31},{4,24},{5,17},{6,26},{7,19},{8,28},{9,... | collective-permute-start | bytes 1179656 | tf_op jit(solution)/shard_map/ppermute | solution.py:467
  64.3 2.6 %collective-permute-start.28 = (f32[256,256]{1,0:T(8,128)S(1)}, f32[256,256]{1,0:T(8,128)S(1)}, u32[]{:S(2)}, u32[]{:S(2)}) collective-permute-start(f32[256,256]{1,0:T(8,128)S(1)} %join.5.refs_2_.refs_4_.refs_0_), channel_id=1, source_target_pairs={{0,17},{1,18},{2,19},{3,16},{4,23},{5,20},{6,21},{7,22},{8,25},{9,... | collective-permute-start | bytes 786440 | tf_op jit(solution)/shard_map/ppermute | solution.py:467
  66.9 2.4 %factor_part.7.refs_0_ = f32[128,128]{1,0:T(8,128)S(1)} custom-call(f32[128,128]{1,0:T(8,128)S(1)} %get-tuple-element.60.refs_2_.refs_0_, f32[128,128]{1,0:T(8,128)S(1)} %get-tuple-element.61.refs_1_, f32[256,256]{1,0:T(8,128)S(1)} %join.5.refs_2_.refs_4_.refs_0_), custom_call_target="tpu_custom_call" | custom-call | flops 1000000000 | bytes 262144 | tf_op jit(solution)/shard_map/factor_part/pallas_call | solution.py:287
  69.2 1.4 %apply_first.1 = (f32[128,8192]{1,0:T(8,128)}, f32[512,128]{1,0:T(8,128)}, f32[8,128]{1,0:T(8,128)S(1)}) custom-call(f32[128,128]{1,0:T(8,128)S(1)} %factor_part.7.refs_0_, f32[512,128]{1,0:T(8,128)S(1)} %get-tuple-element.62.refs_1_, f32[256,384]{1,0:T(8,128)S(1)} %join.3.refs_2_.refs_0_, f32[256,384]{1,0:T(8,128)S(1)} %join.4.refs_2_.refs_3_.refs_0_, ...), custom_call_target="tpu_custom_call" | custom-call | flops 1000000000 | bytes 2097152 | tf_op jit(solution)/shard_map/apply_first/pallas_call | solution.py:431
  74.3 1.6 %apply_next.2.refs_4_ = f32[128,8192]{1,0:T(8,128)} custom-call(f32[128,128]{1,0:T(8,128)S(1)} %factor_part.7.refs_0_, f32[256,384]{1,0:T(8,128)S(1)} %pass_on.6.refs_1_, f32[256,384]{1,0:T(8,128)S(1)} %pass_on.7.refs_2_, f32[256,256]{1,0:T(8,128)S(1)} %pass_on.8.refs_3_, ...), custom_call_target="tpu_custom_call", output_to_operand_aliasing={{}: (7, {})} | custom-call | flops 1000000000 | bytes 2097152 | tf_op jit(solution)/shard_map/apply_next/pallas_call | solution.py:453
  76.0 1.2 %apply_next.3 = f32[128,8192]{1,0:T(8,128)} custom-call(f32[128,128]{1,0:T(8,128)S(1)} %factor_part.7.refs_0_, f32[256,384]{1,0:T(8,128)S(1)} %collective-permute-done.25.refs_1_, f32[256,384]{1,0:T(8,128)S(1)} %collective-permute-done.27.refs_2_, f32[256,256]{1,0:T(8,128)S(1)} %collective-permute-done.29.refs_3_, ...), custom_call_target="tpu_custom_call", output_to_operand_aliasing={{}: (4, {})} | custom-call | flops 1000000000 | bytes 2097152 | tf_op jit(solution)/shard_map/apply_next/pallas_call | solution.py:453
  (84 shorter events, 19.7 us)
Async XLA Ops:
  12.7 7.1 %collective-permute-start.2 = (f32[576,256]{1,0:T(8,128)S(1)}, f32[576,256]{1,0:T(8,128)S(1)}, u32[]{:S(2)}, u32[]{:S(2)}) collective-permute-start(f32[576,256]{1,0:T(8,128)S(1)} %get-tuple-element.40.refs_3_), channel_id=1, source_target_pairs={{0,16},{1,17},{2,18},{3,19},{4,20},{5,21},{6,22},{7,23},{8,24},{9,... | collective-permute-start | bytes 1769480 | tf_op jit(solution)/shard_map/ppermute | solution.py:467
  14.1 9.7 %collective-permute-start.5 = (f32[256,384]{1,0:T(8,128)S(1)}, f32[256,384]{1,0:T(8,128)S(1)}, u32[]{:S(2)}, u32[]{:S(2)}) collective-permute-start(f32[256,384]{1,0:T(8,128)S(1)} %get-tuple-element.47.refs_1_), channel_id=1, source_target_pairs={{0,20},{1,29},{2,22},{3,31},{4,24},{5,17},{6,26},{7,19},{8,28},{9,... | collective-permute-start | bytes 1179656 | tf_op jit(solution)/shard_map/ppermute | solution.py:467
  17.6 7.6 %collective-permute-start.4 = (f32[256,384]{1,0:T(8,128)S(1)}, f32[256,384]{1,0:T(8,128)S(1)}, u32[]{:S(2)}, u32[]{:S(2)}) collective-permute-start(f32[256,384]{1,0:T(8,128)S(1)} %get-tuple-element.46.refs_1_), channel_id=1, source_target_pairs={{0,112},{1,49},{2,114},{3,51},{4,52},{5,117},{6,54},{7,119},{8,120... | collective-permute-start | bytes 1179656 | tf_op jit(solution)/shard_map/ppermute | solution.py:467
  19.9 8.6 %collective-permute-start.3 = (f32[320,256]{1,0:T(8,128)S(1)}, f32[320,256]{1,0:T(8,128)S(1)}, u32[]{:S(2)}, u32[]{:S(2)}) collective-permute-start(f32[320,256]{1,0:T(8,128)S(1)} %get-tuple-element.45.refs_1_), channel_id=1, source_target_pairs={{0,17},{1,18},{2,19},{3,16},{4,23},{5,20},{6,21},{7,22},{8,25},{9,... | collective-permute-start | bytes 983048 | tf_op jit(solution)/shard_map/ppermute | solution.py:467
  23.8 6.0 %collective-permute-start.8 = (f32[128,384]{1,0:T(8,128)S(1)}, f32[128,384]{1,0:T(8,128)S(1)}, u32[]{:S(2)}, u32[]{:S(2)}) collective-permute-start(f32[128,384]{1,0:T(8,128)S(1)} %get-tuple-element.53.refs_1_), channel_id=1, source_target_pairs={{0,28},{1,21},{2,30},{3,23},{4,16},{5,25},{6,18},{7,27},{8,20},{9,... | collective-permute-start | bytes 589832 | tf_op jit(solution)/shard_map/ppermute | solution.py:467
  25.2 6.4 %collective-permute-start.7 = (f32[128,384]{1,0:T(8,128)S(1)}, f32[128,384]{1,0:T(8,128)S(1)}, u32[]{:S(2)}, u32[]{:S(2)}) collective-permute-start(f32[128,384]{1,0:T(8,128)S(1)} %get-tuple-element.52.refs_1_), channel_id=1, source_target_pairs={{0,48},{1,113},{2,50},{3,115},{4,116},{5,53},{6,118},{7,55},{8,56}... | collective-permute-start | bytes 589832 | tf_op jit(solution)/shard_map/ppermute | solution.py:467
  28.6 5.5 %collective-permute-start.6 = (f32[192,256]{1,0:T(8,128)S(1)}, f32[192,256]{1,0:T(8,128)S(1)}, u32[]{:S(2)}, u32[]{:S(2)}) collective-permute-start(f32[192,256]{1,0:T(8,128)S(1)} %get-tuple-element.51.refs_1_), channel_id=1, source_target_pairs={{0,19},{1,16},{2,17},{3,18},{4,21},{5,22},{6,23},{7,20},{8,27},{9,... | collective-permute-start | bytes 589832 | tf_op jit(solution)/shard_map/ppermute | solution.py:467
  29.8 6.9 %collective-permute-start.11 = (f32[128,384]{1,0:T(8,128)S(1)}, f32[128,384]{1,0:T(8,128)S(1)}, u32[]{:S(2)}, u32[]{:S(2)}) collective-permute-start(f32[128,384]{1,0:T(8,128)S(1)} %sum_quarter.3.refs_3_.refs_0_), channel_id=1, source_target_pairs={{0,48},{1,113},{2,50},{3,115},{4,116},{5,53},{6,118},{7,55},{8,56}... | collective-permute-start | bytes 589832 | tf_op jit(solution)/shard_map/ppermute | solution.py:467
  31.6 5.5 %collective-permute-start.10 = (f32[128,384]{1,0:T(8,128)S(1)}, f32[128,384]{1,0:T(8,128)S(1)}, u32[]{:S(2)}, u32[]{:S(2)}) collective-permute-start(f32[128,384]{1,0:T(8,128)S(1)} %sum_quarter.4.refs_3_.refs_0_), channel_id=1, source_target_pairs={{0,19},{1,16},{2,17},{3,18},{4,21},{5,22},{6,23},{7,20},{8,27},{9,... | collective-permute-start | bytes 589832 | tf_op jit(solution)/shard_map/ppermute | solution.py:467
  34.1 6.8 %collective-permute-start.9 = (f32[192,256]{1,0:T(8,128)S(1)}, f32[192,256]{1,0:T(8,128)S(1)}, u32[]{:S(2)}, u32[]{:S(2)}) collective-permute-start(f32[192,256]{1,0:T(8,128)S(1)} %sum_quarter.5.refs_2_.refs_0_), channel_id=1, source_target_pairs={{0,20},{1,29},{2,22},{3,31},{4,24},{5,17},{6,26},{7,19},{8,28},{9,... | collective-permute-start | bytes 589832 | tf_op jit(solution)/shard_map/ppermute | solution.py:467
  36.7 5.5 %collective-permute-start.14 = (f32[128,384]{1,0:T(8,128)S(1)}, f32[128,384]{1,0:T(8,128)S(1)}, u32[]{:S(2)}, u32[]{:S(2)}) collective-permute-start(f32[128,384]{1,0:T(8,128)S(1)} %sum_whole.9.refs_2_.refs_0_), channel_id=1, source_target_pairs={{0,112},{1,49},{2,114},{3,51},{4,52},{5,117},{6,54},{7,119},{8,120... | collective-permute-start | bytes 589832 | tf_op jit(solution)/shard_map/ppermute | solution.py:467
  37.2 7.3 %collective-permute-start.13 = (f32[128,384]{1,0:T(8,128)S(1)}, f32[128,384]{1,0:T(8,128)S(1)}, u32[]{:S(2)}, u32[]{:S(2)}) collective-permute-start(f32[128,384]{1,0:T(8,128)S(1)} %sum_whole.10.refs_2_.refs_0_), channel_id=1, source_target_pairs={{0,17},{1,18},{2,19},{3,16},{4,23},{5,20},{6,21},{7,22},{8,25},{9,... | collective-permute-start | bytes 589832 | tf_op jit(solution)/shard_map/ppermute | solution.py:467
  40.9 5.5 %collective-permute-start.12 = (f32[192,256]{1,0:T(8,128)S(1)}, f32[192,256]{1,0:T(8,128)S(1)}, u32[]{:S(2)}, u32[]{:S(2)}) collective-permute-start(f32[192,256]{1,0:T(8,128)S(1)} %sum_whole.11.refs_2_.refs_0_), channel_id=1, source_target_pairs={{0,28},{1,21},{2,30},{3,23},{4,16},{5,25},{6,18},{7,27},{8,20},{9,... | collective-permute-start | bytes 589832 | tf_op jit(solution)/shard_map/ppermute | solution.py:467
  42.2 6.7 %collective-permute-start.17 = (f32[128,384]{1,0:T(8,128)S(1)}, f32[128,384]{1,0:T(8,128)S(1)}, u32[]{:S(2)}, u32[]{:S(2)}) collective-permute-start(f32[128,384]{1,0:T(8,128)S(1)} %sum_whole.12.refs_2_.refs_0_), channel_id=1, source_target_pairs={{0,17},{1,18},{2,19},{3,16},{4,23},{5,20},{6,21},{7,22},{8,25},{9,... | collective-permute-start | bytes 589832 | tf_op jit(solution)/shard_map/ppermute | solution.py:467
  44.5 5.5 %collective-permute-start.16 = (f32[128,384]{1,0:T(8,128)S(1)}, f32[128,384]{1,0:T(8,128)S(1)}, u32[]{:S(2)}, u32[]{:S(2)}) collective-permute-start(f32[128,384]{1,0:T(8,128)S(1)} %sum_whole.13.refs_2_.refs_0_), channel_id=1, source_target_pairs={{0,28},{1,21},{2,30},{3,23},{4,16},{5,25},{6,18},{7,27},{8,20},{9,... | collective-permute-start | bytes 589832 | tf_op jit(solution)/shard_map/ppermute | solution.py:467
  46.4 6.7 %collective-permute-start.15 = (f32[192,256]{1,0:T(8,128)S(1)}, f32[192,256]{1,0:T(8,128)S(1)}, u32[]{:S(2)}, u32[]{:S(2)}) collective-permute-start(f32[192,256]{1,0:T(8,128)S(1)} %sum_whole.14.refs_2_.refs_0_), channel_id=1, source_target_pairs={{0,48},{1,113},{2,50},{3,115},{4,116},{5,53},{6,118},{7,55},{8,56}... | collective-permute-start | bytes 589832 | tf_op jit(solution)/shard_map/ppermute | solution.py:467
  48.9 5.5 %collective-permute-start.20 = (f32[128,384]{1,0:T(8,128)S(1)}, f32[128,384]{1,0:T(8,128)S(1)}, u32[]{:S(2)}, u32[]{:S(2)}) collective-permute-start(f32[128,384]{1,0:T(8,128)S(1)} %sum_whole.15.refs_2_.refs_0_), channel_id=1, source_target_pairs={{0,19},{1,16},{2,17},{3,18},{4,21},{5,22},{6,23},{7,20},{8,27},{9,... | collective-permute-start | bytes 589832 | tf_op jit(solution)/shard_map/ppermute | solution.py:467
  50.0 6.7 %collective-permute-start.19 = (f32[128,384]{1,0:T(8,128)S(1)}, f32[128,384]{1,0:T(8,128)S(1)}, u32[]{:S(2)}, u32[]{:S(2)}) collective-permute-start(f32[128,384]{1,0:T(8,128)S(1)} %sum_whole.16.refs_2_.refs_0_), channel_id=1, source_target_pairs={{0,20},{1,29},{2,22},{3,31},{4,24},{5,17},{6,26},{7,19},{8,28},{9,... | collective-permute-start | bytes 589832 | tf_op jit(solution)/shard_map/ppermute | solution.py:467
  53.1 6.4 %collective-permute-start.18 = (f32[192,256]{1,0:T(8,128)S(1)}, f32[192,256]{1,0:T(8,128)S(1)}, u32[]{:S(2)}, u32[]{:S(2)}) collective-permute-start(f32[192,256]{1,0:T(8,128)S(1)} %sum_whole.17.refs_2_.refs_0_), channel_id=1, source_target_pairs={{0,112},{1,49},{2,114},{3,51},{4,52},{5,117},{6,54},{7,119},{8,120... | collective-permute-start | bytes 589832 | tf_op jit(solution)/shard_map/ppermute | solution.py:467
  54.4 6.2 %collective-permute-start.21 = (f32[128,384]{1,0:T(8,128)S(1)}, f32[128,384]{1,0:T(8,128)S(1)}, u32[]{:S(2)}, u32[]{:S(2)}) collective-permute-start(f32[128,384]{1,0:T(8,128)S(1)} %sum_last.3.refs_2_.refs_0_), channel_id=1, source_target_pairs={{0,28},{1,21},{2,30},{3,23},{4,16},{5,25},{6,18},{7,27},{8,20},{9,... | collective-permute-start | bytes 589832 | tf_op jit(solution)/shard_map/ppermute | solution.py:467
  56.7 6.7 %collective-permute-start.22 = (f32[128,384]{1,0:T(8,128)S(1)}, f32[128,384]{1,0:T(8,128)S(1)}, u32[]{:S(2)}, u32[]{:S(2)}) collective-permute-start(f32[128,384]{1,0:T(8,128)S(1)} %sum_last.4.refs_2_.refs_0_), channel_id=1, source_target_pairs={{0,48},{1,113},{2,50},{3,115},{4,116},{5,53},{6,118},{7,55},{8,56}... | collective-permute-start | bytes 589832 | tf_op jit(solution)/shard_map/ppermute | solution.py:467
  60.6 11.3 %collective-permute-start.24 = (f32[256,384]{1,0:T(8,128)S(1)}, f32[256,384]{1,0:T(8,128)S(1)}, u32[]{:S(2)}, u32[]{:S(2)}) collective-permute-start(f32[256,384]{1,0:T(8,128)S(1)} %join.3.refs_2_.refs_0_), channel_id=1, source_target_pairs={{0,20},{1,29},{2,22},{3,31},{4,24},{5,17},{6,26},{7,19},{8,28},{9,... | collective-permute-start | bytes 1179656 | tf_op jit(solution)/shard_map/ppermute | solution.py:467
  63.5 8.5 %collective-permute-start.26 = (f32[256,384]{1,0:T(8,128)S(1)}, f32[256,384]{1,0:T(8,128)S(1)}, u32[]{:S(2)}, u32[]{:S(2)}) collective-permute-start(f32[256,384]{1,0:T(8,128)S(1)} %join.4.refs_2_.refs_3_.refs_0_), channel_id=1, source_target_pairs={{0,112},{1,49},{2,114},{3,51},{4,52},{5,117},{6,54},{7,119},{8,120... | collective-permute-start | bytes 1179656 | tf_op jit(solution)/shard_map/ppermute | solution.py:467
  64.3 7.4 %collective-permute-start.28 = (f32[256,256]{1,0:T(8,128)S(1)}, f32[256,256]{1,0:T(8,128)S(1)}, u32[]{:S(2)}, u32[]{:S(2)}) collective-permute-start(f32[256,256]{1,0:T(8,128)S(1)} %join.5.refs_2_.refs_4_.refs_0_), channel_id=1, source_target_pairs={{0,17},{1,18},{2,19},{3,16},{4,23},{5,20},{6,21},{7,22},{8,25},{9,... | collective-permute-start | bytes 786440 | tf_op jit(solution)/shard_map/ppermute | solution.py:467
  (9 other events, 28.7 us)

commit v5 on v4

--- a/solution.py
+++ b/solution.py
@@ -127,7 +127,8 @@
         if k < 4:
             sent_high[k], sent_low[k] = slab_high, slab_low
         else:
-            high[k - 4], low[k - 4] = slab_high, slab_low
+            at = pl.ds((k - 4) * CHUNK, CHUNK)
+            high[:, at], low[:, at] = slab_high, slab_low
         sketch_high, sketch_low = halves(sketch_here[k])
         both = mul(slab_high, jnp.concatenate([sketch_high, sketch_low], axis=1))
         value = both[:, :K] + (both[:, K:] + mul(slab_low, sketch_high))
@@ -151,7 +152,8 @@
         out_shape=[
             jax.ShapeDtypeStruct((rows, K), F32),
             jax.ShapeDtypeStruct((2 * K, rows), BF16),
-            *[jax.ShapeDtypeStruct((4, rows, CHUNK), BF16)] * 4,
+            *[jax.ShapeDtypeStruct((4, rows, CHUNK), BF16)] * 2,
+            *[jax.ShapeDtypeStruct((rows, HALF), BF16)] * 2,
             jax.ShapeDtypeStruct((4 * K, WIDTH[0]), F32),
         ],
         scratch_shapes=[
@@ -190,25 +192,30 @@
     )(left, high, low, after)
 
 
-def keep_kernel(chain, left, high, low, *rest):
-    _, side = here()
+def own_kernel(chain, slots, left, high, low, *rest):
+    place, side = here()
     out = rest[-1]
+    width = WIDTH[chain]
     if len(rest) > 2:
-        out[4 * K :] = rest[0][4 * K :]
-    product(chain, side, left, high, low, out)
-
-
-def keep(chain, left, high, low, sent, after):
-    rows, width = sent.shape
-    args = [left, high, low] + ([sent] if rows > 4 * K else []) + [after]
-    return pl.pallas_call(
-        lambda *refs: keep_kernel(chain, *refs),
+        out[2 * K :] = rest[0][4 * K :]
+    for i, slot in enumerate(slots):
+        quarter = place[chain] ^ two_bits(QUARTERS, side ^ FLIP[chain], slot)
+        at = pl.ds(pl.multiple_of(STARTS[chain] + quarter * width, K), width)
+        both = mul(left[...], high[:, at])
+        out[K * i : K * i + K] = both[:K] + (both[K:] + mul(left[:K], low[:, at]))
+
+
+def own_part(chain, slots, left, high, low, sent, after):
+    args = [left, high, low] + ([] if sent is None else [sent]) + [after]
+    rows = 2 * K + (0 if sent is None else GRAM)
+    return pl.pallas_call(
+        lambda *refs: own_kernel(chain, slots, *refs),
         in_specs=[VMEM] * (len(args) - 1) + [pl.BlockSpec(memory_space=pl.ANY)],
         out_specs=VMEM,
-        out_shape=jax.ShapeDtypeStruct((rows, width), F32),
+        out_shape=jax.ShapeDtypeStruct((rows, WIDTH[chain]), F32),
         compiler_params=pltpu.CompilerParams(vmem_limit_bytes=20 * MIB),
         cost_estimate=pl.CostEstimate(flops=7 * 10**8, bytes_accessed=MIB, transcendentals=0),
-        name="keep",
+        name="own_part",
     )(*args)
 
 
@@ -303,14 +310,18 @@
         hand[half:] = rest
 
 
-def sum_cores(kept, got, after):
-    rows, width = kept.shape
-
-    def body(kept_ref, got_ref, keep, hand):
-        rest = kept_ref[4 * K :] + got_ref[4 * K :] if rows > 4 * K else None
-        split(kept_ref[: 4 * K] + got_ref[: 4 * K], rest, keep, hand)
-
-    return call_in_turn(body, [kept, got], [(2 * K, width), (rows - 2 * K, width)], after, "sum_cores")
+def sum_handed(own, got, after):
+    def body(own_ref, got_ref, out):
+        out[...] = own_ref[...] + got_ref[2 * K :]
+
+    return call_in_turn(body, [own, got], [own.shape], after, "sum_handed")[0]
+
+
+def sum_kept(own, got, after):
+    def body(own_ref, got_ref, out):
+        out[...] = own_ref[...] + got_ref[: 2 * K]
+
+    return call_in_turn(body, [own, got], [own.shape], after, "sum_kept")[0]
 
 
 def sum_half(kept, handed, got, after):
@@ -474,11 +485,14 @@
     sent = [first, *rest_to_send(left, sent_high, sent_low, first)]
     after = sent[2]
     kept, handed, states, near, far = [None] * 3, [None] * 3, [None] * 3, [None] * 3, [None] * 3
+    cores = [None] * 3
     for chain in turns:
-        got = send(sent[chain], CORE_PAIRS)
-        own = keep(chain, left, high, low, sent[chain], after)
-        kept[chain], handed[chain] = sum_cores(own, got, None)
-        after = kept[chain]
+        cores[chain] = send(sent[chain], CORE_PAIRS)
+        own = own_part(chain, (2, 3), left, high, low, sent[2] if chain == 2 else None, after)
+        handed[chain] = after = sum_handed(own, cores[chain], None)
+    for chain in turns:
+        own = own_part(chain, (0, 1), left, high, low, None, after)
+        kept[chain] = after = sum_kept(own, cores[chain], None)
     for chain in turns:
         got = send(handed[chain], ring_pairs(chain, 0, FLIP[chain]))
         kept[chain], handed[chain] = sum_half(kept[chain], handed[chain], got, after)

time: 77.5 us -> 77.4 us (level)
  starting transfers between devices: 42.1 us -> 35.1 us
  waiting for transfers between devices: 12.1 us -> 17.9 us
  Pallas kernels: 22.1 us -> 23.1 us
    ppermute x33, starting transfers between devices: 42.1 us -> 35.1 us  [send(): return lax.ppermute(value, AXES, pairs)]
    ppermute x33, waiting for transfers between devices: 12.1 us -> 17.9 us  [send(): return lax.ppermute(value, AXES, pairs)]
    pallas_call x3 -> x6, Pallas kernels: 2.11 us -> 3.11 us  [own_part(): pl.pallas_call(lambda *refs: own_kernel(chain, slots, *refs), in_specs=[V...]
    pallas_call x28 -> x31, Pallas kernels: 5.19 us -> 5.2 us  [call_in_turn(): pl.pallas_call(kernel, in_specs=[VMEM] * len(args) + [any_space] * len(ex...]
  transfers between devices with their start and end apart: 33 -> 33, of which waited for: 20 -> 19; matrix products, arithmetic and copies ran while one was open for 0% -> 0% of each run, Pallas kernels for 15% -> 16%
where the time goes in v5:
time: 77.4 us; the launch traced here: 77.3 us
  starting transfers between devices  35.1 us (45%)
  Pallas kernels  23.1 us (30%)
  waiting for transfers between devices  17.9 us (23%)
  between operations  1.2 us (2%)
    ppermute x33, starting transfers between devices, send(): return lax.ppermute(value, AXES, pairs)  35.1 us
    ppermute x33, waiting for transfers between devices, send(): return lax.ppermute(value, AXES, pairs)  17.9 us
    pallas_call x1, Pallas kernels, sample(): pl.pallas_call(sample_kernel, in_specs=[HBM, HBM], out_specs=[VMEM] * 7,...  9.2 us
    pallas_call x31, Pallas kernels, call_in_turn(): pl.pallas_call(kernel, in_specs=[VMEM] * len(args) + [any_space] * len(ex...  5.2 us
    pallas_call x6, Pallas kernels, own_part(): pl.pallas_call(lambda *refs: own_kernel(chain, slots, *refs), in_specs=[V...  3.11 us
    pallas_call x2, Pallas kernels, apply_next(): pl.pallas_call(lambda *refs: apply_next_kernel(pieces, *refs), in_specs=[...  2.87 us
  transfers between devices with their start and end apart: 33, of which 19 were waited for; matrix products, arithmetic and copies ran while one was open for 0% of the time, Pallas kernels for 16%

profile of v5, /device:TPU:1, one launch (start us, length us, event | category | flops | bytes accessed | tf_op | source)
XLA Modules:
  0.0 77.3 jit_solution(800234610530548252)
XLA Ops:
  0.6 9.2 %sample.1 = (f32[512,128]{1,0:T(8,128)S(1)}, bf16[256,512]{1,0:T(8,128)(2,1)S(1)}, bf16[4,512,1024]{2,1,0:T(8,128)(2,1)S(1)}, bf16[4,512,1024]{2,1,0:T(8,128)(2,...) custom-call(f32[512,8192]{1,0:T(8,128)} %slab.1, f32[8192,128]{1,0:T(8,128)} %sketch.1), custom_call_target="tpu_custom_call" | custom-call | flops 8000000000 | bytes 22020096 | tf_op jit(solution)/shard_map/sample/pallas_call | solution.py:148
  9.8 1.5 %collective-permute-start = (f32[512,384]{1,0:T(8,128)S(1)}, f32[512,384]{1,0:T(8,128)S(1)}, u32[]{:S(2)}, u32[]{:S(2)}) collective-permute-start(f32[512,384]{1,0:T(8,128)S(1)} %get-tuple-element.33.after), channel_id=1, source_target_pairs={{0,16},{1,17},{2,18},{3,19},{4,20},{5,21},{6,22},{7,23},{8,24},{9,... | collective-permute-start | bytes 2359304 | tf_op jit(solution)/shard_map/ppermute | solution.py:478
  11.3 1.3 %rest_to_send.1 = (f32[512,384]{1,0:T(8,128)S(1)}, f32[576,256]{1,0:T(8,128)S(1)}) custom-call(bf16[256,512]{1,0:T(8,128)(2,1)S(1)} %get-tuple-element.28.left.refs_0_, bf16[4,512,1024]{2,1,0:T(8,128)(2,1)S(1)} %get-tuple-element.31.high, bf16[4,512,1024]{2,1,0:T(8,128)(2,1)S(1)} %get-tuple-element.32.low, f32[512,384]{1,0:T(8,128)S(1)} %get-tuple-element.33.after), custom_call_target="tpu_custom_call" | custom-call | flops 1500000000 | bytes 1048576 | tf_op jit(solution)/shard_map/rest_to_send/pallas_call | solution.py:181
  13.9 2.6 %collective-permute-start.5 = (f32[256,384]{1,0:T(8,128)S(1)}, f32[256,384]{1,0:T(8,128)S(1)}, u32[]{:S(2)}, u32[]{:S(2)}) collective-permute-start(f32[256,384]{1,0:T(8,128)S(1)} %sum_handed.3.refs_3_.refs_1_), channel_id=1, source_target_pairs={{0,20},{1,29},{2,22},{3,31},{4,24},{5,17},{6,26},{7,19},{8,28},{9,... | collective-permute-start | bytes 1179656 | tf_op jit(solution)/shard_map/ppermute | solution.py:478
  17.1 1.7 %collective-permute-start.4 = (f32[256,384]{1,0:T(8,128)S(1)}, f32[256,384]{1,0:T(8,128)S(1)}, u32[]{:S(2)}, u32[]{:S(2)}) collective-permute-start(f32[256,384]{1,0:T(8,128)S(1)} %sum_handed.4.refs_4_.refs_1_), channel_id=1, source_target_pairs={{0,112},{1,49},{2,114},{3,51},{4,52},{5,117},{6,54},{7,119},{8,120... | collective-permute-start | bytes 1179656 | tf_op jit(solution)/shard_map/ppermute | solution.py:478
  19.2 4.0 %collective-permute-start.3 = (f32[320,256]{1,0:T(8,128)S(1)}, f32[320,256]{1,0:T(8,128)S(1)}, u32[]{:S(2)}, u32[]{:S(2)}) collective-permute-start(f32[320,256]{1,0:T(8,128)S(1)} %sum_handed.5.refs_3_.refs_1_), channel_id=1, source_target_pairs={{0,17},{1,18},{2,19},{3,16},{4,23},{5,20},{6,21},{7,22},{8,25},{9,... | collective-permute-start | bytes 983048 | tf_op jit(solution)/shard_map/ppermute | solution.py:478
  25.4 2.2 %collective-permute-start.7 = (f32[128,384]{1,0:T(8,128)S(1)}, f32[128,384]{1,0:T(8,128)S(1)}, u32[]{:S(2)}, u32[]{:S(2)}) collective-permute-start(f32[128,384]{1,0:T(8,128)S(1)} %get-tuple-element.40.refs_1_), channel_id=1, source_target_pairs={{0,48},{1,113},{2,50},{3,115},{4,116},{5,53},{6,118},{7,55},{8,56}... | collective-permute-start | bytes 589832 | tf_op jit(solution)/shard_map/ppermute | solution.py:478
  30.2 2.3 %collective-permute-start.11 = (f32[128,384]{1,0:T(8,128)S(1)}, f32[128,384]{1,0:T(8,128)S(1)}, u32[]{:S(2)}, u32[]{:S(2)}) collective-permute-start(f32[128,384]{1,0:T(8,128)S(1)} %sum_quarter.3.refs_3_.refs_0_), channel_id=1, source_target_pairs={{0,48},{1,113},{2,50},{3,115},{4,116},{5,53},{6,118},{7,55},{8,56}... | collective-permute-start | bytes 589832 | tf_op jit(solution)/shard_map/ppermute | solution.py:478
  33.8 1.3 %collective-permute-start.9 = (f32[192,256]{1,0:T(8,128)S(1)}, f32[192,256]{1,0:T(8,128)S(1)}, u32[]{:S(2)}, u32[]{:S(2)}) collective-permute-start(f32[192,256]{1,0:T(8,128)S(1)} %sum_quarter.5.refs_2_.refs_0_), channel_id=1, source_target_pairs={{0,20},{1,29},{2,22},{3,31},{4,24},{5,17},{6,26},{7,19},{8,28},{9,... | collective-permute-start | bytes 589832 | tf_op jit(solution)/shard_map/ppermute | solution.py:478
  35.1 1.8 %collective-permute-done.11.refs_1_ = f32[128,384]{1,0:T(8,128)S(1)} collective-permute-done((f32[128,384]{1,0:T(8,128)S(1)}, f32[128,384]{1,0:T(8,128)S(1)}, u32[]{:S(2)}, u32[]{:S(2)}) %collective-permute-start.11) | collective-permute-done | bytes 196640 | tf_op jit(solution)/shard_map/ppermute | solution.py:478
  38.0 2.4 %collective-permute-start.13 = (f32[128,384]{1,0:T(8,128)S(1)}, f32[128,384]{1,0:T(8,128)S(1)}, u32[]{:S(2)}, u32[]{:S(2)}) collective-permute-start(f32[128,384]{1,0:T(8,128)S(1)} %sum_whole.10.refs_2_.refs_0_), channel_id=1, source_target_pairs={{0,17},{1,18},{2,19},{3,16},{4,23},{5,20},{6,21},{7,22},{8,25},{9,... | collective-permute-start | bytes 589832 | tf_op jit(solution)/shard_map/ppermute | solution.py:478
  41.1 1.3 %collective-permute-done.14.refs_1_ = f32[128,384]{1,0:T(8,128)S(1)} collective-permute-done((f32[128,384]{1,0:T(8,128)S(1)}, f32[128,384]{1,0:T(8,128)S(1)}, u32[]{:S(2)}, u32[]{:S(2)}) %collective-permute-start.14) | collective-permute-done | bytes 196640 | tf_op jit(solution)/shard_map/ppermute | solution.py:478
  42.4 1.4 %collective-permute-start.17 = (f32[128,384]{1,0:T(8,128)S(1)}, f32[128,384]{1,0:T(8,128)S(1)}, u32[]{:S(2)}, u32[]{:S(2)}) collective-permute-start(f32[128,384]{1,0:T(8,128)S(1)} %sum_whole.12.refs_2_.refs_0_), channel_id=1, source_target_pairs={{0,17},{1,18},{2,19},{3,16},{4,23},{5,20},{6,21},{7,22},{8,25},{9,... | collective-permute-start | bytes 589832 | tf_op jit(solution)/shard_map/ppermute | solution.py:478
  46.0 2.3 %collective-permute-start.15 = (f32[192,256]{1,0:T(8,128)S(1)}, f32[192,256]{1,0:T(8,128)S(1)}, u32[]{:S(2)}, u32[]{:S(2)}) collective-permute-start(f32[192,256]{1,0:T(8,128)S(1)} %sum_whole.14.refs_2_.refs_0_), channel_id=1, source_target_pairs={{0,48},{1,113},{2,50},{3,115},{4,116},{5,53},{6,118},{7,55},{8,56}... | collective-permute-start | bytes 589832 | tf_op jit(solution)/shard_map/ppermute | solution.py:478
  50.2 2.2 %collective-permute-start.19 = (f32[128,384]{1,0:T(8,128)S(1)}, f32[128,384]{1,0:T(8,128)S(1)}, u32[]{:S(2)}, u32[]{:S(2)}) collective-permute-start(f32[128,384]{1,0:T(8,128)S(1)} %sum_whole.16.refs_2_.refs_0_), channel_id=1, source_target_pairs={{0,20},{1,29},{2,22},{3,31},{4,24},{5,17},{6,26},{7,19},{8,28},{9,... | collective-permute-start | bytes 589832 | tf_op jit(solution)/shard_map/ppermute | solution.py:478
  52.8 1.8 %collective-permute-done.20.refs_1_ = f32[128,384]{1,0:T(8,128)S(1)} collective-permute-done((f32[128,384]{1,0:T(8,128)S(1)}, f32[128,384]{1,0:T(8,128)S(1)}, u32[]{:S(2)}, u32[]{:S(2)}) %collective-permute-start.20) | collective-permute-done | bytes 196640 | tf_op jit(solution)/shard_map/ppermute | solution.py:478
  54.7 2.2 %collective-permute-done.19.refs_1_ = f32[128,384]{1,0:T(8,128)S(1)} collective-permute-done((f32[128,384]{1,0:T(8,128)S(1)}, f32[128,384]{1,0:T(8,128)S(1)}, u32[]{:S(2)}, u32[]{:S(2)}) %collective-permute-start.19) | collective-permute-done | bytes 196640 | tf_op jit(solution)/shard_map/ppermute | solution.py:478
  56.9 2.1 %collective-permute-start.22 = (f32[128,384]{1,0:T(8,128)S(1)}, f32[128,384]{1,0:T(8,128)S(1)}, u32[]{:S(2)}, u32[]{:S(2)}) collective-permute-start(f32[128,384]{1,0:T(8,128)S(1)} %sum_last.4.refs_2_.refs_0_), channel_id=1, source_target_pairs={{0,48},{1,113},{2,50},{3,115},{4,116},{5,53},{6,118},{7,55},{8,56}... | collective-permute-start | bytes 589832 | tf_op jit(solution)/shard_map/ppermute | solution.py:478
  60.2 1.8 %collective-permute-start.24 = (f32[256,384]{1,0:T(8,128)S(1)}, f32[256,384]{1,0:T(8,128)S(1)}, u32[]{:S(2)}, u32[]{:S(2)}) collective-permute-start(f32[256,384]{1,0:T(8,128)S(1)} %join.3.refs_2_.refs_0_), channel_id=1, source_target_pairs={{0,20},{1,29},{2,22},{3,31},{4,24},{5,17},{6,26},{7,19},{8,28},{9,... | collective-permute-start | bytes 1179656 | tf_op jit(solution)/shard_map/ppermute | solution.py:478
  64.4 2.0 %collective-permute-start.28 = (f32[256,256]{1,0:T(8,128)S(1)}, f32[256,256]{1,0:T(8,128)S(1)}, u32[]{:S(2)}, u32[]{:S(2)}) collective-permute-start(f32[256,256]{1,0:T(8,128)S(1)} %join.5.refs_2_.refs_4_.refs_0_), channel_id=1, source_target_pairs={{0,17},{1,18},{2,19},{3,16},{4,23},{5,20},{6,21},{7,22},{8,25},{9,... | collective-permute-start | bytes 786440 | tf_op jit(solution)/shard_map/ppermute | solution.py:478
  66.4 2.4 %factor_part.7.refs_0_ = f32[128,128]{1,0:T(8,128)S(1)} custom-call(f32[128,128]{1,0:T(8,128)S(1)} %get-tuple-element.48.refs_2_.refs_0_, f32[128,128]{1,0:T(8,128)S(1)} %get-tuple-element.49.refs_1_, f32[256,256]{1,0:T(8,128)S(1)} %join.5.refs_2_.refs_4_.refs_0_), custom_call_target="tpu_custom_call" | custom-call | flops 1000000000 | bytes 262144 | tf_op jit(solution)/shard_map/factor_part/pallas_call | solution.py:294
  68.8 1.4 %apply_first.1 = (f32[128,8192]{1,0:T(8,128)}, f32[512,128]{1,0:T(8,128)}, f32[8,128]{1,0:T(8,128)S(1)}) custom-call(f32[128,128]{1,0:T(8,128)S(1)} %factor_part.7.refs_0_, f32[512,128]{1,0:T(8,128)S(1)} %get-tuple-element.50.refs_1_, f32[256,384]{1,0:T(8,128)S(1)} %join.3.refs_2_.refs_0_, f32[256,384]{1,0:T(8,128)S(1)} %join.4.refs_2_.refs_3_.refs_0_, ...), custom_call_target="tpu_custom_call" | custom-call | flops 1000000000 | bytes 2097152 | tf_op jit(solution)/shard_map/apply_first/pallas_call | solution.py:442
  70.2 1.3 %collective-permute-done.28.refs_0_ = f32[256,256]{1,0:T(8,128)S(1)} collective-permute-done((f32[256,256]{1,0:T(8,128)S(1)}, f32[256,256]{1,0:T(8,128)S(1)}, u32[]{:S(2)}, u32[]{:S(2)}) %collective-permute-start.28) | collective-permute-done | bytes 262176 | tf_op jit(solution)/shard_map/ppermute | solution.py:478
  74.2 1.6 %apply_next.2.refs_4_ = f32[128,8192]{1,0:T(8,128)} custom-call(f32[128,128]{1,0:T(8,128)S(1)} %factor_part.7.refs_0_, f32[256,384]{1,0:T(8,128)S(1)} %pass_on.6.refs_1_, f32[256,384]{1,0:T(8,128)S(1)} %pass_on.7.refs_2_, f32[256,256]{1,0:T(8,128)S(1)} %pass_on.8.refs_3_, ...), custom_call_target="tpu_custom_call", output_to_operand_aliasing={{}: (7, {})} | custom-call | flops 1000000000 | bytes 2097152 | tf_op jit(solution)/shard_map/apply_next/pallas_call | solution.py:464
  (90 shorter events, 22.2 us)
Async XLA Ops:
  12.7 6.4 %collective-permute-start.2 = (f32[576,256]{1,0:T(8,128)S(1)}, f32[576,256]{1,0:T(8,128)S(1)}, u32[]{:S(2)}, u32[]{:S(2)}) collective-permute-start(f32[576,256]{1,0:T(8,128)S(1)} %get-tuple-element.34.refs_3_), channel_id=1, source_target_pairs={{0,16},{1,17},{2,18},{3,19},{4,20},{5,21},{6,22},{7,23},{8,24},{9,... | collective-permute-start | bytes 1769480 | tf_op jit(solution)/shard_map/ppermute | solution.py:478
  13.9 11.1 %collective-permute-start.5 = (f32[256,384]{1,0:T(8,128)S(1)}, f32[256,384]{1,0:T(8,128)S(1)}, u32[]{:S(2)}, u32[]{:S(2)}) collective-permute-start(f32[256,384]{1,0:T(8,128)S(1)} %sum_handed.3.refs_3_.refs_1_), channel_id=1, source_target_pairs={{0,20},{1,29},{2,22},{3,31},{4,24},{5,17},{6,26},{7,19},{8,28},{9,... | collective-permute-start | bytes 1179656 | tf_op jit(solution)/shard_map/ppermute | solution.py:478
  17.1 8.2 %collective-permute-start.4 = (f32[256,384]{1,0:T(8,128)S(1)}, f32[256,384]{1,0:T(8,128)S(1)}, u32[]{:S(2)}, u32[]{:S(2)}) collective-permute-start(f32[256,384]{1,0:T(8,128)S(1)} %sum_handed.4.refs_4_.refs_1_), channel_id=1, source_target_pairs={{0,112},{1,49},{2,114},{3,51},{4,52},{5,117},{6,54},{7,119},{8,120... | collective-permute-start | bytes 1179656 | tf_op jit(solution)/shard_map/ppermute | solution.py:478
  19.2 9.1 %collective-permute-start.3 = (f32[320,256]{1,0:T(8,128)S(1)}, f32[320,256]{1,0:T(8,128)S(1)}, u32[]{:S(2)}, u32[]{:S(2)}) collective-permute-start(f32[320,256]{1,0:T(8,128)S(1)} %sum_handed.5.refs_3_.refs_1_), channel_id=1, source_target_pairs={{0,17},{1,18},{2,19},{3,16},{4,23},{5,20},{6,21},{7,22},{8,25},{9,... | collective-permute-start | bytes 983048 | tf_op jit(solution)/shard_map/ppermute | solution.py:478
  25.4 7.1 %collective-permute-start.7 = (f32[128,384]{1,0:T(8,128)S(1)}, f32[128,384]{1,0:T(8,128)S(1)}, u32[]{:S(2)}, u32[]{:S(2)}) collective-permute-start(f32[128,384]{1,0:T(8,128)S(1)} %get-tuple-element.40.refs_1_), channel_id=1, source_target_pairs={{0,48},{1,113},{2,50},{3,115},{4,116},{5,53},{6,118},{7,55},{8,56}... | collective-permute-start | bytes 589832 | tf_op jit(solution)/shard_map/ppermute | solution.py:478
  28.3 5.5 %collective-permute-start.6 = (f32[192,256]{1,0:T(8,128)S(1)}, f32[192,256]{1,0:T(8,128)S(1)}, u32[]{:S(2)}, u32[]{:S(2)}) collective-permute-start(f32[192,256]{1,0:T(8,128)S(1)} %get-tuple-element.39.refs_1_), channel_id=1, source_target_pairs={{0,19},{1,16},{2,17},{3,18},{4,21},{5,22},{6,23},{7,20},{8,27},{9,... | collective-permute-start | bytes 589832 | tf_op jit(solution)/shard_map/ppermute | solution.py:478
  30.2 6.7 %collective-permute-start.11 = (f32[128,384]{1,0:T(8,128)S(1)}, f32[128,384]{1,0:T(8,128)S(1)}, u32[]{:S(2)}, u32[]{:S(2)}) collective-permute-start(f32[128,384]{1,0:T(8,128)S(1)} %sum_quarter.3.refs_3_.refs_0_), channel_id=1, source_target_pairs={{0,48},{1,113},{2,50},{3,115},{4,116},{5,53},{6,118},{7,55},{8,56}... | collective-permute-start | bytes 589832 | tf_op jit(solution)/shard_map/ppermute | solution.py:478
  32.5 5.5 %collective-permute-start.10 = (f32[128,384]{1,0:T(8,128)S(1)}, f32[128,384]{1,0:T(8,128)S(1)}, u32[]{:S(2)}, u32[]{:S(2)}) collective-permute-start(f32[128,384]{1,0:T(8,128)S(1)} %sum_quarter.4.refs_3_.refs_0_), channel_id=1, source_target_pairs={{0,19},{1,16},{2,17},{3,18},{4,21},{5,22},{6,23},{7,20},{8,27},{9,... | collective-permute-start | bytes 589832 | tf_op jit(solution)/shard_map/ppermute | solution.py:478
  33.8 6.7 %collective-permute-start.9 = (f32[192,256]{1,0:T(8,128)S(1)}, f32[192,256]{1,0:T(8,128)S(1)}, u32[]{:S(2)}, u32[]{:S(2)}) collective-permute-start(f32[192,256]{1,0:T(8,128)S(1)} %sum_quarter.5.refs_2_.refs_0_), channel_id=1, source_target_pairs={{0,20},{1,29},{2,22},{3,31},{4,24},{5,17},{6,26},{7,19},{8,28},{9,... | collective-permute-start | bytes 589832 | tf_op jit(solution)/shard_map/ppermute | solution.py:478
  36.9 5.5 %collective-permute-start.14 = (f32[128,384]{1,0:T(8,128)S(1)}, f32[128,384]{1,0:T(8,128)S(1)}, u32[]{:S(2)}, u32[]{:S(2)}) collective-permute-start(f32[128,384]{1,0:T(8,128)S(1)} %sum_whole.9.refs_2_.refs_0_), channel_id=1, source_target_pairs={{0,112},{1,49},{2,114},{3,51},{4,52},{5,117},{6,54},{7,119},{8,120... | collective-permute-start | bytes 589832 | tf_op jit(solution)/shard_map/ppermute | solution.py:478
  38.0 6.7 %collective-permute-start.13 = (f32[128,384]{1,0:T(8,128)S(1)}, f32[128,384]{1,0:T(8,128)S(1)}, u32[]{:S(2)}, u32[]{:S(2)}) collective-permute-start(f32[128,384]{1,0:T(8,128)S(1)} %sum_whole.10.refs_2_.refs_0_), channel_id=1, source_target_pairs={{0,17},{1,18},{2,19},{3,16},{4,23},{5,20},{6,21},{7,22},{8,25},{9,... | collective-permute-start | bytes 589832 | tf_op jit(solution)/shard_map/ppermute | solution.py:478
  40.5 5.5 %collective-permute-start.12 = (f32[192,256]{1,0:T(8,128)S(1)}, f32[192,256]{1,0:T(8,128)S(1)}, u32[]{:S(2)}, u32[]{:S(2)}) collective-permute-start(f32[192,256]{1,0:T(8,128)S(1)} %sum_whole.11.refs_2_.refs_0_), channel_id=1, source_target_pairs={{0,28},{1,21},{2,30},{3,23},{4,16},{5,25},{6,18},{7,27},{8,20},{9,... | collective-permute-start | bytes 589832 | tf_op jit(solution)/shard_map/ppermute | solution.py:478
  42.4 6.7 %collective-permute-start.17 = (f32[128,384]{1,0:T(8,128)S(1)}, f32[128,384]{1,0:T(8,128)S(1)}, u32[]{:S(2)}, u32[]{:S(2)}) collective-permute-start(f32[128,384]{1,0:T(8,128)S(1)} %sum_whole.12.refs_2_.refs_0_), channel_id=1, source_target_pairs={{0,17},{1,18},{2,19},{3,16},{4,23},{5,20},{6,21},{7,22},{8,25},{9,... | collective-permute-start | bytes 589832 | tf_op jit(solution)/shard_map/ppermute | solution.py:478
  44.7 5.5 %collective-permute-start.16 = (f32[128,384]{1,0:T(8,128)S(1)}, f32[128,384]{1,0:T(8,128)S(1)}, u32[]{:S(2)}, u32[]{:S(2)}) collective-permute-start(f32[128,384]{1,0:T(8,128)S(1)} %sum_whole.13.refs_2_.refs_0_), channel_id=1, source_target_pairs={{0,28},{1,21},{2,30},{3,23},{4,16},{5,25},{6,18},{7,27},{8,20},{9,... | collective-permute-start | bytes 589832 | tf_op jit(solution)/shard_map/ppermute | solution.py:478
  46.0 6.7 %collective-permute-start.15 = (f32[192,256]{1,0:T(8,128)S(1)}, f32[192,256]{1,0:T(8,128)S(1)}, u32[]{:S(2)}, u32[]{:S(2)}) collective-permute-start(f32[192,256]{1,0:T(8,128)S(1)} %sum_whole.14.refs_2_.refs_0_), channel_id=1, source_target_pairs={{0,48},{1,113},{2,50},{3,115},{4,116},{5,53},{6,118},{7,55},{8,56}... | collective-permute-start | bytes 589832 | tf_op jit(solution)/shard_map/ppermute | solution.py:478
  49.1 5.4 %collective-permute-start.20 = (f32[128,384]{1,0:T(8,128)S(1)}, f32[128,384]{1,0:T(8,128)S(1)}, u32[]{:S(2)}, u32[]{:S(2)}) collective-permute-start(f32[128,384]{1,0:T(8,128)S(1)} %sum_whole.15.refs_2_.refs_0_), channel_id=1, source_target_pairs={{0,19},{1,16},{2,17},{3,18},{4,21},{5,22},{6,23},{7,20},{8,27},{9,... | collective-permute-start | bytes 589832 | tf_op jit(solution)/shard_map/ppermute | solution.py:478
  50.2 6.7 %collective-permute-start.19 = (f32[128,384]{1,0:T(8,128)S(1)}, f32[128,384]{1,0:T(8,128)S(1)}, u32[]{:S(2)}, u32[]{:S(2)}) collective-permute-start(f32[128,384]{1,0:T(8,128)S(1)} %sum_whole.16.refs_2_.refs_0_), channel_id=1, source_target_pairs={{0,20},{1,29},{2,22},{3,31},{4,24},{5,17},{6,26},{7,19},{8,28},{9,... | collective-permute-start | bytes 589832 | tf_op jit(solution)/shard_map/ppermute | solution.py:478
  52.7 6.3 %collective-permute-start.18 = (f32[192,256]{1,0:T(8,128)S(1)}, f32[192,256]{1,0:T(8,128)S(1)}, u32[]{:S(2)}, u32[]{:S(2)}) collective-permute-start(f32[192,256]{1,0:T(8,128)S(1)} %sum_whole.17.refs_2_.refs_0_), channel_id=1, source_target_pairs={{0,112},{1,49},{2,114},{3,51},{4,52},{5,117},{6,54},{7,119},{8,120... | collective-permute-start | bytes 589832 | tf_op jit(solution)/shard_map/ppermute | solution.py:478
  54.6 5.6 %collective-permute-start.21 = (f32[128,384]{1,0:T(8,128)S(1)}, f32[128,384]{1,0:T(8,128)S(1)}, u32[]{:S(2)}, u32[]{:S(2)}) collective-permute-start(f32[128,384]{1,0:T(8,128)S(1)} %sum_last.3.refs_2_.refs_0_), channel_id=1, source_target_pairs={{0,28},{1,21},{2,30},{3,23},{4,16},{5,25},{6,18},{7,27},{8,20},{9,... | collective-permute-start | bytes 589832 | tf_op jit(solution)/shard_map/ppermute | solution.py:478
  56.9 6.7 %collective-permute-start.22 = (f32[128,384]{1,0:T(8,128)S(1)}, f32[128,384]{1,0:T(8,128)S(1)}, u32[]{:S(2)}, u32[]{:S(2)}) collective-permute-start(f32[128,384]{1,0:T(8,128)S(1)} %sum_last.4.refs_2_.refs_0_), channel_id=1, source_target_pairs={{0,48},{1,113},{2,50},{3,115},{4,116},{5,53},{6,118},{7,55},{8,56}... | collective-permute-start | bytes 589832 | tf_op jit(solution)/shard_map/ppermute | solution.py:478
  59.1 5.3 %collective-permute-start.23 = (f32[128,256]{1,0:T(8,128)S(1)}, f32[128,256]{1,0:T(8,128)S(1)}, u32[]{:S(2)}, u32[]{:S(2)}) collective-permute-start(f32[128,256]{1,0:T(8,128)S(1)} %get-tuple-element.43.refs_1_.refs_0_), channel_id=1, source_target_pairs={{0,19},{1,16},{2,17},{3,18},{4,21},{5,22},{6,23},{7,20},{8,27},{9,... | collective-permute-start | bytes 393224 | tf_op jit(solution)/shard_map/ppermute | solution.py:478
  60.2 11.3 %collective-permute-start.24 = (f32[256,384]{1,0:T(8,128)S(1)}, f32[256,384]{1,0:T(8,128)S(1)}, u32[]{:S(2)}, u32[]{:S(2)}) collective-permute-start(f32[256,384]{1,0:T(8,128)S(1)} %join.3.refs_2_.refs_0_), channel_id=1, source_target_pairs={{0,20},{1,29},{2,22},{3,31},{4,24},{5,17},{6,26},{7,19},{8,28},{9,... | collective-permute-start | bytes 1179656 | tf_op jit(solution)/shard_map/ppermute | solution.py:478
  63.6 7.9 %collective-permute-start.26 = (f32[256,384]{1,0:T(8,128)S(1)}, f32[256,384]{1,0:T(8,128)S(1)}, u32[]{:S(2)}, u32[]{:S(2)}) collective-permute-start(f32[256,384]{1,0:T(8,128)S(1)} %join.4.refs_2_.refs_3_.refs_0_), channel_id=1, source_target_pairs={{0,112},{1,49},{2,114},{3,51},{4,52},{5,117},{6,54},{7,119},{8,120... | collective-permute-start | bytes 1179656 | tf_op jit(solution)/shard_map/ppermute | solution.py:478
  64.4 7.1 %collective-permute-start.28 = (f32[256,256]{1,0:T(8,128)S(1)}, f32[256,256]{1,0:T(8,128)S(1)}, u32[]{:S(2)}, u32[]{:S(2)}) collective-permute-start(f32[256,256]{1,0:T(8,128)S(1)} %join.5.refs_2_.refs_4_.refs_0_), channel_id=1, source_target_pairs={{0,17},{1,18},{2,19},{3,16},{4,23},{5,20},{6,21},{7,22},{8,25},{9,... | collective-permute-start | bytes 786440 | tf_op jit(solution)/shard_map/ppermute | solution.py:478
  (9 other events, 28.8 us)

commit v6 on v5

--- a/solution.py
+++ b/solution.py
@@ -511,11 +511,11 @@
         after = states[chain]
         gram = rest[0] if rest else gram
     state = [gram]
-    for chain, panels in zip(turns, ((0, 2), (2, 4), (4, 6))):
+    for chain, panels in zip(turns, ((0, 2), (2, 4), (4, 5))):
         state = factor_part(state, panels, after)
         got = send(states[chain], ring_pairs(chain, 1, FLIP[chain]))
         near[chain] = after = join(states[chain], got, state[0])
-    (inverse,) = factor_part(state, (6, 16), after)
+    (inverse,) = factor_part(state, (5, 16), after)
     scale = math.sqrt(total_rows)
     out, basis, mark = apply_first(inverse, near, [(a, 0, 0) for a in range(3)], sampled, scale)
     near_other = [send(pass_on(part, mark), CORE_PAIRS) for part in near]

time: 77.4 us -> 77.3 us (level)
  no operation moved by 1% of the time
where the time goes in v6:
time: 77.3 us; the launch traced here: 77.1 us
  starting transfers between devices  35.3 us (46%)
  Pallas kernels  23 us (30%)
  waiting for transfers between devices  17.7 us (23%)
  between operations  1.2 us (2%)
    ppermute x33, starting transfers between devices, send(): return lax.ppermute(value, AXES, pairs)  35.3 us
    ppermute x33, waiting for transfers between devices, send(): return lax.ppermute(value, AXES, pairs)  17.7 us
    pallas_call x1, Pallas kernels, sample(): pl.pallas_call(sample_kernel, in_specs=[HBM, HBM], out_specs=[VMEM] * 7,...  9.2 us
    pallas_call x31, Pallas kernels, call_in_turn(): pl.pallas_call(kernel, in_specs=[VMEM] * len(args) + [any_space] * len(ex...  5.14 us
    pallas_call x6, Pallas kernels, own_part(): pl.pallas_call(lambda *refs: own_kernel(chain, slots, *refs), in_specs=[V...  3.11 us
    pallas_call x2, Pallas kernels, apply_next(): pl.pallas_call(lambda *refs: apply_next_kernel(pieces, *refs), in_specs=[...  2.87 us
  transfers between devices with their start and end apart: 33, of which 19 were waited for; matrix products, arithmetic and copies ran while one was open for 0% of the time, Pallas kernels for 16%

profile of v6, /device:TPU:1, one launch (start us, length us, event | category | flops | bytes accessed | tf_op | source)
XLA Modules:
  0.0 77.1 jit_solution(7672416759775697847)
XLA Ops:
  0.6 9.2 %sample.1 = (f32[512,128]{1,0:T(8,128)S(1)}, bf16[256,512]{1,0:T(8,128)(2,1)S(1)}, bf16[4,512,1024]{2,1,0:T(8,128)(2,1)S(1)}, bf16[4,512,1024]{2,1,0:T(8,128)(2,...) custom-call(f32[512,8192]{1,0:T(8,128)} %slab.1, f32[8192,128]{1,0:T(8,128)} %sketch.1), custom_call_target="tpu_custom_call" | custom-call | flops 8000000000 | bytes 22020096 | tf_op jit(solution)/shard_map/sample/pallas_call | solution.py:148
  9.8 1.5 %collective-permute-start = (f32[512,384]{1,0:T(8,128)S(1)}, f32[512,384]{1,0:T(8,128)S(1)}, u32[]{:S(2)}, u32[]{:S(2)}) collective-permute-start(f32[512,384]{1,0:T(8,128)S(1)} %get-tuple-element.33.after), channel_id=1, source_target_pairs={{0,16},{1,17},{2,18},{3,19},{4,20},{5,21},{6,22},{7,23},{8,24},{9,... | collective-permute-start | bytes 2359304 | tf_op jit(solution)/shard_map/ppermute | solution.py:478
  11.3 1.3 %rest_to_send.1 = (f32[512,384]{1,0:T(8,128)S(1)}, f32[576,256]{1,0:T(8,128)S(1)}) custom-call(bf16[256,512]{1,0:T(8,128)(2,1)S(1)} %get-tuple-element.28.left.refs_0_, bf16[4,512,1024]{2,1,0:T(8,128)(2,1)S(1)} %get-tuple-element.31.high, bf16[4,512,1024]{2,1,0:T(8,128)(2,1)S(1)} %get-tuple-element.32.low, f32[512,384]{1,0:T(8,128)S(1)} %get-tuple-element.33.after), custom_call_target="tpu_custom_call" | custom-call | flops 1500000000 | bytes 1048576 | tf_op jit(solution)/shard_map/rest_to_send/pallas_call | solution.py:181
  13.9 2.6 %collective-permute-start.5 = (f32[256,384]{1,0:T(8,128)S(1)}, f32[256,384]{1,0:T(8,128)S(1)}, u32[]{:S(2)}, u32[]{:S(2)}) collective-permute-start(f32[256,384]{1,0:T(8,128)S(1)} %sum_handed.3.refs_3_.refs_1_), channel_id=1, source_target_pairs={{0,20},{1,29},{2,22},{3,31},{4,24},{5,17},{6,26},{7,19},{8,28},{9,... | collective-permute-start | bytes 1179656 | tf_op jit(solution)/shard_map/ppermute | solution.py:478
  17.1 1.7 %collective-permute-start.4 = (f32[256,384]{1,0:T(8,128)S(1)}, f32[256,384]{1,0:T(8,128)S(1)}, u32[]{:S(2)}, u32[]{:S(2)}) collective-permute-start(f32[256,384]{1,0:T(8,128)S(1)} %sum_handed.4.refs_4_.refs_1_), channel_id=1, source_target_pairs={{0,112},{1,49},{2,114},{3,51},{4,52},{5,117},{6,54},{7,119},{8,120... | collective-permute-start | bytes 1179656 | tf_op jit(solution)/shard_map/ppermute | solution.py:478
  19.2 4.0 %collective-permute-start.3 = (f32[320,256]{1,0:T(8,128)S(1)}, f32[320,256]{1,0:T(8,128)S(1)}, u32[]{:S(2)}, u32[]{:S(2)}) collective-permute-start(f32[320,256]{1,0:T(8,128)S(1)} %sum_handed.5.refs_3_.refs_1_), channel_id=1, source_target_pairs={{0,17},{1,18},{2,19},{3,16},{4,23},{5,20},{6,21},{7,22},{8,25},{9,... | collective-permute-start | bytes 983048 | tf_op jit(solution)/shard_map/ppermute | solution.py:478
  25.4 2.2 %collective-permute-start.7 = (f32[128,384]{1,0:T(8,128)S(1)}, f32[128,384]{1,0:T(8,128)S(1)}, u32[]{:S(2)}, u32[]{:S(2)}) collective-permute-start(f32[128,384]{1,0:T(8,128)S(1)} %get-tuple-element.40.refs_1_), channel_id=1, source_target_pairs={{0,48},{1,113},{2,50},{3,115},{4,116},{5,53},{6,118},{7,55},{8,56}... | collective-permute-start | bytes 589832 | tf_op jit(solution)/shard_map/ppermute | solution.py:478
  30.2 2.3 %collective-permute-start.11 = (f32[128,384]{1,0:T(8,128)S(1)}, f32[128,384]{1,0:T(8,128)S(1)}, u32[]{:S(2)}, u32[]{:S(2)}) collective-permute-start(f32[128,384]{1,0:T(8,128)S(1)} %sum_quarter.3.refs_3_.refs_0_), channel_id=1, source_target_pairs={{0,48},{1,113},{2,50},{3,115},{4,116},{5,53},{6,118},{7,55},{8,56}... | collective-permute-start | bytes 589832 | tf_op jit(solution)/shard_map/ppermute | solution.py:478
  33.8 1.3 %collective-permute-start.9 = (f32[192,256]{1,0:T(8,128)S(1)}, f32[192,256]{1,0:T(8,128)S(1)}, u32[]{:S(2)}, u32[]{:S(2)}) collective-permute-start(f32[192,256]{1,0:T(8,128)S(1)} %sum_quarter.5.refs_2_.refs_0_), channel_id=1, source_target_pairs={{0,20},{1,29},{2,22},{3,31},{4,24},{5,17},{6,26},{7,19},{8,28},{9,... | collective-permute-start | bytes 589832 | tf_op jit(solution)/shard_map/ppermute | solution.py:478
  35.1 1.8 %collective-permute-done.11.refs_1_ = f32[128,384]{1,0:T(8,128)S(1)} collective-permute-done((f32[128,384]{1,0:T(8,128)S(1)}, f32[128,384]{1,0:T(8,128)S(1)}, u32[]{:S(2)}, u32[]{:S(2)}) %collective-permute-start.11) | collective-permute-done | bytes 196640 | tf_op jit(solution)/shard_map/ppermute | solution.py:478
  38.0 2.4 %collective-permute-start.13 = (f32[128,384]{1,0:T(8,128)S(1)}, f32[128,384]{1,0:T(8,128)S(1)}, u32[]{:S(2)}, u32[]{:S(2)}) collective-permute-start(f32[128,384]{1,0:T(8,128)S(1)} %sum_whole.10.refs_2_.refs_0_), channel_id=1, source_target_pairs={{0,17},{1,18},{2,19},{3,16},{4,23},{5,20},{6,21},{7,22},{8,25},{9,... | collective-permute-start | bytes 589832 | tf_op jit(solution)/shard_map/ppermute | solution.py:478
  41.1 1.3 %collective-permute-done.14.refs_1_ = f32[128,384]{1,0:T(8,128)S(1)} collective-permute-done((f32[128,384]{1,0:T(8,128)S(1)}, f32[128,384]{1,0:T(8,128)S(1)}, u32[]{:S(2)}, u32[]{:S(2)}) %collective-permute-start.14) | collective-permute-done | bytes 196640 | tf_op jit(solution)/shard_map/ppermute | solution.py:478
  42.4 1.4 %collective-permute-start.17 = (f32[128,384]{1,0:T(8,128)S(1)}, f32[128,384]{1,0:T(8,128)S(1)}, u32[]{:S(2)}, u32[]{:S(2)}) collective-permute-start(f32[128,384]{1,0:T(8,128)S(1)} %sum_whole.12.refs_2_.refs_0_), channel_id=1, source_target_pairs={{0,17},{1,18},{2,19},{3,16},{4,23},{5,20},{6,21},{7,22},{8,25},{9,... | collective-permute-start | bytes 589832 | tf_op jit(solution)/shard_map/ppermute | solution.py:478
  46.0 2.3 %collective-permute-start.15 = (f32[192,256]{1,0:T(8,128)S(1)}, f32[192,256]{1,0:T(8,128)S(1)}, u32[]{:S(2)}, u32[]{:S(2)}) collective-permute-start(f32[192,256]{1,0:T(8,128)S(1)} %sum_whole.14.refs_2_.refs_0_), channel_id=1, source_target_pairs={{0,48},{1,113},{2,50},{3,115},{4,116},{5,53},{6,118},{7,55},{8,56}... | collective-permute-start | bytes 589832 | tf_op jit(solution)/shard_map/ppermute | solution.py:478
  50.2 2.2 %collective-permute-start.19 = (f32[128,384]{1,0:T(8,128)S(1)}, f32[128,384]{1,0:T(8,128)S(1)}, u32[]{:S(2)}, u32[]{:S(2)}) collective-permute-start(f32[128,384]{1,0:T(8,128)S(1)} %sum_whole.16.refs_2_.refs_0_), channel_id=1, source_target_pairs={{0,20},{1,29},{2,22},{3,31},{4,24},{5,17},{6,26},{7,19},{8,28},{9,... | collective-permute-start | bytes 589832 | tf_op jit(solution)/shard_map/ppermute | solution.py:478
  52.8 1.8 %collective-permute-done.20.refs_1_ = f32[128,384]{1,0:T(8,128)S(1)} collective-permute-done((f32[128,384]{1,0:T(8,128)S(1)}, f32[128,384]{1,0:T(8,128)S(1)}, u32[]{:S(2)}, u32[]{:S(2)}) %collective-permute-start.20) | collective-permute-done | bytes 196640 | tf_op jit(solution)/shard_map/ppermute | solution.py:478
  54.7 2.2 %collective-permute-done.19.refs_1_ = f32[128,384]{1,0:T(8,128)S(1)} collective-permute-done((f32[128,384]{1,0:T(8,128)S(1)}, f32[128,384]{1,0:T(8,128)S(1)}, u32[]{:S(2)}, u32[]{:S(2)}) %collective-permute-start.19) | collective-permute-done | bytes 196640 | tf_op jit(solution)/shard_map/ppermute | solution.py:478
  56.9 2.1 %collective-permute-start.22 = (f32[128,384]{1,0:T(8,128)S(1)}, f32[128,384]{1,0:T(8,128)S(1)}, u32[]{:S(2)}, u32[]{:S(2)}) collective-permute-start(f32[128,384]{1,0:T(8,128)S(1)} %sum_last.4.refs_2_.refs_0_), channel_id=1, source_target_pairs={{0,48},{1,113},{2,50},{3,115},{4,116},{5,53},{6,118},{7,55},{8,56}... | collective-permute-start | bytes 589832 | tf_op jit(solution)/shard_map/ppermute | solution.py:478
  60.2 1.8 %collective-permute-start.24 = (f32[256,384]{1,0:T(8,128)S(1)}, f32[256,384]{1,0:T(8,128)S(1)}, u32[]{:S(2)}, u32[]{:S(2)}) collective-permute-start(f32[256,384]{1,0:T(8,128)S(1)} %join.3.refs_2_.refs_0_), channel_id=1, source_target_pairs={{0,20},{1,29},{2,22},{3,31},{4,24},{5,17},{6,26},{7,19},{8,28},{9,... | collective-permute-start | bytes 1179656 | tf_op jit(solution)/shard_map/ppermute | solution.py:478
  64.1 2.1 %collective-permute-start.28 = (f32[256,256]{1,0:T(8,128)S(1)}, f32[256,256]{1,0:T(8,128)S(1)}, u32[]{:S(2)}, u32[]{:S(2)}) collective-permute-start(f32[256,256]{1,0:T(8,128)S(1)} %join.5.refs_2_.refs_4_.refs_0_), channel_id=1, source_target_pairs={{0,17},{1,18},{2,19},{3,16},{4,23},{5,20},{6,21},{7,22},{8,25},{9,... | collective-permute-start | bytes 786440 | tf_op jit(solution)/shard_map/ppermute | solution.py:478
  66.2 2.6 %factor_part.7.refs_0_ = f32[128,128]{1,0:T(8,128)S(1)} custom-call(f32[128,128]{1,0:T(8,128)S(1)} %get-tuple-element.48.refs_2_.refs_0_, f32[128,128]{1,0:T(8,128)S(1)} %get-tuple-element.49.refs_1_, f32[256,256]{1,0:T(8,128)S(1)} %join.5.refs_2_.refs_4_.refs_0_), custom_call_target="tpu_custom_call" | custom-call | flops 1000000000 | bytes 262144 | tf_op jit(solution)/shard_map/factor_part/pallas_call | solution.py:294
  68.9 1.4 %apply_first.1 = (f32[128,8192]{1,0:T(8,128)}, f32[512,128]{1,0:T(8,128)}, f32[8,128]{1,0:T(8,128)S(1)}) custom-call(f32[128,128]{1,0:T(8,128)S(1)} %factor_part.7.refs_0_, f32[512,128]{1,0:T(8,128)S(1)} %get-tuple-element.50.refs_1_, f32[256,384]{1,0:T(8,128)S(1)} %join.3.refs_2_.refs_0_, f32[256,384]{1,0:T(8,128)S(1)} %join.4.refs_2_.refs_3_.refs_0_, ...), custom_call_target="tpu_custom_call" | custom-call | flops 1000000000 | bytes 2097152 | tf_op jit(solution)/shard_map/apply_first/pallas_call | solution.py:442
  74.1 1.6 %apply_next.2.refs_4_ = f32[128,8192]{1,0:T(8,128)} custom-call(f32[128,128]{1,0:T(8,128)S(1)} %factor_part.7.refs_0_, f32[256,384]{1,0:T(8,128)S(1)} %pass_on.6.refs_1_, f32[256,384]{1,0:T(8,128)S(1)} %pass_on.7.refs_2_, f32[256,256]{1,0:T(8,128)S(1)} %pass_on.8.refs_3_, ...), custom_call_target="tpu_custom_call", output_to_operand_aliasing={{}: (7, {})} | custom-call | flops 1000000000 | bytes 2097152 | tf_op jit(solution)/shard_map/apply_next/pallas_call | solution.py:464
  75.7 1.2 %apply_next.3 = f32[128,8192]{1,0:T(8,128)} custom-call(f32[128,128]{1,0:T(8,128)S(1)} %factor_part.7.refs_0_, f32[256,384]{1,0:T(8,128)S(1)} %collective-permute-done.25.refs_1_, f32[256,384]{1,0:T(8,128)S(1)} %collective-permute-done.27.refs_2_, f32[256,256]{1,0:T(8,128)S(1)} %collective-permute-done.29.refs_3_, ...), custom_call_target="tpu_custom_call", output_to_operand_aliasing={{}: (4, {})} | custom-call | flops 1000000000 | bytes 2097152 | tf_op jit(solution)/shard_map/apply_next/pallas_call | solution.py:464
  (90 shorter events, 21.7 us)
Async XLA Ops:
  12.7 6.4 %collective-permute-start.2 = (f32[576,256]{1,0:T(8,128)S(1)}, f32[576,256]{1,0:T(8,128)S(1)}, u32[]{:S(2)}, u32[]{:S(2)}) collective-permute-start(f32[576,256]{1,0:T(8,128)S(1)} %get-tuple-element.34.refs_3_), channel_id=1, source_target_pairs={{0,16},{1,17},{2,18},{3,19},{4,20},{5,21},{6,22},{7,23},{8,24},{9,... | collective-permute-start | bytes 1769480 | tf_op jit(solution)/shard_map/ppermute | solution.py:478
  13.9 11.1 %collective-permute-start.5 = (f32[256,384]{1,0:T(8,128)S(1)}, f32[256,384]{1,0:T(8,128)S(1)}, u32[]{:S(2)}, u32[]{:S(2)}) collective-permute-start(f32[256,384]{1,0:T(8,128)S(1)} %sum_handed.3.refs_3_.refs_1_), channel_id=1, source_target_pairs={{0,20},{1,29},{2,22},{3,31},{4,24},{5,17},{6,26},{7,19},{8,28},{9,... | collective-permute-start | bytes 1179656 | tf_op jit(solution)/shard_map/ppermute | solution.py:478
  17.1 8.2 %collective-permute-start.4 = (f32[256,384]{1,0:T(8,128)S(1)}, f32[256,384]{1,0:T(8,128)S(1)}, u32[]{:S(2)}, u32[]{:S(2)}) collective-permute-start(f32[256,384]{1,0:T(8,128)S(1)} %sum_handed.4.refs_4_.refs_1_), channel_id=1, source_target_pairs={{0,112},{1,49},{2,114},{3,51},{4,52},{5,117},{6,54},{7,119},{8,120... | collective-permute-start | bytes 1179656 | tf_op jit(solution)/shard_map/ppermute | solution.py:478
  19.2 9.1 %collective-permute-start.3 = (f32[320,256]{1,0:T(8,128)S(1)}, f32[320,256]{1,0:T(8,128)S(1)}, u32[]{:S(2)}, u32[]{:S(2)}) collective-permute-start(f32[320,256]{1,0:T(8,128)S(1)} %sum_handed.5.refs_3_.refs_1_), channel_id=1, source_target_pairs={{0,17},{1,18},{2,19},{3,16},{4,23},{5,20},{6,21},{7,22},{8,25},{9,... | collective-permute-start | bytes 983048 | tf_op jit(solution)/shard_map/ppermute | solution.py:478
  25.0 5.2 %collective-permute-start.8 = (f32[128,384]{1,0:T(8,128)S(1)}, f32[128,384]{1,0:T(8,128)S(1)}, u32[]{:S(2)}, u32[]{:S(2)}) collective-permute-start(f32[128,384]{1,0:T(8,128)S(1)} %get-tuple-element.41.refs_1_), channel_id=1, source_target_pairs={{0,28},{1,21},{2,30},{3,23},{4,16},{5,25},{6,18},{7,27},{8,20},{9,... | collective-permute-start | bytes 589832 | tf_op jit(solution)/shard_map/ppermute | solution.py:478
  25.4 7.1 %collective-permute-start.7 = (f32[128,384]{1,0:T(8,128)S(1)}, f32[128,384]{1,0:T(8,128)S(1)}, u32[]{:S(2)}, u32[]{:S(2)}) collective-permute-start(f32[128,384]{1,0:T(8,128)S(1)} %get-tuple-element.40.refs_1_), channel_id=1, source_target_pairs={{0,48},{1,113},{2,50},{3,115},{4,116},{5,53},{6,118},{7,55},{8,56}... | collective-permute-start | bytes 589832 | tf_op jit(solution)/shard_map/ppermute | solution.py:478
  28.3 5.5 %collective-permute-start.6 = (f32[192,256]{1,0:T(8,128)S(1)}, f32[192,256]{1,0:T(8,128)S(1)}, u32[]{:S(2)}, u32[]{:S(2)}) collective-permute-start(f32[192,256]{1,0:T(8,128)S(1)} %get-tuple-element.39.refs_1_), channel_id=1, source_target_pairs={{0,19},{1,16},{2,17},{3,18},{4,21},{5,22},{6,23},{7,20},{8,27},{9,... | collective-permute-start | bytes 589832 | tf_op jit(solution)/shard_map/ppermute | solution.py:478
  30.2 6.7 %collective-permute-start.11 = (f32[128,384]{1,0:T(8,128)S(1)}, f32[128,384]{1,0:T(8,128)S(1)}, u32[]{:S(2)}, u32[]{:S(2)}) collective-permute-start(f32[128,384]{1,0:T(8,128)S(1)} %sum_quarter.3.refs_3_.refs_0_), channel_id=1, source_target_pairs={{0,48},{1,113},{2,50},{3,115},{4,116},{5,53},{6,118},{7,55},{8,56}... | collective-permute-start | bytes 589832 | tf_op jit(solution)/shard_map/ppermute | solution.py:478
  32.5 5.5 %collective-permute-start.10 = (f32[128,384]{1,0:T(8,128)S(1)}, f32[128,384]{1,0:T(8,128)S(1)}, u32[]{:S(2)}, u32[]{:S(2)}) collective-permute-start(f32[128,384]{1,0:T(8,128)S(1)} %sum_quarter.4.refs_3_.refs_0_), channel_id=1, source_target_pairs={{0,19},{1,16},{2,17},{3,18},{4,21},{5,22},{6,23},{7,20},{8,27},{9,... | collective-permute-start | bytes 589832 | tf_op jit(solution)/shard_map/ppermute | solution.py:478
  33.8 6.7 %collective-permute-start.9 = (f32[192,256]{1,0:T(8,128)S(1)}, f32[192,256]{1,0:T(8,128)S(1)}, u32[]{:S(2)}, u32[]{:S(2)}) collective-permute-start(f32[192,256]{1,0:T(8,128)S(1)} %sum_quarter.5.refs_2_.refs_0_), channel_id=1, source_target_pairs={{0,20},{1,29},{2,22},{3,31},{4,24},{5,17},{6,26},{7,19},{8,28},{9,... | collective-permute-start | bytes 589832 | tf_op jit(solution)/shard_map/ppermute | solution.py:478
  36.9 5.5 %collective-permute-start.14 = (f32[128,384]{1,0:T(8,128)S(1)}, f32[128,384]{1,0:T(8,128)S(1)}, u32[]{:S(2)}, u32[]{:S(2)}) collective-permute-start(f32[128,384]{1,0:T(8,128)S(1)} %sum_whole.9.refs_2_.refs_0_), channel_id=1, source_target_pairs={{0,112},{1,49},{2,114},{3,51},{4,52},{5,117},{6,54},{7,119},{8,120... | collective-permute-start | bytes 589832 | tf_op jit(solution)/shard_map/ppermute | solution.py:478
  38.0 6.7 %collective-permute-start.13 = (f32[128,384]{1,0:T(8,128)S(1)}, f32[128,384]{1,0:T(8,128)S(1)}, u32[]{:S(2)}, u32[]{:S(2)}) collective-permute-start(f32[128,384]{1,0:T(8,128)S(1)} %sum_whole.10.refs_2_.refs_0_), channel_id=1, source_target_pairs={{0,17},{1,18},{2,19},{3,16},{4,23},{5,20},{6,21},{7,22},{8,25},{9,... | collective-permute-start | bytes 589832 | tf_op jit(solution)/shard_map/ppermute | solution.py:478
  40.5 5.5 %collective-permute-start.12 = (f32[192,256]{1,0:T(8,128)S(1)}, f32[192,256]{1,0:T(8,128)S(1)}, u32[]{:S(2)}, u32[]{:S(2)}) collective-permute-start(f32[192,256]{1,0:T(8,128)S(1)} %sum_whole.11.refs_2_.refs_0_), channel_id=1, source_target_pairs={{0,28},{1,21},{2,30},{3,23},{4,16},{5,25},{6,18},{7,27},{8,20},{9,... | collective-permute-start | bytes 589832 | tf_op jit(solution)/shard_map/ppermute | solution.py:478
  42.4 6.7 %collective-permute-start.17 = (f32[128,384]{1,0:T(8,128)S(1)}, f32[128,384]{1,0:T(8,128)S(1)}, u32[]{:S(2)}, u32[]{:S(2)}) collective-permute-start(f32[128,384]{1,0:T(8,128)S(1)} %sum_whole.12.refs_2_.refs_0_), channel_id=1, source_target_pairs={{0,17},{1,18},{2,19},{3,16},{4,23},{5,20},{6,21},{7,22},{8,25},{9,... | collective-permute-start | bytes 589832 | tf_op jit(solution)/shard_map/ppermute | solution.py:478
  44.7 5.5 %collective-permute-start.16 = (f32[128,384]{1,0:T(8,128)S(1)}, f32[128,384]{1,0:T(8,128)S(1)}, u32[]{:S(2)}, u32[]{:S(2)}) collective-permute-start(f32[128,384]{1,0:T(8,128)S(1)} %sum_whole.13.refs_2_.refs_0_), channel_id=1, source_target_pairs={{0,28},{1,21},{2,30},{3,23},{4,16},{5,25},{6,18},{7,27},{8,20},{9,... | collective-permute-start | bytes 589832 | tf_op jit(solution)/shard_map/ppermute | solution.py:478
  46.0 6.7 %collective-permute-start.15 = (f32[192,256]{1,0:T(8,128)S(1)}, f32[192,256]{1,0:T(8,128)S(1)}, u32[]{:S(2)}, u32[]{:S(2)}) collective-permute-start(f32[192,256]{1,0:T(8,128)S(1)} %sum_whole.14.refs_2_.refs_0_), channel_id=1, source_target_pairs={{0,48},{1,113},{2,50},{3,115},{4,116},{5,53},{6,118},{7,55},{8,56}... | collective-permute-start | bytes 589832 | tf_op jit(solution)/shard_map/ppermute | solution.py:478
  49.1 5.4 %collective-permute-start.20 = (f32[128,384]{1,0:T(8,128)S(1)}, f32[128,384]{1,0:T(8,128)S(1)}, u32[]{:S(2)}, u32[]{:S(2)}) collective-permute-start(f32[128,384]{1,0:T(8,128)S(1)} %sum_whole.15.refs_2_.refs_0_), channel_id=1, source_target_pairs={{0,19},{1,16},{2,17},{3,18},{4,21},{5,22},{6,23},{7,20},{8,27},{9,... | collective-permute-start | bytes 589832 | tf_op jit(solution)/shard_map/ppermute | solution.py:478
  50.2 6.7 %collective-permute-start.19 = (f32[128,384]{1,0:T(8,128)S(1)}, f32[128,384]{1,0:T(8,128)S(1)}, u32[]{:S(2)}, u32[]{:S(2)}) collective-permute-start(f32[128,384]{1,0:T(8,128)S(1)} %sum_whole.16.refs_2_.refs_0_), channel_id=1, source_target_pairs={{0,20},{1,29},{2,22},{3,31},{4,24},{5,17},{6,26},{7,19},{8,28},{9,... | collective-permute-start | bytes 589832 | tf_op jit(solution)/shard_map/ppermute | solution.py:478
  52.7 6.3 %collective-permute-start.18 = (f32[192,256]{1,0:T(8,128)S(1)}, f32[192,256]{1,0:T(8,128)S(1)}, u32[]{:S(2)}, u32[]{:S(2)}) collective-permute-start(f32[192,256]{1,0:T(8,128)S(1)} %sum_whole.17.refs_2_.refs_0_), channel_id=1, source_target_pairs={{0,112},{1,49},{2,114},{3,51},{4,52},{5,117},{6,54},{7,119},{8,120... | collective-permute-start | bytes 589832 | tf_op jit(solution)/shard_map/ppermute | solution.py:478
  54.6 5.6 %collective-permute-start.21 = (f32[128,384]{1,0:T(8,128)S(1)}, f32[128,384]{1,0:T(8,128)S(1)}, u32[]{:S(2)}, u32[]{:S(2)}) collective-permute-start(f32[128,384]{1,0:T(8,128)S(1)} %sum_last.3.refs_2_.refs_0_), channel_id=1, source_target_pairs={{0,28},{1,21},{2,30},{3,23},{4,16},{5,25},{6,18},{7,27},{8,20},{9,... | collective-permute-start | bytes 589832 | tf_op jit(solution)/shard_map/ppermute | solution.py:478
  56.9 6.7 %collective-permute-start.22 = (f32[128,384]{1,0:T(8,128)S(1)}, f32[128,384]{1,0:T(8,128)S(1)}, u32[]{:S(2)}, u32[]{:S(2)}) collective-permute-start(f32[128,384]{1,0:T(8,128)S(1)} %sum_last.4.refs_2_.refs_0_), channel_id=1, source_target_pairs={{0,48},{1,113},{2,50},{3,115},{4,116},{5,53},{6,118},{7,55},{8,56}... | collective-permute-start | bytes 589832 | tf_op jit(solution)/shard_map/ppermute | solution.py:478
  60.2 11.2 %collective-permute-start.24 = (f32[256,384]{1,0:T(8,128)S(1)}, f32[256,384]{1,0:T(8,128)S(1)}, u32[]{:S(2)}, u32[]{:S(2)}) collective-permute-start(f32[256,384]{1,0:T(8,128)S(1)} %join.3.refs_2_.refs_0_), channel_id=1, source_target_pairs={{0,20},{1,29},{2,22},{3,31},{4,24},{5,17},{6,26},{7,19},{8,28},{9,... | collective-permute-start | bytes 1179656 | tf_op jit(solution)/shard_map/ppermute | solution.py:478
  63.6 7.8 %collective-permute-start.26 = (f32[256,384]{1,0:T(8,128)S(1)}, f32[256,384]{1,0:T(8,128)S(1)}, u32[]{:S(2)}, u32[]{:S(2)}) collective-permute-start(f32[256,384]{1,0:T(8,128)S(1)} %join.4.refs_2_.refs_3_.refs_0_), channel_id=1, source_target_pairs={{0,112},{1,49},{2,114},{3,51},{4,52},{5,117},{6,54},{7,119},{8,120... | collective-permute-start | bytes 1179656 | tf_op jit(solution)/shard_map/ppermute | solution.py:478
  64.1 7.3 %collective-permute-start.28 = (f32[256,256]{1,0:T(8,128)S(1)}, f32[256,256]{1,0:T(8,128)S(1)}, u32[]{:S(2)}, u32[]{:S(2)}) collective-permute-start(f32[256,256]{1,0:T(8,128)S(1)} %join.5.refs_2_.refs_4_.refs_0_), channel_id=1, source_target_pairs={{0,17},{1,18},{2,19},{3,16},{4,23},{5,20},{6,21},{7,22},{8,25},{9,... | collective-permute-start | bytes 786440 | tf_op jit(solution)/shard_map/ppermute | solution.py:478
  (9 other events, 28.6 us)
